TPU v7x, 256 devices: a whole 4x4x8 slice. The times are simulated.
256 devices in a mesh: frame: 64 (over x, z, y_hi), patch: 4 (over y_lo, core).
Axes of the slice: x: 4, y: 4 (y_hi: 2, y_lo: 2; y = y_hi * 2 + y_lo), z: 8, core: 2. Of those that a mesh axis runs over, the one named last changes fastest.
Arguments:
- hidden_in: bfloat16 [128, 512, 1152], P('frame', 'patch'), may hold values from -24 to 24
- grad_out: bfloat16 [128, 512, 1152], P('frame', 'patch'), may hold values from -6 to 6
- w_qkv: bfloat16 [1152, 3456], replicated, may hold values from -0.1875 to 0.1875
- w_out: bfloat16 [1152, 1152], replicated, may hold values from -0.1875 to 0.1875
Outputs:
- grad_in: bfloat16 [128, 512, 1152], P('frame', 'patch')
- grad_wqkv: float32 [1152, 3456], P('frame', 'patch')
- grad_wout: float32 [1152, 1152], P('frame', 'patch')
All inputs are finite; a program needn't handle non-finite values.
Results may differ from a plain program's by a relative error of at most 0.015.
The roundings to bfloat16 on the way count: a program that leaves them out, or rounds other values in their place, can miss the bound.
Values may be sent and summed in bfloat16 or wider, within the bound.
No kernel may reach another device: no remote copies, remote signals or barrier semaphores. Data moves between devices by JAX's collectives and lax.ppermute only.
A program may use at most 128 MiB of HBM per device.

v0:
```python
import jax
import jax.numpy as jnp
from jax import lax
from jax.experimental import pallas as pl
from jax.experimental.pallas import tpu as pltpu
from jax.sharding import Mesh, PartitionSpec as P

HEADS, HD, D = 16, 72, 1152
ROWS = 256
FRAME = ("x", "z", "yh")
Y = ("yh", "yl")
BF, F32 = jnp.bfloat16, jnp.float32
NN = ((1,), (0,))
NT = ((1,), (1,))
TN = ((0,), (0,))
VMEM = pl.BlockSpec(memory_space=pltpu.VMEM)
ANY = pl.BlockSpec(memory_space=pl.ANY)
SMEM = pl.BlockSpec(memory_space=pltpu.SMEM)
LIMIT = 56 * 1024 * 1024


def flip(array, axes, step):
    size = 4 if axes == "x" or axes == Y else 2
    return lax.ppermute(array, axes, [(i, i ^ step) for i in range(size)])


def mm(a, b, contract):
    return lax.dot_general(a, b, (contract, ((), ())), preferred_element_type=F32)


def pick(rows, cols, source):
    i = lax.broadcasted_iota(jnp.int32, (rows, cols), 0)
    j = lax.broadcasted_iota(jnp.int32, (rows, cols), 1)
    return (j == source(i)).astype(F32).astype(BF)


def pack_kernel(hidden, grad, out):
    at = lambda a: pick(
        512, ROWS, lambda i: jnp.where(((i >> 2) & 1) == a, ((i >> 1) & 1) * 128 + (i >> 3) * 2 + (i & 1), -1)
    )
    out[...] = (mm(at(0), hidden[...], NN) + mm(at(1), grad[...], NN)).astype(BF)


def attend_kernel(blocks, got, order, w_qkv, w_out, x_out, dg_own, dg_other, dq_out,
                  w1, w2, sems, qkv_t, do_t, dqkv_t, attn_t):
    loads = [pltpu.make_async_copy(w_out, w2, sems.at[0])] + [
        pltpu.make_async_copy(w_qkv.at[:, pl.ds(D * i, D)], w1.at[i], sems.at[1 + i]) for i in range(3)
    ]
    for load in loads:
        load.start()
    place = lambda a: lambda i: ((i >> 1) & 63) * 8 + a * 4 + (i & 1) * 2 + (i >> 7)
    recv = got[...]
    hid = mm(pick(ROWS, 512, place(0)), recv, NN).astype(BF)
    gout = mm(pick(ROWS, 512, place(1)), recv, NN).astype(BF)
    gout_t = gout.astype(F32).T.astype(BF)
    for b in range(4):
        rows = gout_t[288 * b : 288 * (b + 1)]

        @pl.when(blocks[b] < 2)
        def _():
            dg_own[blocks[b], 864:, :] = rows

        @pl.when(blocks[b] >= 2)
        def _():
            dg_other[blocks[b] - 2, 864:, :] = rows

    chosen = [
        (lax.broadcasted_iota(jnp.int32, (384, D), 1) == order[384 * i : 384 * (i + 1), :])
        .astype(F32)
        .astype(BF)
        for i in range(3)
    ]
    for i in range(3):
        x_out[384 * i : 384 * (i + 1), :] = mm(chosen[i], hid, NT).astype(BF)
    loads[0].wait()
    for i in range(3):
        do_t[384 * i : 384 * (i + 1), :] = mm(w2[384 * i : 384 * (i + 1), :], gout, NT).astype(BF).astype(F32)
    for i in range(3):
        loads[1 + i].wait()
        for j in range(3):
            part = mm(hid, w1[i, :, 384 * j : 384 * (j + 1)], NN).astype(BF).astype(F32)
            qkv_t[D * i + 384 * j : D * i + 384 * (j + 1), :] = part.T

    scale = 1.0 / HD**0.5

    def head(h, carry):
        at = lambda i: pl.ds(pl.multiple_of(D * i + HD * h, 8), HD)
        q_t, k_t, v_t = (qkv_t[at(i), :].astype(BF) for i in range(3))
        d_t = do_t[at(0), :].astype(BF)
        results = []
        for p in range(2):
            cut = slice(128 * p, 128 * (p + 1))
            q, k, v, do = q_t[:, cut], k_t[:, cut], v_t[:, cut], d_t[:, cut]
            scores = mm(k, q, TN) * scale
            grown = jnp.exp(scores - jnp.max(scores, axis=0, keepdims=True))
            probs = grown * (1.0 / jnp.sum(grown, axis=0, keepdims=True))
            probs_b = probs.astype(BF)
            dprob = mm(v, do, TN)
            dscore = probs * (dprob - jnp.sum(probs * dprob, axis=0, keepdims=True)) * scale
            dscore = dscore.astype(BF)
            attn_t[at(0), cut] = mm(v, probs_b, NN)
            dqkv_t[at(0), cut] = mm(k, dscore, NN)
            dqkv_t[at(1), cut] = mm(q, dscore, NT)
            dqkv_t[at(2), cut] = mm(do, probs_b, NT)
        return carry

    lax.fori_loop(0, HEADS, head, 0, unroll=4)

    attn = attn_t[...].astype(BF)
    for i in range(3):
        x_out[D + 384 * i : D + 384 * (i + 1), :] = mm(chosen[i], attn, NN).astype(BF)
    back = pick(ROWS, ROWS, lambda i: (i & 127) * 2 + (i >> 7))
    for b in range(4):
        rows = dqkv_t[864 * b : 864 * (b + 1), :].astype(BF)

        @pl.when(blocks[b] < 2)
        def _():
            dg_own[blocks[b], :864, :] = rows

        @pl.when(blocks[b] >= 2)
        def _():
            dg_other[blocks[b] - 2, :864, :] = rows

        dq_out[864 * b : 864 * (b + 1), :] = mm(rows, back, NN).astype(BF)


def product_kernel(x_own, x_oth, dg_own, dg_oth, *parts):
    row = lax.broadcasted_iota(jnp.int32, (128, ROWS), 0)
    for r in range(2):
        for s in range(8):
            rows = 144
            cut = slice(rows * s, rows * (s + 1))
            low = slice(D + rows * s, D + rows * (s + 1))
            pieces = []
            for lo in (0, 384):
                pieces.append(mm(x_own[cut, :], dg_own[r, lo : lo + 384, :], NT)
                              + mm(x_oth[cut, :], dg_oth[r, lo : lo + 384, :], NT))
            own, oth = dg_own[r, 768:896, :], dg_oth[r, 768:896, :]
            none = jnp.zeros_like(own)
            mixed = (mm(x_own[cut, :], jnp.where(row < 96, own, none), NT)
                     + mm(x_oth[cut, :], jnp.where(row < 96, oth, none), NT)
                     + mm(x_own[low, :], jnp.where(row >= 96, own, none), NT)
                     + mm(x_oth[low, :], jnp.where(row >= 96, oth, none), NT))
            right = (mm(x_own[low, :], dg_own[r, 896:, :], NT)
                     + mm(x_oth[low, :], dg_oth[r, 896:, :], NT))
            if s < 4:
                out, at = parts[s], slice(None)
                put = lambda c, v: out.__setitem__((r, at, c), v.astype(BF))
            else:
                ra, half = (s - 4) // 2, (s - 4) % 2
                out, at = parts[4 + 2 * ra + r], slice(rows * half, rows * (half + 1))
                put = lambda c, v: out.__setitem__((at, c), v.astype(BF))
            put(slice(0, 384), pieces[0])
            put(slice(384, 768), pieces[1])
            put(slice(768, 896), mixed)
            put(slice(896, D), right)


def shape(*dims, dtype=BF):
    return jax.ShapeDtypeStruct(dims, dtype)


def call(kernel, outs, ins, flops, scratch=(), specs=None):
    return pl.pallas_call(
        kernel,
        out_shape=outs,
        in_specs=specs or [VMEM] * len(ins),
        out_specs=jax.tree.map(lambda _: VMEM, outs),
        scratch_shapes=list(scratch),
        compiler_params=pltpu.CompilerParams(vmem_limit_bytes=LIMIT),
        cost_estimate=pl.CostEstimate(flops=flops, bytes_accessed=10**7, transcendentals=0),
    )(*ins)


def column_order(x, yh):
    at = jnp.arange(576)
    k, zz = at % 18, at // 18 % 4
    rx_a, ra_a = at // 144, at // 72 % 2
    ra_b, rx_b = at // 288, at // 72 % 4
    half_a = (x ^ rx_a) * 288 + zz * 36 + (yh ^ ra_a) * 18 + k
    half_b = (x ^ rx_b) * 288 + (4 + zz) * 36 + (yh ^ ra_b) * 18 + k
    return jnp.concatenate([half_a, half_b])


def total(own, others):
    return own.astype(F32) + sum(g.astype(F32) for g in others)


def per_device(hidden_in, grad_out, w_qkv, w_out):
    x, yh, yl, c = (lax.axis_index(a) for a in ("x", "yh", "yl", "c"))
    both = call(pack_kernel, shape(512, D), (hidden_in.reshape(ROWS, D), grad_out.reshape(ROWS, D)), 10**9)
    both = lax.all_to_all(both, FRAME, split_axis=0, concat_axis=0, tiled=True)
    order = column_order(x, yh).astype(jnp.int32).reshape(D, 1)
    blocks = jnp.stack([(b // 2 ^ yl) + 2 * (b % 2 ^ c) for b in range(4)]).astype(jnp.int32)
    x_own, dg_own, dg_other, dqkv = call(
        attend_kernel,
        (shape(2 * D, ROWS), shape(2, D, ROWS), shape(2, D, ROWS), shape(3 * D, ROWS)),
        (blocks, both, order, w_qkv, w_out),
        10 * 10**9,
        scratch=[
            pltpu.VMEM((3, D, D), BF),
            pltpu.VMEM((D, D), BF),
            pltpu.SemaphoreType.DMA((4,)),
            pltpu.VMEM((3 * D, ROWS), F32),
            pltpu.VMEM((D, ROWS), F32),
            pltpu.VMEM((3 * D, ROWS), F32),
            pltpu.VMEM((D, ROWS), F32),
        ],
        specs=[SMEM, VMEM, VMEM, ANY, ANY],
    )
    x_oth, dg_oth = flip(x_own, "c", 1), flip(dg_other, "c", 1)
    parts = call(
        product_kernel,
        [shape(2, 144, D)] * 4 + [shape(288, D)] * 4,
        (x_own, x_oth, dg_own, dg_oth),
        6 * 10**9,
    )
    part_a, part_b = parts[:4], parts[4:]
    got_a = [flip(part_a[rx], "x", rx) for rx in (1, 3, 2)]
    got_b = [flip(part_b[s], Y, s) for s in (1, 3, 2)]
    sum_a = total(part_a[0], got_a).astype(BF).reshape(2, 2, 72, D)
    sum_b = total(part_b[0], got_b).astype(BF).reshape(4, 72, D)
    got_a = [flip(sum_a[s & 1, s >> 1], Y, s) for s in (1, 3, 2)]
    got_b = [flip(sum_b[rx], "x", rx) for rx in (1, 3, 2)]
    last = jnp.concatenate([total(sum_a[0, 0], got_a), total(sum_b[0], got_b)])
    last = last.astype(BF).reshape(8, 18, D)
    last = lax.all_to_all(last, "z", split_axis=0, concat_axis=0, tiled=True)
    grad_w = jnp.sum(last.astype(F32), axis=0)

    grad_in = mm(dqkv, w_qkv, ((0,), (1,))).astype(BF)
    grad_in = lax.all_to_all(grad_in, FRAME, split_axis=0, concat_axis=0, tiled=True)
    grad_in = grad_in.reshape(64, 2, 2, D).transpose(1, 0, 2, 3).reshape(2, 128, D)
    return grad_in, grad_w[:, :864], grad_w[:, 864:]


def solution(mesh):
    fine = Mesh(mesh.devices.reshape(4, 8, 2, 2, 2), ("x", "z", "yh", "yl", "c"))
    patch = ("yl", "c")
    in_specs = (P(FRAME, patch, None), P(FRAME, patch, None), P(), P())
    out_specs = (P(FRAME, patch, None), P(FRAME, patch), P(FRAME, patch))
    return jax.shard_map(
        per_device, mesh=fine, in_specs=in_specs, out_specs=out_specs, check_vma=False
    )
```

profile of v0, /device:TPU:8, one launch (start us, length us, event | category | flops | bytes accessed | tf_op | source)
XLA Modules:
  0.0 179.3 jit_solution(3737927173546933150)
XLA Ops:
  0.6 3.2 %shard_map.67 = bf16[512,1152]{1,0:T(8,128)(2,1)} custom-call(bf16[256,1152]{1,0:T(8,128)(2,1)} %bitcast.30, bf16[256,1152]{1,0:T(8,128)(2,1)} %bitcast.31), custom_call_target="tpu_custom_call" | custom-call | flops 1000000000 | bytes 10000000 | tf_op jit(solution)/shard_map/pallas_call | solution.py:164
  3.8 13.7 %all-to-all-start = ((bf16[64,8,1152]{2,1,0:T(8,128)(2,1)}), bf16[64,8,1152]{2,1,0:T(8,128)(2,1)S(1)}, u32[]{:S(2)}, u32[]{:S(2)}) async-start(bf16[64,8,1152]{2,1,0:T(8,128)(2,1)} %bitcast.29), calls=%async_computation | async-start | bytes 2359296 | tf_op jit(solution)/shard_map/all_to_all | solution.py:192
  17.6 1.0 reshape.50.order
  19.3 31.5 %all-to-all-done = bf16[64,8,1152]{2,1,0:T(8,128)(2,1)S(1)} async-done(((bf16[64,8,1152]{2,1,0:T(8,128)(2,1)}), bf16[64,8,1152]{2,1,0:T(8,128)(2,1)S(1)}, u32[]{:S(2)}, u32[]{:S(2)}) %all-to-all-start) | async-done | bytes 1179680 | tf_op jit(solution)/shard_map/all_to_all | solution.py:192
  50.7 1.1 copy-done
  51.8 22.8 %shard_map.68 = (bf16[2304,256]{1,0:T(8,128)(2,1)}, bf16[2,1152,256]{2,1,0:T(8,128)(2,1)}, bf16[2,1152,256]{2,1,0:T(8,128)(2,1)}, bf16[3456,256]{1,0:T(8,128)(2,1)}) custom-call(s32[4]{0:T(128)} %pad_add_fusion.1.blocks, bf16[512,1152]{1,0:T(8,128)(2,1)} %bitcast.28, s32[1152,1]{1,0:T(8,128)} %reshape.50.order, bf16[1152,3456]{1,0:T(8,128)(2,1)} %w_qkv.1, ...), custom_call_target="tpu_custom_call" | custom-call | flops 10000000000 | bytes 10000000 | tf_op jit(solution)/shard_map/pallas_call | solution.py:164
  75.2 2.5 %collective-permute-done.1.dg_oth = bf16[2,1152,256]{2,1,0:T(8,128)(2,1)S(1)} collective-permute-done((bf16[2,1152,256]{2,1,0:T(8,128)(2,1)}, bf16[2,1152,256]{2,1,0:T(8,128)(2,1)S(1)}, u32[]{:S(2)}, u32[]{:S(2)}) %collective-permute-start.1) | collective-permute-done | bytes 1179680 | tf_op jit(solution)/shard_map/ppermute | solution.py:24
  77.8 1.7 collective-permute-done.x_oth
  79.4 1.0 copy-done.4
  80.5 9.4 %shard_map.69 = (bf16[2,144,1152]{2,1,0:T(8,128)(2,1)}, bf16[2,144,1152]{2,1,0:T(8,128)(2,1)}, bf16[2,144,1152]{2,1,0:T(8,128)(2,1)}, bf16[2,144,1152]{2,1,0:T(8...) custom-call(bf16[2304,256]{1,0:T(8,128)(2,1)} %get-tuple-element.16., ...), custom_call_target="tpu_custom_call" | custom-call | flops 6000000000 | bytes 10000000 | tf_op jit(solution)/shard_map/pallas_call | solution.py:164
  89.9 0.7 collective-permute-start.2
  91.2 2.8 %collective-permute-start.4 = (bf16[2,144,1152]{2,1,0:T(8,128)(2,1)}, bf16[2,144,1152]{2,1,0:T(8,128)(2,1)S(1)}, u32[]{:S(2)}, u32[]{:S(2)}) collective-permute-start(bf16[2,144,1152]{2,1,0:T(8,128)(2,1)} %get-tuple-element.22), channel_id=1, source_target_pairs={{0,128},{64,192},{128,0},{192,64},{1,129},{65,193},{129,1},{193,65... | collective-permute-start | bytes 1990664 | tf_op jit(solution)/shard_map/ppermute | solution.py:24
  94.0 5.8 %convolution_convert_fusion = bf16[256,1152]{1,0:T(8,128)(2,1)S(1)} fusion(bf16[3456,256]{1,0:T(8,128)(2,1)S(1)} %copy-done.5, bf16[1152,3456]{1,0:T(8,128)(2,1)} %w_qkv.1), kind=kOutput, calls=%fused_computation | convolution fusion | flops 2038726656 | bytes 10321920 | tf_op jit(solution)/shard_map/dot_general | solution.py:28
  99.9 1.0 all_to_all.19
  100.8 6.0 %all-to-all-start.1 = ((bf16[64,4,1152]{2,1,0:T(4,128)(2,1)}), bf16[64,4,1152]{2,1,0:T(4,128)(2,1)S(1)}, u32[]{:S(2)}, u32[]{:S(2)}) async-start(bf16[64,4,1152]{2,1,0:T(4,128)(2,1)} %all_to_all.19), calls=%async_computation.1 | async-start | bytes 1179648 | tf_op jit(solution)/shard_map/all_to_all | solution.py:231
  106.8 1.4 collective-permute-start.8
  108.2 2.3 %collective-permute-start.9 = (bf16[288,1152]{1,0:T(8,128)(2,1)}, bf16[288,1152]{1,0:T(8,128)(2,1)S(1)}, u32[]{:S(2)}, u32[]{:S(2)}) collective-permute-start(bf16[288,1152]{1,0:T(8,128)(2,1)} %get-tuple-element.25), channel_id=1, source_target_pairs={{0,6},{2,4},{4,2},{6,0},{1,7},{3,5},{5,3},{7,1},{8,14},{10,12},{12... | collective-permute-start | bytes 1990664 | tf_op jit(solution)/shard_map/ppermute | solution.py:24
  111.0 18.1 %collective-permute-done.3 = bf16[2,144,1152]{2,1,0:T(8,128)(2,1)S(1)} collective-permute-done((bf16[2,144,1152]{2,1,0:T(8,128)(2,1)}, bf16[2,144,1152]{2,1,0:T(8,128)(2,1)S(1)}, u32[]{:S(2)}, u32[]{:S(2)}) %collective-permute-start.3) | collective-permute-done | bytes 663584 | tf_op jit(solution)/shard_map/ppermute | solution.py:24
  129.4 1.4 collective-permute-start.5
  131.3 1.7 collective-permute-start.6
  133.0 12.3 %collective-permute-done.9 = bf16[288,1152]{1,0:T(8,128)(2,1)S(1)} collective-permute-done((bf16[288,1152]{1,0:T(8,128)(2,1)}, bf16[288,1152]{1,0:T(8,128)(2,1)S(1)}, u32[]{:S(2)}, u32[]{:S(2)}) %collective-permute-start.9) | collective-permute-done | bytes 663584 | tf_op jit(solution)/shard_map/ppermute | solution.py:24
  145.3 1.3 collective-permute-done.10
  147.0 1.7 collective-permute-start.11
  148.7 2.6 %collective-permute-start.13 = (bf16[72,1152]{1,0:T(8,128)(2,1)S(1)}, bf16[72,1152]{1,0:T(8,128)(2,1)S(1)}, u32[]{:S(2)}, u32[]{:S(2)}) collective-permute-start(bf16[72,1152]{1,0:T(8,128)(2,1)S(1)} %get-tuple-element.31), channel_id=1, source_target_pairs={{0,128},{64,192},{128,0},{192,64},{1,129},{65,193},{129,1},{193,65... | collective-permute-start | bytes 497672 | tf_op jit(solution)/shard_map/ppermute | solution.py:24
  152.5 4.0 %collective-permute-done.13 = bf16[72,1152]{1,0:T(8,128)(2,1)S(1)} collective-permute-done((bf16[72,1152]{1,0:T(8,128)(2,1)S(1)}, bf16[72,1152]{1,0:T(8,128)(2,1)S(1)}, u32[]{:S(2)}, u32[]{:S(2)}) %collective-permute-start.13) | collective-permute-done | bytes 165920 | tf_op jit(solution)/shard_map/ppermute | solution.py:24
  156.4 1.7 collective-permute-done.12
  158.3 0.9 convert_element_type.88
  159.2 6.2 %all-to-all-start.2 = ((bf16[8,18,1152]{2,1,0:T(8,128)(2,1)}), bf16[8,18,1152]{2,1,0:T(8,128)(2,1)S(1)}, u32[]{:S(2)}, u32[]{:S(2)}) async-start(bf16[8,18,1152]{2,1,0:T(8,128)(2,1)} %convert_element_type.88), calls=%async_computation.2 | async-start | bytes 884736 | tf_op jit(solution)/shard_map/all_to_all | solution.py:227
  166.1 1.0 reshape.47
  167.1 10.7 %all-to-all-done.2 = bf16[8,18,1152]{2,1,0:T(8,128)(2,1)S(1)} async-done(((bf16[8,18,1152]{2,1,0:T(8,128)(2,1)}), bf16[8,18,1152]{2,1,0:T(8,128)(2,1)S(1)}, u32[]{:S(2)}, u32[]{:S(2)}) %all-to-all-start.2) | async-done | bytes 331808 | tf_op jit(solution)/shard_map/all_to_all | solution.py:227
  177.9 0.7 slice.53
  178.6 0.6 slice.52
  (37 shorter events, 5.6 us)
Async XLA Ops:
  3.8 46.9 %all-to-all-start = ((bf16[64,8,1152]{2,1,0:T(8,128)(2,1)}), bf16[64,8,1152]{2,1,0:T(8,128)(2,1)S(1)}, u32[]{:S(2)}, u32[]{:S(2)}) async-start(bf16[64,8,1152]{2,1,0:T(8,128)(2,1)} %bitcast.29), calls=%async_computation | async-start | bytes 2359296 | tf_op jit(solution)/shard_map/all_to_all | solution.py:192
  50.7 1.1 copy-start
  74.6 3.1 %collective-permute-start.1 = (bf16[2,1152,256]{2,1,0:T(8,128)(2,1)}, bf16[2,1152,256]{2,1,0:T(8,128)(2,1)S(1)}, u32[]{:S(2)}, u32[]{:S(2)}) collective-permute-start(bf16[2,1152,256]{2,1,0:T(8,128)(2,1)} %get-tuple-element.18), channel_id=1, source_target_pairs={{0,1},{1,0},{2,3},{3,2},{4,5},{5,4},{6,7},{7,6},{8,9},{9,8},{10,11... | collective-permute-start | bytes 3538952 | tf_op jit(solution)/shard_map/ppermute | solution.py:24
  74.7 4.7 %collective-permute-start = (bf16[2304,256]{1,0:T(8,128)(2,1)}, bf16[2304,256]{1,0:T(8,128)(2,1)S(1)}, u32[]{:S(2)}, u32[]{:S(2)}) collective-permute-start(bf16[2304,256]{1,0:T(8,128)(2,1)} %get-tuple-element.16.x_own), channel_id=1, source_target_pairs={{0,1},{1,0},{2,3},{3,2},{4,5},{5,4},{6,7},{7,6},{8,9},{9,8},{10,11... | collective-permute-start | bytes 3538952 | tf_op jit(solution)/shard_map/ppermute | solution.py:24
  77.8 1.7 copy-start.3
  79.4 1.1 copy-start.4
  80.5 13.5 %copy-start.5 = (bf16[3456,256]{1,0:T(8,128)(2,1)S(1)}, bf16[3456,256]{1,0:T(8,128)(2,1)}, u32[]{:S(2)}) copy-start(bf16[3456,256]{1,0:T(8,128)(2,1)} %get-tuple-element.15) | copy-start | bytes 5308420
  89.9 20.6 %collective-permute-start.2 = (bf16[2,144,1152]{2,1,0:T(8,128)(2,1)}, bf16[2,144,1152]{2,1,0:T(8,128)(2,1)S(1)}, u32[]{:S(2)}, u32[]{:S(2)}) collective-permute-start(bf16[2,144,1152]{2,1,0:T(8,128)(2,1)} %get-tuple-element.20), channel_id=1, source_target_pairs={{0,64},{64,0},{128,192},{192,128},{1,65},{65,1},{129,193},{193,129... | collective-permute-start | bytes 1990664 | tf_op jit(solution)/shard_map/ppermute | solution.py:24
  90.6 38.4 %collective-permute-start.3 = (bf16[2,144,1152]{2,1,0:T(8,128)(2,1)}, bf16[2,144,1152]{2,1,0:T(8,128)(2,1)S(1)}, u32[]{:S(2)}, u32[]{:S(2)}) collective-permute-start(bf16[2,144,1152]{2,1,0:T(8,128)(2,1)} %get-tuple-element.21), channel_id=1, source_target_pairs={{0,192},{64,128},{128,64},{192,0},{1,193},{65,129},{129,65},{193,1... | collective-permute-start | bytes 1990664 | tf_op jit(solution)/shard_map/ppermute | solution.py:24
  91.2 37.8 %collective-permute-start.4 = (bf16[2,144,1152]{2,1,0:T(8,128)(2,1)}, bf16[2,144,1152]{2,1,0:T(8,128)(2,1)S(1)}, u32[]{:S(2)}, u32[]{:S(2)}) collective-permute-start(bf16[2,144,1152]{2,1,0:T(8,128)(2,1)} %get-tuple-element.22), channel_id=1, source_target_pairs={{0,128},{64,192},{128,0},{192,64},{1,129},{65,193},{129,1},{193,65... | collective-permute-start | bytes 1990664 | tf_op jit(solution)/shard_map/ppermute | solution.py:24
  99.9 29.2 %copy-start.2 = (bf16[2,144,1152]{2,1,0:T(8,128)(2,1)S(1)}, bf16[2,144,1152]{2,1,0:T(8,128)(2,1)}, u32[]{:S(2)}) copy-start(bf16[2,144,1152]{2,1,0:T(8,128)(2,1)} %get-tuple-element.19) | copy-start | bytes 1990660
  100.8 58.4 %all-to-all-start.1 = ((bf16[64,4,1152]{2,1,0:T(4,128)(2,1)}), bf16[64,4,1152]{2,1,0:T(4,128)(2,1)S(1)}, u32[]{:S(2)}, u32[]{:S(2)}) async-start(bf16[64,4,1152]{2,1,0:T(4,128)(2,1)} %all_to_all.19), calls=%async_computation.1 | async-start | bytes 1179648 | tf_op jit(solution)/shard_map/all_to_all | solution.py:231
  106.8 24.5 %collective-permute-start.8 = (bf16[288,1152]{1,0:T(8,128)(2,1)}, bf16[288,1152]{1,0:T(8,128)(2,1)S(1)}, u32[]{:S(2)}, u32[]{:S(2)}) collective-permute-start(bf16[288,1152]{1,0:T(8,128)(2,1)} %get-tuple-element.24), channel_id=1, source_target_pairs={{0,2},{2,0},{4,6},{6,4},{1,3},{3,1},{5,7},{7,5},{8,10},{10,8},{12,... | collective-permute-start | bytes 1990664 | tf_op jit(solution)/shard_map/ppermute | solution.py:24
  108.2 37.1 %collective-permute-start.9 = (bf16[288,1152]{1,0:T(8,128)(2,1)}, bf16[288,1152]{1,0:T(8,128)(2,1)S(1)}, u32[]{:S(2)}, u32[]{:S(2)}) collective-permute-start(bf16[288,1152]{1,0:T(8,128)(2,1)} %get-tuple-element.25), channel_id=1, source_target_pairs={{0,6},{2,4},{4,2},{6,0},{1,7},{3,5},{5,3},{7,1},{8,14},{10,12},{12... | collective-permute-start | bytes 1990664 | tf_op jit(solution)/shard_map/ppermute | solution.py:24
  110.5 36.1 %collective-permute-start.10 = (bf16[288,1152]{1,0:T(8,128)(2,1)}, bf16[288,1152]{1,0:T(8,128)(2,1)S(1)}, u32[]{:S(2)}, u32[]{:S(2)}) collective-permute-start(bf16[288,1152]{1,0:T(8,128)(2,1)} %get-tuple-element.26), channel_id=1, source_target_pairs={{0,4},{2,6},{4,0},{6,2},{1,5},{3,7},{5,1},{7,3},{8,12},{10,14},{12... | collective-permute-start | bytes 1990664 | tf_op jit(solution)/shard_map/ppermute | solution.py:24
  129.4 17.3 %copy-start.1 = (bf16[288,1152]{1,0:T(8,128)(2,1)S(1)}, bf16[288,1152]{1,0:T(8,128)(2,1)}, u32[]{:S(2)}) copy-start(bf16[288,1152]{1,0:T(8,128)(2,1)} %get-tuple-element.23) | copy-start | bytes 1990660
  129.4 21.9 %collective-permute-start.5 = (bf16[72,1152]{1,0:T(8,128)(2,1)S(1)}, bf16[72,1152]{1,0:T(8,128)(2,1)S(1)}, u32[]{:S(2)}, u32[]{:S(2)}) collective-permute-start(bf16[72,1152]{1,0:T(8,128)(2,1)S(1)} %get-tuple-element.27), channel_id=1, source_target_pairs={{0,2},{2,0},{4,6},{6,4},{1,3},{3,1},{5,7},{7,5},{8,10},{10,8},{12,... | collective-permute-start | bytes 497672 | tf_op jit(solution)/shard_map/ppermute | solution.py:24
  130.9 21.1 %collective-permute-start.7 = (bf16[72,1152]{1,0:T(8,128)(2,1)S(1)}, bf16[72,1152]{1,0:T(8,128)(2,1)S(1)}, u32[]{:S(2)}, u32[]{:S(2)}) collective-permute-start(bf16[72,1152]{1,0:T(8,128)(2,1)S(1)} %get-tuple-element.28), channel_id=1, source_target_pairs={{0,4},{2,6},{4,0},{6,2},{1,5},{3,7},{5,1},{7,3},{8,12},{10,14},{12... | collective-permute-start | bytes 497672 | tf_op jit(solution)/shard_map/ppermute | solution.py:24
  131.3 20.7 %collective-permute-start.6 = (bf16[72,1152]{1,0:T(8,128)(2,1)S(1)}, bf16[72,1152]{1,0:T(8,128)(2,1)S(1)}, u32[]{:S(2)}, u32[]{:S(2)}) collective-permute-start(bf16[72,1152]{1,0:T(8,128)(2,1)S(1)} %get-tuple-element.29), channel_id=1, source_target_pairs={{0,6},{2,4},{4,2},{6,0},{1,7},{3,5},{5,3},{7,1},{8,14},{10,12},{12... | collective-permute-start | bytes 497672 | tf_op jit(solution)/shard_map/ppermute | solution.py:24
  147.0 5.4 %collective-permute-start.11 = (bf16[72,1152]{1,0:T(8,128)(2,1)S(1)}, bf16[72,1152]{1,0:T(8,128)(2,1)S(1)}, u32[]{:S(2)}, u32[]{:S(2)}) collective-permute-start(bf16[72,1152]{1,0:T(8,128)(2,1)S(1)} %get-tuple-element.30), channel_id=1, source_target_pairs={{0,64},{64,0},{128,192},{192,128},{1,65},{65,1},{129,193},{193,129... | collective-permute-start | bytes 497672 | tf_op jit(solution)/shard_map/ppermute | solution.py:24
  148.7 7.7 %collective-permute-start.13 = (bf16[72,1152]{1,0:T(8,128)(2,1)S(1)}, bf16[72,1152]{1,0:T(8,128)(2,1)S(1)}, u32[]{:S(2)}, u32[]{:S(2)}) collective-permute-start(bf16[72,1152]{1,0:T(8,128)(2,1)S(1)} %get-tuple-element.31), channel_id=1, source_target_pairs={{0,128},{64,192},{128,0},{192,64},{1,129},{65,193},{129,1},{193,65... | collective-permute-start | bytes 497672 | tf_op jit(solution)/shard_map/ppermute | solution.py:24
  151.3 6.9 %collective-permute-start.12 = (bf16[72,1152]{1,0:T(8,128)(2,1)S(1)}, bf16[72,1152]{1,0:T(8,128)(2,1)S(1)}, u32[]{:S(2)}, u32[]{:S(2)}) collective-permute-start(bf16[72,1152]{1,0:T(8,128)(2,1)S(1)} %get-tuple-element.32), channel_id=1, source_target_pairs={{0,192},{64,128},{128,64},{192,0},{1,193},{65,129},{129,65},{193,1... | collective-permute-start | bytes 497672 | tf_op jit(solution)/shard_map/ppermute | solution.py:24
  159.2 18.7 %all-to-all-start.2 = ((bf16[8,18,1152]{2,1,0:T(8,128)(2,1)}), bf16[8,18,1152]{2,1,0:T(8,128)(2,1)S(1)}, u32[]{:S(2)}, u32[]{:S(2)}) async-start(bf16[8,18,1152]{2,1,0:T(8,128)(2,1)} %convert_element_type.88), calls=%async_computation.2 | async-start | bytes 884736 | tf_op jit(solution)/shard_map/all_to_all | solution.py:227
where the time goes:
time: 180 us; the launch traced here: 179 us
  waiting for transfers between devices  84.4 us (47%)
  starting transfers between devices  43.1 us (24%)
  Pallas kernels  35.4 us (20%)
  local copies, waits for them, and re-layouts  8.07 us (4%)
  matrix products  5.83 us (3%)
    ppermute x14, waiting for transfers between devices, flip(): return lax.ppermute(array, axes, [(i, i ^ step) for i in range(size)])  42.2 us
    pallas_call x3, Pallas kernels, call(): pl.pallas_call(kernel, out_shape=outs, in_specs=specs or [VMEM] * len(ins...  35.4 us
    all_to_all x1, waiting for transfers between devices, per_device(): both = lax.all_to_all(both, FRAME, split_axis=0, concat_axis=0, tiled=True)  31.5 us
    ppermute x14, starting transfers between devices, flip(): return lax.ppermute(array, axes, [(i, i ^ step) for i in range(size)])  17.2 us
    all_to_all x1, starting transfers between devices, per_device(): both = lax.all_to_all(both, FRAME, split_axis=0, concat_axis=0, tiled=True)  13.7 us
    all_to_all x1, waiting for transfers between devices, per_device(): last = lax.all_to_all(last, 'z', split_axis=0, concat_axis=0, tiled=True)  10.7 us
    all_to_all x1, starting transfers between devices, per_device(): last = lax.all_to_all(last, 'z', split_axis=0, concat_axis=0, tiled=True)  6.25 us
    all_to_all x1, starting transfers between devices, per_device(): lax.all_to_all(grad_in, FRAME, split_axis=0, concat_axis=0, tiled=True)  5.95 us
  transfers between devices with their start and end apart: 17, of which 11 were waited for; matrix products, arithmetic and copies ran while one was open for 6% of the time, Pallas kernels for 0%

commit v1 on v0

v1 whole, which is shorter than its diff:
```python
import jax
import jax.numpy as jnp
from jax import lax
from jax.experimental import pallas as pl
from jax.experimental.pallas import tpu as pltpu
from jax.sharding import Mesh, PartitionSpec as P

HEADS, HD, D = 16, 72, 1152
ROWS = 256
FRAME = ("x", "z", "yh")
Y = ("yh", "yl")
BF, F32 = jnp.bfloat16, jnp.float32
NN = ((1,), (0,))
NT = ((1,), (1,))
TN = ((0,), (0,))
VMEM = pl.BlockSpec(memory_space=pltpu.VMEM)
ANY = pl.BlockSpec(memory_space=pl.ANY)
SMEM = pl.BlockSpec(memory_space=pltpu.SMEM)
MIB = 1024 * 1024
CUTS = 2


def flip(array, axes, step):
    size = {"x": 4, "z": 8, Y: 4, "c": 2}[axes]
    return lax.ppermute(array, axes, [(i, i ^ step) for i in range(size)])


def mm(a, b, contract):
    return lax.dot_general(a, b, (contract, ((), ())), preferred_element_type=F32)


def pick(rows, cols, source):
    i = lax.broadcasted_iota(jnp.int32, (rows, cols), 0)
    j = lax.broadcasted_iota(jnp.int32, (rows, cols), 1)
    return (j == source(i)).astype(F32).astype(BF)


def pack_kernel(hidden, grad, out, held, sent, sems):
    loads = [pltpu.make_async_copy(array, held.at[i], sems.at[i]) for i, array in enumerate((hidden, grad))]
    for load in loads:
        load.start()
    at = lambda a: pick(
        512, ROWS, lambda i: jnp.where(((i >> 2) & 1) == a, ((i >> 1) & 1) * 128 + (i >> 3) * 2 + (i & 1), -1)
    )
    for load in loads:
        load.wait()
    sent[...] = (mm(at(0), held[0], NN) + mm(at(1), held[1], NN)).astype(BF)
    store = pltpu.make_async_copy(sent, out, sems.at[2])
    store.start()
    store.wait()


def column_order(place, start, count):
    x, z, yh = place[0], place[1], place[2]
    at = lax.broadcasted_iota(jnp.int32, (count, 1), 0) + start
    q = ((at.astype(F32) + 0.5) * (1.0 / 18)).astype(jnp.int32)
    first = q < 32
    rx = jnp.where(first, q >> 3, (q >> 2) & 3)
    ra = jnp.where(first, (q >> 2) & 1, (q >> 4) & 1)
    rz = (q & 3) + jnp.where(first, 0, 4)
    return (x ^ rx) * 288 + (z ^ rz) * 36 + (yh ^ ra) * 18 + (at - 18 * q)


def slot(place, b):
    return ((b // 2) ^ place[3]) + 2 * ((b % 2) ^ place[4])


def prepare_kernel(place, w_qkv, w_out, out, held, made, sems):
    loads = [
        pltpu.make_async_copy(w_qkv.at[:, pl.ds(D * i, D)], held.at[i], sems.at[i]) for i in range(3)
    ] + [pltpu.make_async_copy(w_out, made.at[pl.ds(3 * D, D)], sems.at[3])]
    for load in loads:
        load.start()
    for i in range(3):
        order = column_order(place, 384 * i, 384)
        cols = lax.broadcasted_iota(jnp.int32, (384, D), 1)
        made[4 * D + 384 * i : 4 * D + 384 * (i + 1), :] = (cols == order).astype(F32).astype(BF)
    for i in range(3):
        loads[i].wait()
        for j in range(3):
            made[D * i + 384 * j : D * i + 384 * (j + 1), :] = held[i, :, 384 * j : 384 * (j + 1)].T
    loads[3].wait()
    store = pltpu.make_async_copy(made, out.at[pl.ds(0, 5 * D)], sems.at[4])
    store.start()
    store.wait()


def attend_kernel(home, got, prepared, x_out, dg_own, dg_other, weights, sems, qkv_t, do_t, dqkv_t, attn_t):
    order = (3, 0, 1, 2, 4)
    loads = [pltpu.make_async_copy(prepared.at[pl.ds(D * i, D)], weights.at[i], sems.at[i]) for i in order]
    for load in loads:
        load.start()
    place = lambda a: lambda i: ((i >> 1) & 63) * 8 + a * 4 + (i & 1) * 2 + (i >> 7)
    gout = mm(pick(ROWS, 512, place(1)), got[...], NN).astype(BF)
    hid = mm(pick(ROWS, 512, place(0)), got[...], NN).astype(BF)
    loads[0].wait()
    for i in range(3):
        cut = slice(384 * i, 384 * (i + 1))
        do_t[cut, :] = mm(weights[3, cut, :], gout, NT).astype(BF).astype(F32)
    for i in range(3):
        loads[1 + i].wait()
        for j in range(3):
            part = mm(weights[i, 384 * j : 384 * (j + 1), :], hid, NT)
            qkv_t[D * i + 384 * j : D * i + 384 * (j + 1), :] = part.astype(BF).astype(F32)

    def keep(b, rows, at):
        @pl.when(slot(home, b) < 2)
        def _():
            dg_own[slot(home, b) & 1, at, :] = rows

        @pl.when(slot(home, b) >= 2)
        def _():
            dg_other[slot(home, b) & 1, at, :] = rows

    gout_t = gout.T
    for b in range(4):
        keep(b, gout_t[288 * b : 288 * (b + 1)], slice(864, D))

    scale = 1.0 / HD**0.5

    def head(h, carry):
        at = lambda i: pl.ds(pl.multiple_of(D * i + HD * h, 8), HD)
        q_t, k_t, v_t = (qkv_t[at(i), :].astype(BF) for i in range(3))
        d_t = do_t[at(0), :].astype(BF)
        for p in range(2):
            cut = slice(128 * p, 128 * (p + 1))
            q, k, v, do = q_t[:, cut], k_t[:, cut], v_t[:, cut], d_t[:, cut]
            scores = mm(k, q, TN) * scale
            grown = jnp.exp(scores - jnp.max(scores, axis=0, keepdims=True))
            probs = grown * (1.0 / jnp.sum(grown, axis=0, keepdims=True))
            probs_b = probs.astype(BF)
            dprob = mm(v, do, TN)
            dscore = probs * (dprob - jnp.sum(probs * dprob, axis=0, keepdims=True)) * scale
            dscore = dscore.astype(BF)
            attn_t[at(0), cut] = mm(v, probs_b, NN)
            dqkv_t[at(0), cut] = mm(k, dscore, NN)
            dqkv_t[at(1), cut] = mm(q, dscore, NT)
            dqkv_t[at(2), cut] = mm(do, probs_b, NT)
        return carry

    lax.fori_loop(0, HEADS, head, 0, unroll=16)

    attn = attn_t[...].astype(BF)
    loads[4].wait()
    for i in range(3):
        chosen = weights[4, 384 * i : 384 * (i + 1), :]
        x_out[384 * i : 384 * (i + 1), :] = mm(chosen, hid, NT).astype(BF)
        x_out[D + 384 * i : D + 384 * (i + 1), :] = mm(chosen, attn, NN).astype(BF)
    for b in range(4):
        keep(b, dqkv_t[864 * b : 864 * (b + 1), :].astype(BF), slice(0, 864))


def grad_in_kernel(home, dg_own, dg_other, prepared, out, w_t, sent, sems):
    loads = [pltpu.make_async_copy(prepared.at[pl.ds(864 * i, 864)], w_t.at[i], sems.at[i]) for i in range(4)]
    for load in loads:
        load.start()
    total = None
    for b in range(4):
        kept = dg_own[slot(home, b) & 1, :864, :]
        away = dg_other[slot(home, b) & 1, :864, :]
        rows = jnp.where(slot(home, b) < 2, kept, away)
        loads[b].wait()
        part = mm(rows, w_t[b], TN)
        total = part if total is None else total + part
    total = total.astype(BF)
    at = lambda a: pick(
        512, ROWS, lambda i: jnp.where(((i >> 2) & 1) == a, (i & 1) * 128 + (i >> 3) * 2 + ((i >> 1) & 1), -1)
    )
    sent[...] = (mm(at(0), total[:, :640], NN) + mm(at(1), total[:, 512:], NN)).astype(BF)
    store = pltpu.make_async_copy(sent, out, sems.at[4])
    store.start()
    store.wait()


def unpack_kernel(got, out):
    recv = got[...]
    at = lambda a: pick(ROWS, 512, lambda i: ((i >> 1) & 63) * 8 + a * 4 + (i >> 7) * 2 + (i & 1))
    out[:, :640] = mm(at(0), recv, NN).astype(BF)
    out[:, 640:] = mm(at(1), recv[:, 128:], NN).astype(BF)


def product_kernel(x_own, x_oth, dg_own, dg_oth, *parts):
    row = lax.broadcasted_iota(jnp.int32, (128, 2 * ROWS), 0)
    both = lambda at: jnp.concatenate([x_own[at, :], x_oth[at, :]], axis=1)
    for r in range(2):
        d_all = jnp.concatenate([dg_own[r], dg_oth[r]], axis=1)
        edge = d_all[768:896]
        none = jnp.zeros_like(edge)
        edge = jnp.concatenate([jnp.where(row < 96, edge, none), jnp.where(row < 96, none, edge)], axis=1)
        for s in range(0, 8, 8 // CUTS):
            rows = D // CUTS
            hid = both(slice(144 * s, 144 * s + rows))
            attn = both(slice(D + 144 * s, D + 144 * s + rows))
            pieces = [
                (0, mm(hid, d_all[:384], NT)),
                (384, mm(hid, d_all[384:768], NT)),
                (768, mm(jnp.concatenate([hid, attn], axis=1), edge, NT)),
                (896, mm(attn, d_all[896:], NT)),
            ]
            for lo, piece in pieces:
                cols = slice(lo, lo + piece.shape[1])
                piece = piece.astype(BF)
                for t in range(8 // CUTS):
                    part = piece[144 * t : 144 * (t + 1)]
                    if s + t < 4:
                        parts[s + t][r, :, cols] = part
                    else:
                        ra, half = divmod(s + t - 4, 2)
                        parts[4 + 2 * ra + r][144 * half : 144 * (half + 1), cols] = part


def shape(*dims, dtype=BF):
    return jax.ShapeDtypeStruct(dims, dtype)


def call(kernel, outs, ins, flops, mib, scratch=(), specs=None):
    return pl.pallas_call(
        kernel,
        out_shape=outs,
        in_specs=specs or [VMEM] * len(ins),
        out_specs=[VMEM] * len(outs) if isinstance(outs, list) else ANY,
        scratch_shapes=list(scratch),
        compiler_params=pltpu.CompilerParams(vmem_limit_bytes=mib * MIB),
        cost_estimate=pl.CostEstimate(flops=flops, bytes_accessed=10**7, transcendentals=0),
    )(*ins)


def prepare_call(place, w_qkv, w_out):
    return call(
        prepare_kernel,
        shape(14 * D, D),
        (place, w_qkv, w_out),
        10**9,
        32,
        scratch=[pltpu.VMEM((3, D, D), BF), pltpu.VMEM((5 * D, D), BF), pltpu.SemaphoreType.DMA((5,))],
        specs=[SMEM, ANY, ANY],
    )


def attend_call(place, both, prepared):
    return call(
        attend_kernel,
        [shape(2 * D, ROWS), shape(2, D, ROWS), shape(2, D, ROWS)],
        (place, both, prepared),
        10 * 10**9,
        28,
        scratch=[
            pltpu.VMEM((5, D, D), BF),
            pltpu.SemaphoreType.DMA((5,)),
            pltpu.VMEM((3 * D, ROWS), F32),
            pltpu.VMEM((D, ROWS), F32),
            pltpu.VMEM((3 * D, ROWS), F32),
            pltpu.VMEM((D, ROWS), F32),
        ],
        specs=[SMEM, VMEM, ANY],
    )


def total(own, others):
    return own.astype(F32) + sum(g.astype(F32) for g in others)


def per_device(hidden_in, grad_out, w_qkv, w_out):
    place = jnp.stack([lax.axis_index(a) for a in ("x", "z", "yh", "yl", "c")]).astype(jnp.int32)
    both = call(
        pack_kernel,
        shape(512, D),
        (hidden_in.reshape(ROWS, D), grad_out.reshape(ROWS, D)),
        10**9,
        58,
        scratch=[pltpu.VMEM((2, ROWS, D), BF), pltpu.VMEM((512, D), BF), pltpu.SemaphoreType.DMA((3,))],
        specs=[ANY, ANY],
    )
    both = lax.all_to_all(both, FRAME, split_axis=0, concat_axis=0, tiled=True)
    prepared = prepare_call(place, w_qkv, w_out)
    x_own, dg_own, dg_other = attend_call(place, both, prepared)
    x_oth, dg_oth = flip(x_own, "c", 1), flip(dg_other, "c", 1)
    parts = call(
        product_kernel,
        [shape(2, 144, D)] * 4 + [shape(288, D)] * 4,
        (x_own, x_oth, dg_own, dg_oth),
        6 * 10**9,
        20,
    )
    part_a, part_b = parts[:4], parts[4:]
    got_a, got_b = [], []
    for s in (2, 1, 3):
        got_a.append(flip(part_a[s], "x", s))
        got_b.append(flip(part_b[s], Y, s))

    dg_own, dg_other, _ = lax.optimization_barrier((dg_own, dg_other, got_a[0]))
    grad_in = call(
        grad_in_kernel,
        shape(512, 640),
        (place, dg_own, dg_other, prepared),
        3 * 10**9,
        20,
        scratch=[pltpu.VMEM((4, 864, D), BF), pltpu.VMEM((512, 640), BF), pltpu.SemaphoreType.DMA((5,))],
        specs=[SMEM, VMEM, VMEM, ANY],
    )

    sum_a = total(part_a[0], got_a).astype(BF).reshape(2, 2, 72, D)
    sum_b = total(part_b[0], got_b).astype(BF).reshape(4, 72, D)
    got_a, got_b = [], []
    for s in (2, 1, 3):
        got_a.append(flip(sum_a[s & 1, s >> 1], Y, s))
        got_b.append(flip(sum_b[s], "x", s))
    sum_a = total(sum_a[0, 0], got_a).reshape(4, 18, D)
    sum_b = total(sum_b[0], got_b).reshape(4, 18, D)
    got = [flip(jnp.concatenate([sum_a[s], sum_b[s]]).astype(BF), "z", s) for s in (2, 1, 3)]
    near = total(sum_a[0], [g[:18] for g in got])
    far = flip(total(sum_b[0], [g[18:] for g in got]).astype(BF), "z", 4)
    grad_wqkv = total(near[:, :864], [far[:, :864]])
    grad_wout = total(near[:, 864:], [far[:, 864:]])
    grad_in = lax.all_to_all(grad_in, FRAME, split_axis=0, concat_axis=0, tiled=True)
    (grad_in,) = call(unpack_kernel, [shape(ROWS, D)], (grad_in,), 10**9, 16)
    return grad_in.reshape(2, 128, D), grad_wqkv, grad_wout


def solution(mesh):
    fine = Mesh(mesh.devices.reshape(4, 8, 2, 2, 2), ("x", "z", "yh", "yl", "c"))
    patch = ("yl", "c")
    in_specs = (P(FRAME, patch, None), P(FRAME, patch, None), P(), P())
    out_specs = (P(FRAME, patch, None), P(FRAME, patch), P(FRAME, patch))
    return jax.shard_map(
        per_device, mesh=fine, in_specs=in_specs, out_specs=out_specs, check_vma=False
    )
```

time: 180 us -> 159 us (0.88)
  waiting for transfers between devices: 84.4 us -> 52.6 us
  Pallas kernels: 35.4 us -> 45.9 us
  matrix products: 5.83 us -> 0 us
  starting transfers between devices: 43.1 us -> 47.7 us
  other arithmetic: 1.66 us -> 5.35 us
  local copies, waits for them, and re-layouts: 8.07 us -> 5.26 us
    all_to_all x1, waiting for transfers between devices: 31.5 us -> 18.7 us  [per_device(): both = lax.all_to_all(both, FRAME, split_axis=0, concat_axis=0, tiled=True)]
    all_to_all x1 -> x0, waiting for transfers between devices: 10.7 us -> none  [per_device(): last = lax.all_to_all(last, 'z', split_axis=0, concat_axis=0, tiled=True)]
    pallas_call x3 -> x6, Pallas kernels: 35.4 us -> 45.9 us  [call(): pl.pallas_call(kernel, out_shape=outs, in_specs=specs or [VMEM] * len(ins...]
    ppermute x14 -> x18, starting transfers between devices: 17.2 us -> 25.8 us  [flip(): return lax.ppermute(array, axes, [(i, i ^ step) for i in range(size)])]
    ppermute x14 -> x18, waiting for transfers between devices: 42.2 us -> 34 us  [flip(): return lax.ppermute(array, axes, [(i, i ^ step) for i in range(size)])]
    all_to_all x1 -> x0, starting transfers between devices: 6.25 us -> none  [per_device(): last = lax.all_to_all(last, 'z', split_axis=0, concat_axis=0, tiled=True)]
    dot_general x1 -> x0, matrix products: 5.83 us -> none  [mm(): lax.dot_general(a, b, (contract, ((), ())), preferred_element_type=F32)]
    unnamed x12 -> x6, local copies, waits for them, and re-layouts: 2.12 us -> 5.01 us
  transfers between devices with their start and end apart: 17 -> 20, of which waited for: 11 -> 12; matrix products, arithmetic and copies ran while one was open for 6% -> 4% of each run, Pallas kernels for 0% -> 11%
where the time goes in v1:
time: 159 us; the launch traced here: 158 us
  waiting for transfers between devices  52.6 us (33%)
  starting transfers between devices  47.7 us (30%)
  Pallas kernels  45.9 us (29%)
  other arithmetic  5.35 us (3%)
  local copies, waits for them, and re-layouts  5.26 us (3%)
    pallas_call x6, Pallas kernels, call(): pl.pallas_call(kernel, out_shape=outs, in_specs=specs or [VMEM] * len(ins...  45.9 us
    ppermute x18, waiting for transfers between devices, flip(): return lax.ppermute(array, axes, [(i, i ^ step) for i in range(size)])  34 us
    ppermute x18, starting transfers between devices, flip(): return lax.ppermute(array, axes, [(i, i ^ step) for i in range(size)])  25.8 us
    all_to_all x1, waiting for transfers between devices, per_device(): both = lax.all_to_all(both, FRAME, split_axis=0, concat_axis=0, tiled=True)  18.7 us
    all_to_all x1, starting transfers between devices, per_device(): both = lax.all_to_all(both, FRAME, split_axis=0, concat_axis=0, tiled=True)  13.7 us
    all_to_all x1, starting transfers between devices, per_device(): lax.all_to_all(grad_in, FRAME, split_axis=0, concat_axis=0, tiled=True)  8.2 us
    unnamed x6, local copies, waits for them, and re-layouts  5.01 us
  transfers between devices with their start and end apart: 20, of which 12 were waited for; matrix products, arithmetic and copies ran while one was open for 4% of the time, Pallas kernels for 11%

profile of v1, /device:TPU:8, one launch (start us, length us, event | category | flops | bytes accessed | tf_op | source)
XLA Modules:
  0.0 157.6 jit_solution(2444372644162612076)
XLA Ops:
  0.6 3.2 %shard_map.67 = bf16[512,1152]{1,0:T(8,128)(2,1)} custom-call(bf16[256,1152]{1,0:T(8,128)(2,1)} %bitcast.30, bf16[256,1152]{1,0:T(8,128)(2,1)} %bitcast.31), custom_call_target="tpu_custom_call" | custom-call | flops 1000000000 | bytes 10000000 | tf_op jit(solution)/shard_map/pallas_call | solution.py:217
  3.8 13.7 %all-to-all-start = ((bf16[64,8,1152]{2,1,0:T(8,128)(2,1)}), bf16[64,8,1152]{2,1,0:T(8,128)(2,1)S(1)}, u32[]{:S(2)}, u32[]{:S(2)}) async-start(bf16[64,8,1152]{2,1,0:T(8,128)(2,1)} %bitcast.29), calls=%async_computation | async-start | bytes 2359296 | tf_op jit(solution)/shard_map/all_to_all | solution.py:274
  17.6 3.3 %copy-done = bf16[1152,3456]{1,0:T(8,128)(2,1)S(1)} copy-done((bf16[1152,3456]{1,0:T(8,128)(2,1)S(1)}, bf16[1152,3456]{1,0:T(8,128)(2,1)}, u32[]{:S(2)}) %copy-start) | copy-done | bytes 7962648
  20.9 1.7 %copy-done.1 = bf16[1152,1152]{1,0:T(8,128)(2,1)S(1)} copy-done((bf16[1152,1152]{1,0:T(8,128)(2,1)S(1)}, bf16[1152,1152]{1,0:T(8,128)(2,1)}, u32[]{:S(2)}) %copy-start.1) | copy-done | bytes 2654232
  22.6 9.5 %shard_map.68.prepared = bf16[16128,1152]{1,0:T(8,128)(2,1)} custom-call(s32[5]{0:T(128)S(1)} %stack.23.place.home, bf16[1152,3456]{1,0:T(8,128)(2,1)S(1)} %copy-done, bf16[1152,1152]{1,0:T(8,128)(2,1)S(1)} %copy-done.1), custom_call_target="tpu_custom_call" | custom-call | flops 1000000000 | bytes 10000000 | tf_op jit(solution)/shard_map/pallas_call | solution.py:217
  32.1 18.7 %all-to-all-done = bf16[64,8,1152]{2,1,0:T(8,128)(2,1)S(1)} async-done(((bf16[64,8,1152]{2,1,0:T(8,128)(2,1)}), bf16[64,8,1152]{2,1,0:T(8,128)(2,1)S(1)}, u32[]{:S(2)}, u32[]{:S(2)}) %all-to-all-start) | async-done | bytes 1179680 | tf_op jit(solution)/shard_map/all_to_all | solution.py:274
  50.7 18.8 %shard_map.69 = (bf16[2304,256]{1,0:T(8,128)(2,1)S(1)}, bf16[2,1152,256]{2,1,0:T(8,128)(2,1)S(1)}, bf16[2,1152,256]{2,1,0:T(8,128)(2,1)S(1)}) custom-call(s32[5]{0:T(128)S(1)} %stack.23.place.home, bf16[512,1152]{1,0:T(8,128)(2,1)S(1)} %bitcast.25, bf16[16128,1152]{1,0:T(8,128)(2,1)} %shard_map.68.prepared), custom_call_target="tpu_custom_call" | custom-call | flops 10000000000 | bytes 10000000 | tf_op jit(solution)/shard_map/pallas_call | solution.py:217
  70.1 2.3 %collective-permute-done.1.dg_oth = bf16[2,1152,256]{2,1,0:T(8,128)(2,1)S(1)} collective-permute-done((bf16[2,1152,256]{2,1,0:T(8,128)(2,1)S(1)}, bf16[2,1152,256]{2,1,0:T(8,128)(2,1)S(1)}, u32[]{:S(2)}, u32[]{:S(2)}) %collective-permute-start.1) | collective-permute-done | bytes 1179680 | tf_op jit(solution)/shard_map/ppermute | solution.py:25
  72.5 1.7 %collective-permute-done.x_oth = bf16[2304,256]{1,0:T(8,128)(2,1)S(1)} collective-permute-done((bf16[2304,256]{1,0:T(8,128)(2,1)S(1)}, bf16[2304,256]{1,0:T(8,128)(2,1)S(1)}, u32[]{:S(2)}, u32[]{:S(2)}) %collective-permute-start) | collective-permute-done | bytes 1179680 | tf_op jit(solution)/shard_map/ppermute | solution.py:25
  74.2 5.6 %shard_map.70 = (bf16[2,144,1152]{2,1,0:T(8,128)(2,1)S(1)}, bf16[2,144,1152]{2,1,0:T(8,128)(2,1)}, bf16[2,144,1152]{2,1,0:T(8,128)(2,1)S(1)}, bf16[2,144,1152]{2...) custom-call(bf16[2304,256]{1,0:T(8,128)(2,1)S(1)} %get-tuple-element, ...), custom_call_target="tpu_custom_call" | custom-call | flops 6000000000 | bytes 10000000 | tf_op jit(solution)/shard_map/pallas_call | solution.py:217
  80.5 1.2 collective-permute-start.3
  81.7 2.2 %collective-permute-start.4 = (bf16[2,144,1152]{2,1,0:T(8,128)(2,1)}, bf16[2,144,1152]{2,1,0:T(8,128)(2,1)}, u32[]{:S(2)}, u32[]{:S(2)}) collective-permute-start(bf16[2,144,1152]{2,1,0:T(8,128)(2,1)} %get-tuple-element.24), channel_id=1, source_target_pairs={{0,192},{64,128},{128,64},{192,0},{1,193},{65,129},{129,65},{193,1... | collective-permute-start | bytes 1990664 | tf_op jit(solution)/shard_map/ppermute | solution.py:25
  84.4 1.3 collective-permute-start.9
  85.8 13.3 %collective-permute-done.2 = bf16[2,144,1152]{2,1,0:T(8,128)(2,1)S(1)} collective-permute-done((bf16[2,144,1152]{2,1,0:T(8,128)(2,1)S(1)}, bf16[2,144,1152]{2,1,0:T(8,128)(2,1)S(1)}, u32[]{:S(2)}, u32[]{:S(2)}) %collective-permute-start.2) | collective-permute-done | bytes 663584 | tf_op jit(solution)/shard_map/ppermute | solution.py:25
  99.1 7.5 %shard_map.71 = bf16[512,640]{1,0:T(8,128)(2,1)} custom-call(s32[5]{0:T(128)S(1)} %stack.23.place.home, bf16[2,1152,256]{2,1,0:T(8,128)(2,1)S(1)} %get-tuple-element.20.dg_own, bf16[2,1152,256]{2,1,0:T(8,128)(2,1)S(1)} %get-tuple-element.21.dg_other, bf16[16128,1152]{1,0:T(8,128)(2,1)} %shard_map.68.prepared), custom_call_target="tpu_custom_call" | custom-call | flops 3000000000 | bytes 10000000 | tf_op jit(solution)/shard_map/pallas_call | solution.py:217
  106.7 8.2 %all-to-all-start.1 = ((bf16[64,8,640]{2,1,0:T(8,128)(2,1)}), bf16[64,8,640]{2,1,0:T(8,128)(2,1)S(1)}, u32[]{:S(2)}, u32[]{:S(2)}) async-start(bf16[64,8,640]{2,1,0:T(8,128)(2,1)} %bitcast.9), calls=%async_computation.1 | async-start | bytes 1310720 | tf_op jit(solution)/shard_map/all_to_all | solution.py:315
  114.9 1.9 %add_convert_fusion.1 = bf16[2,144,1152]{2,1,0:T(8,128)(2,1)S(1)} fusion(bf16[2,144,1152]{2,1,0:T(8,128)(2,1)} %collective-permute-done.4, bf16[2,144,1152]{2,1,0:T(8,128)(2,1)} %collective-permute-done.3, bf16[2,144,1152]{2,1,0:T(8,128)(2,1)} %copy-done.2, bf16[2,144,1152]{2,1,0:T(8,128)(2,1)S(1)} %get-tuple-element.22), kind=kLoop, calls=%fused_computation.1 | loop fusion | flops 2654208 | bytes 3317760 | tf_op jit(solution)/shard_map/convert_element_type | solution.py:302
  116.8 3.2 %collective-permute-start.5 = (bf16[72,1152]{1,0:T(8,128)(2,1)S(1)}, bf16[72,1152]{1,0:T(8,128)(2,1)S(1)}, u32[]{:S(2)}, u32[]{:S(2)}) collective-permute-start(bf16[72,1152]{1,0:T(8,128)(2,1)S(1)} %get-tuple-element.36), channel_id=1, source_target_pairs={{0,4},{2,6},{4,0},{6,2},{1,5},{3,7},{5,1},{7,3},{8,12},{10,14},{12... | collective-permute-start | bytes 497672 | tf_op jit(solution)/shard_map/ppermute | solution.py:25
  119.9 1.6 %collective-permute-start.6 = (bf16[72,1152]{1,0:T(8,128)(2,1)S(1)}, bf16[72,1152]{1,0:T(8,128)(2,1)S(1)}, u32[]{:S(2)}, u32[]{:S(2)}) collective-permute-start(bf16[72,1152]{1,0:T(8,128)(2,1)S(1)} %get-tuple-element.38), channel_id=1, source_target_pairs={{0,2},{2,0},{4,6},{6,4},{1,3},{3,1},{5,7},{7,5},{8,10},{10,8},{12,... | collective-permute-start | bytes 497672 | tf_op jit(solution)/shard_map/ppermute | solution.py:25
  121.6 1.8 %add_convert_fusion = bf16[288,1152]{1,0:T(8,128)(2,1)S(1)} fusion(bf16[288,1152]{1,0:T(8,128)(2,1)} %collective-permute-done.10, bf16[288,1152]{1,0:T(8,128)(2,1)} %collective-permute-done.9, bf16[288,1152]{1,0:T(8,128)(2,1)} %collective-permute-done.8, bf16[288,1152]{1,0:T(8,128)(2,1)S(1)} %get-tuple-element.25), kind=kLoop, calls=%fused_computation | loop fusion | flops 2654208 | bytes 3317760 | tf_op jit(solution)/shard_map/convert_element_type | solution.py:303
  123.4 3.3 %collective-permute-start.11 = (bf16[72,1152]{1,0:T(8,128)(2,1)S(1)}, bf16[72,1152]{1,0:T(8,128)(2,1)S(1)}, u32[]{:S(2)}, u32[]{:S(2)}) collective-permute-start(bf16[72,1152]{1,0:T(8,128)(2,1)S(1)} %get-tuple-element.33), channel_id=1, source_target_pairs={{0,128},{64,192},{128,0},{192,64},{1,129},{65,193},{129,1},{193,65... | collective-permute-start | bytes 497672 | tf_op jit(solution)/shard_map/ppermute | solution.py:25
  128.4 1.6 %collective-permute-start.12 = (bf16[72,1152]{1,0:T(8,128)(2,1)S(1)}, bf16[72,1152]{1,0:T(8,128)(2,1)S(1)}, u32[]{:S(2)}, u32[]{:S(2)}) collective-permute-start(bf16[72,1152]{1,0:T(8,128)(2,1)S(1)} %get-tuple-element.35), channel_id=1, source_target_pairs={{0,64},{64,0},{128,192},{192,128},{1,65},{65,1},{129,193},{193,129... | collective-permute-start | bytes 497672 | tf_op jit(solution)/shard_map/ppermute | solution.py:25
  130.0 1.7 %collective-permute-done.7 = bf16[72,1152]{1,0:T(8,128)(2,1)S(1)} collective-permute-done((bf16[72,1152]{1,0:T(8,128)(2,1)S(1)}, bf16[72,1152]{1,0:T(8,128)(2,1)S(1)}, u32[]{:S(2)}, u32[]{:S(2)}) %collective-permute-start.7) | collective-permute-done | bytes 165920 | tf_op jit(solution)/shard_map/ppermute | solution.py:25
  131.8 1.9 %collective-permute-done.11 = bf16[72,1152]{1,0:T(8,128)(2,1)S(1)} collective-permute-done((bf16[72,1152]{1,0:T(8,128)(2,1)S(1)}, bf16[72,1152]{1,0:T(8,128)(2,1)S(1)}, u32[]{:S(2)}, u32[]{:S(2)}) %collective-permute-start.11) | collective-permute-done | bytes 165920 | tf_op jit(solution)/shard_map/ppermute | solution.py:25
  133.7 1.8 %collective-permute-done.13 = bf16[72,1152]{1,0:T(8,128)(2,1)S(1)} collective-permute-done((bf16[72,1152]{1,0:T(8,128)(2,1)S(1)}, bf16[72,1152]{1,0:T(8,128)(2,1)S(1)}, u32[]{:S(2)}, u32[]{:S(2)}) %collective-permute-start.13) | collective-permute-done | bytes 165920 | tf_op jit(solution)/shard_map/ppermute | solution.py:25
  136.5 2.2 %collective-permute-start.16 = (bf16[36,1152]{1,0:T(8,128)(2,1)S(1)}, bf16[36,1152]{1,0:T(8,128)(2,1)S(1)}, u32[]{:S(2)}, u32[]{:S(2)}) collective-permute-start(bf16[36,1152]{1,0:T(8,128)(2,1)S(1)} %pad_maximum_fusion.2), channel_id=1, source_target_pairs={{0,24},{8,16},{16,8},{24,0},{32,56},{40,48},{48,40},{56,32},{1,25}... | collective-permute-start | bytes 248840 | tf_op jit(solution)/shard_map/ppermute | solution.py:25
  139.5 2.0 %collective-permute-done.15 = bf16[36,1152]{1,0:T(8,128)(2,1)S(1)} collective-permute-done((bf16[36,1152]{1,0:T(8,128)(2,1)S(1)}, bf16[36,1152]{1,0:T(8,128)(2,1)S(1)}, u32[]{:S(2)}, u32[]{:S(2)}) %collective-permute-start.15) | collective-permute-done | bytes 82976 | tf_op jit(solution)/shard_map/ppermute | solution.py:25
  141.5 1.9 %collective-permute-done.16 = bf16[36,1152]{1,0:T(8,128)(2,1)S(1)} collective-permute-done((bf16[36,1152]{1,0:T(8,128)(2,1)S(1)}, bf16[36,1152]{1,0:T(8,128)(2,1)S(1)}, u32[]{:S(2)}, u32[]{:S(2)}) %collective-permute-start.16) | collective-permute-done | bytes 82976 | tf_op jit(solution)/shard_map/ppermute | solution.py:25
  143.4 3.3 %collective-permute-done.14 = bf16[36,1152]{1,0:T(8,128)(2,1)S(1)} collective-permute-done((bf16[36,1152]{1,0:T(8,128)(2,1)S(1)}, bf16[36,1152]{1,0:T(8,128)(2,1)S(1)}, u32[]{:S(2)}, u32[]{:S(2)}) %collective-permute-start.14) | collective-permute-done | bytes 82976 | tf_op jit(solution)/shard_map/ppermute | solution.py:25
  146.8 4.8 %collective-permute-start.17 = (bf16[18,1152]{1,0:T(8,128)(2,1)S(1)}, bf16[18,1152]{1,0:T(8,128)(2,1)S(1)}, u32[]{:S(2)}, u32[]{:S(2)}) collective-permute-start(bf16[18,1152]{1,0:T(8,128)(2,1)S(1)} %get-tuple-element.39), channel_id=1, source_target_pairs={{0,32},{8,40},{16,48},{24,56},{32,0},{40,8},{48,16},{56,24},{1,33}... | collective-permute-start | bytes 124424 | tf_op jit(solution)/shard_map/ppermute | solution.py:25
  151.6 3.4 %collective-permute-done.17 = bf16[18,1152]{1,0:T(8,128)(2,1)S(1)} collective-permute-done((bf16[18,1152]{1,0:T(8,128)(2,1)S(1)}, bf16[18,1152]{1,0:T(8,128)(2,1)S(1)}, u32[]{:S(2)}, u32[]{:S(2)}) %collective-permute-start.17) | collective-permute-done | bytes 41504 | tf_op jit(solution)/shard_map/ppermute | solution.py:25
  156.3 1.3 shard_map.72
  (34 shorter events, 7.0 us)
Async XLA Ops:
  3.8 46.9 %all-to-all-start = ((bf16[64,8,1152]{2,1,0:T(8,128)(2,1)}), bf16[64,8,1152]{2,1,0:T(8,128)(2,1)S(1)}, u32[]{:S(2)}, u32[]{:S(2)}) async-start(bf16[64,8,1152]{2,1,0:T(8,128)(2,1)} %bitcast.29), calls=%async_computation | async-start | bytes 2359296 | tf_op jit(solution)/shard_map/all_to_all | solution.py:274
  17.6 3.3 %copy-start = (bf16[1152,3456]{1,0:T(8,128)(2,1)S(1)}, bf16[1152,3456]{1,0:T(8,128)(2,1)}, u32[]{:S(2)}) copy-start(bf16[1152,3456]{1,0:T(8,128)(2,1)} %w_qkv.1) | copy-start | bytes 23887876
  20.9 1.7 %copy-start.1 = (bf16[1152,1152]{1,0:T(8,128)(2,1)S(1)}, bf16[1152,1152]{1,0:T(8,128)(2,1)}, u32[]{:S(2)}) copy-start(bf16[1152,1152]{1,0:T(8,128)(2,1)} %w_out.1) | copy-start | bytes 7962628
  69.5 2.9 %collective-permute-start.1 = (bf16[2,1152,256]{2,1,0:T(8,128)(2,1)S(1)}, bf16[2,1152,256]{2,1,0:T(8,128)(2,1)S(1)}, u32[]{:S(2)}, u32[]{:S(2)}) collective-permute-start(bf16[2,1152,256]{2,1,0:T(8,128)(2,1)S(1)} %get-tuple-element.21.dg_other), channel_id=1, source_target_pairs={{0,1},{1,0},{2,3},{3,2},{4,5},{5,4},{6,7},{7,6},{8,9},{9,8},{10,11... | collective-permute-start | bytes 3538952 | tf_op jit(solution)/shard_map/ppermute | solution.py:25
  69.6 4.5 %collective-permute-start = (bf16[2304,256]{1,0:T(8,128)(2,1)S(1)}, bf16[2304,256]{1,0:T(8,128)(2,1)S(1)}, u32[]{:S(2)}, u32[]{:S(2)}) collective-permute-start(bf16[2304,256]{1,0:T(8,128)(2,1)S(1)} %get-tuple-element.18.x_own), channel_id=1, source_target_pairs={{0,1},{1,0},{2,3},{3,2},{4,5},{5,4},{6,7},{7,6},{8,9},{9,8},{10,11... | collective-permute-start | bytes 3538952 | tf_op jit(solution)/shard_map/ppermute | solution.py:25
  79.8 19.3 %collective-permute-start.2 = (bf16[2,144,1152]{2,1,0:T(8,128)(2,1)S(1)}, bf16[2,144,1152]{2,1,0:T(8,128)(2,1)S(1)}, u32[]{:S(2)}, u32[]{:S(2)}) collective-permute-start(bf16[2,144,1152]{2,1,0:T(8,128)(2,1)S(1)} %get-tuple-element.19), channel_id=1, source_target_pairs={{0,128},{64,192},{128,0},{192,64},{1,129},{65,193},{129,1},{193,65... | collective-permute-start | bytes 1990664 | tf_op jit(solution)/shard_map/ppermute | solution.py:25
  80.5 34.3 %collective-permute-start.3 = (bf16[2,144,1152]{2,1,0:T(8,128)(2,1)}, bf16[2,144,1152]{2,1,0:T(8,128)(2,1)}, u32[]{:S(2)}, u32[]{:S(2)}) collective-permute-start(bf16[2,144,1152]{2,1,0:T(8,128)(2,1)} %get-tuple-element.23), channel_id=1, source_target_pairs={{0,64},{64,0},{128,192},{192,128},{1,65},{65,1},{129,193},{193,129... | collective-permute-start | bytes 1990664 | tf_op jit(solution)/shard_map/ppermute | solution.py:25
  81.7 33.2 %collective-permute-start.4 = (bf16[2,144,1152]{2,1,0:T(8,128)(2,1)}, bf16[2,144,1152]{2,1,0:T(8,128)(2,1)}, u32[]{:S(2)}, u32[]{:S(2)}) collective-permute-start(bf16[2,144,1152]{2,1,0:T(8,128)(2,1)} %get-tuple-element.24), channel_id=1, source_target_pairs={{0,192},{64,128},{128,64},{192,0},{1,193},{65,129},{129,65},{193,1... | collective-permute-start | bytes 1990664 | tf_op jit(solution)/shard_map/ppermute | solution.py:25
  83.9 36.0 %collective-permute-start.8 = (bf16[288,1152]{1,0:T(8,128)(2,1)}, bf16[288,1152]{1,0:T(8,128)(2,1)}, u32[]{:S(2)}, u32[]{:S(2)}) collective-permute-start(bf16[288,1152]{1,0:T(8,128)(2,1)} %get-tuple-element.26), channel_id=1, source_target_pairs={{0,4},{2,6},{4,0},{6,2},{1,5},{3,7},{5,1},{7,3},{8,12},{10,14},{12... | collective-permute-start | bytes 1990664 | tf_op jit(solution)/shard_map/ppermute | solution.py:25
  84.4 37.2 %collective-permute-start.9 = (bf16[288,1152]{1,0:T(8,128)(2,1)S(1)}, bf16[288,1152]{1,0:T(8,128)(2,1)}, u32[]{:S(2)}, u32[]{:S(2)}) collective-permute-start(bf16[288,1152]{1,0:T(8,128)(2,1)S(1)} %get-tuple-element.27), channel_id=1, source_target_pairs={{0,2},{2,0},{4,6},{6,4},{1,3},{3,1},{5,7},{7,5},{8,10},{10,8},{12,... | collective-permute-start | bytes 1990664 | tf_op jit(solution)/shard_map/ppermute | solution.py:25
  99.1 7.5 %copy-start.2 = (bf16[2,144,1152]{2,1,0:T(8,128)(2,1)}, bf16[2,144,1152]{2,1,0:T(8,128)(2,1)S(1)}, u32[]{:S(2)}) copy-start(bf16[2,144,1152]{2,1,0:T(8,128)(2,1)S(1)} %collective-permute-done.2) | copy-start | bytes 1990660
  99.1 22.5 %collective-permute-start.10 = (bf16[288,1152]{1,0:T(8,128)(2,1)S(1)}, bf16[288,1152]{1,0:T(8,128)(2,1)}, u32[]{:S(2)}, u32[]{:S(2)}) collective-permute-start(bf16[288,1152]{1,0:T(8,128)(2,1)S(1)} %get-tuple-element.28), channel_id=1, source_target_pairs={{0,6},{2,4},{4,2},{6,0},{1,7},{3,5},{5,3},{7,1},{8,14},{10,12},{12... | collective-permute-start | bytes 1990664 | tf_op jit(solution)/shard_map/ppermute | solution.py:25
  106.7 49.6 %all-to-all-start.1 = ((bf16[64,8,640]{2,1,0:T(8,128)(2,1)}), bf16[64,8,640]{2,1,0:T(8,128)(2,1)S(1)}, u32[]{:S(2)}, u32[]{:S(2)}) async-start(bf16[64,8,640]{2,1,0:T(8,128)(2,1)} %bitcast.9), calls=%async_computation.1 | async-start | bytes 1310720 | tf_op jit(solution)/shard_map/all_to_all | solution.py:315
  116.8 11.6 %collective-permute-start.5 = (bf16[72,1152]{1,0:T(8,128)(2,1)S(1)}, bf16[72,1152]{1,0:T(8,128)(2,1)S(1)}, u32[]{:S(2)}, u32[]{:S(2)}) collective-permute-start(bf16[72,1152]{1,0:T(8,128)(2,1)S(1)} %get-tuple-element.36), channel_id=1, source_target_pairs={{0,4},{2,6},{4,0},{6,2},{1,5},{3,7},{5,1},{7,3},{8,12},{10,14},{12... | collective-permute-start | bytes 497672 | tf_op jit(solution)/shard_map/ppermute | solution.py:25
  119.9 11.8 %collective-permute-start.7 = (bf16[72,1152]{1,0:T(8,128)(2,1)S(1)}, bf16[72,1152]{1,0:T(8,128)(2,1)S(1)}, u32[]{:S(2)}, u32[]{:S(2)}) collective-permute-start(bf16[72,1152]{1,0:T(8,128)(2,1)S(1)} %get-tuple-element.37), channel_id=1, source_target_pairs={{0,6},{2,4},{4,2},{6,0},{1,7},{3,5},{5,3},{7,1},{8,14},{10,12},{12... | collective-permute-start | bytes 497672 | tf_op jit(solution)/shard_map/ppermute | solution.py:25
  119.9 11.8 %collective-permute-start.6 = (bf16[72,1152]{1,0:T(8,128)(2,1)S(1)}, bf16[72,1152]{1,0:T(8,128)(2,1)S(1)}, u32[]{:S(2)}, u32[]{:S(2)}) collective-permute-start(bf16[72,1152]{1,0:T(8,128)(2,1)S(1)} %get-tuple-element.38), channel_id=1, source_target_pairs={{0,2},{2,0},{4,6},{6,4},{1,3},{3,1},{5,7},{7,5},{8,10},{10,8},{12,... | collective-permute-start | bytes 497672 | tf_op jit(solution)/shard_map/ppermute | solution.py:25
  123.4 10.2 %collective-permute-start.11 = (bf16[72,1152]{1,0:T(8,128)(2,1)S(1)}, bf16[72,1152]{1,0:T(8,128)(2,1)S(1)}, u32[]{:S(2)}, u32[]{:S(2)}) collective-permute-start(bf16[72,1152]{1,0:T(8,128)(2,1)S(1)} %get-tuple-element.33), channel_id=1, source_target_pairs={{0,128},{64,192},{128,0},{192,64},{1,129},{65,193},{129,1},{193,65... | collective-permute-start | bytes 497672 | tf_op jit(solution)/shard_map/ppermute | solution.py:25
  126.7 8.7 %collective-permute-start.13 = (bf16[72,1152]{1,0:T(8,128)(2,1)S(1)}, bf16[72,1152]{1,0:T(8,128)(2,1)S(1)}, u32[]{:S(2)}, u32[]{:S(2)}) collective-permute-start(bf16[72,1152]{1,0:T(8,128)(2,1)S(1)} %get-tuple-element.34), channel_id=1, source_target_pairs={{0,192},{64,128},{128,64},{192,0},{1,193},{65,129},{129,65},{193,1... | collective-permute-start | bytes 497672 | tf_op jit(solution)/shard_map/ppermute | solution.py:25
  128.4 7.0 %collective-permute-start.12 = (bf16[72,1152]{1,0:T(8,128)(2,1)S(1)}, bf16[72,1152]{1,0:T(8,128)(2,1)S(1)}, u32[]{:S(2)}, u32[]{:S(2)}) collective-permute-start(bf16[72,1152]{1,0:T(8,128)(2,1)S(1)} %get-tuple-element.35), channel_id=1, source_target_pairs={{0,64},{64,0},{128,192},{192,128},{1,65},{65,1},{129,193},{193,129... | collective-permute-start | bytes 497672 | tf_op jit(solution)/shard_map/ppermute | solution.py:25
  135.7 5.8 %collective-permute-start.15 = (bf16[36,1152]{1,0:T(8,128)(2,1)S(1)}, bf16[36,1152]{1,0:T(8,128)(2,1)S(1)}, u32[]{:S(2)}, u32[]{:S(2)}) collective-permute-start(bf16[36,1152]{1,0:T(8,128)(2,1)S(1)} %pad_maximum_fusion.1), channel_id=1, source_target_pairs={{0,8},{8,0},{16,24},{24,16},{32,40},{40,32},{48,56},{56,48},{1,9},... | collective-permute-start | bytes 248840 | tf_op jit(solution)/shard_map/ppermute | solution.py:25
  136.5 6.9 %collective-permute-start.16 = (bf16[36,1152]{1,0:T(8,128)(2,1)S(1)}, bf16[36,1152]{1,0:T(8,128)(2,1)S(1)}, u32[]{:S(2)}, u32[]{:S(2)}) collective-permute-start(bf16[36,1152]{1,0:T(8,128)(2,1)S(1)} %pad_maximum_fusion.2), channel_id=1, source_target_pairs={{0,24},{8,16},{16,8},{24,0},{32,56},{40,48},{48,40},{56,32},{1,25}... | collective-permute-start | bytes 248840 | tf_op jit(solution)/shard_map/ppermute | solution.py:25
  138.8 7.9 %collective-permute-start.14 = (bf16[36,1152]{1,0:T(8,128)(2,1)S(1)}, bf16[36,1152]{1,0:T(8,128)(2,1)S(1)}, u32[]{:S(2)}, u32[]{:S(2)}) collective-permute-start(bf16[36,1152]{1,0:T(8,128)(2,1)S(1)} %pad_maximum_fusion), channel_id=1, source_target_pairs={{0,16},{8,24},{16,0},{24,8},{32,48},{40,56},{48,32},{56,40},{1,17}... | collective-permute-start | bytes 248840 | tf_op jit(solution)/shard_map/ppermute | solution.py:25
  146.8 8.2 %collective-permute-start.17 = (bf16[18,1152]{1,0:T(8,128)(2,1)S(1)}, bf16[18,1152]{1,0:T(8,128)(2,1)S(1)}, u32[]{:S(2)}, u32[]{:S(2)}) collective-permute-start(bf16[18,1152]{1,0:T(8,128)(2,1)S(1)} %get-tuple-element.39), channel_id=1, source_target_pairs={{0,32},{8,40},{16,48},{24,56},{32,0},{40,8},{48,16},{56,24},{1,33}... | collective-permute-start | bytes 124424 | tf_op jit(solution)/shard_map/ppermute | solution.py:25

commit v2 on v1

--- a/solution.py
+++ b/solution.py
@@ -18,6 +18,7 @@
 SMEM = pl.BlockSpec(memory_space=pltpu.SMEM)
 MIB = 1024 * 1024
 CUTS = 2
+TOGETHER = 4
 
 
 def flip(array, axes, step):
@@ -57,7 +58,7 @@
     first = q < 32
     rx = jnp.where(first, q >> 3, (q >> 2) & 3)
     ra = jnp.where(first, (q >> 2) & 1, (q >> 4) & 1)
-    rz = (q & 3) + jnp.where(first, 0, 4)
+    rz = ((q & 1) + 3 * (q & 2)) ^ jnp.where(first, 0, 2)
     return (x ^ rx) * 288 + (z ^ rz) * 36 + (yh ^ ra) * 18 + (at - 18 * q)
 
 
@@ -118,27 +119,32 @@
 
     scale = 1.0 / HD**0.5
 
-    def head(h, carry):
-        at = lambda i: pl.ds(pl.multiple_of(D * i + HD * h, 8), HD)
-        q_t, k_t, v_t = (qkv_t[at(i), :].astype(BF) for i in range(3))
-        d_t = do_t[at(0), :].astype(BF)
-        for p in range(2):
-            cut = slice(128 * p, 128 * (p + 1))
-            q, k, v, do = q_t[:, cut], k_t[:, cut], v_t[:, cut], d_t[:, cut]
-            scores = mm(k, q, TN) * scale
-            grown = jnp.exp(scores - jnp.max(scores, axis=0, keepdims=True))
-            probs = grown * (1.0 / jnp.sum(grown, axis=0, keepdims=True))
-            probs_b = probs.astype(BF)
-            dprob = mm(v, do, TN)
-            dscore = probs * (dprob - jnp.sum(probs * dprob, axis=0, keepdims=True)) * scale
-            dscore = dscore.astype(BF)
-            attn_t[at(0), cut] = mm(v, probs_b, NN)
-            dqkv_t[at(0), cut] = mm(k, dscore, NN)
-            dqkv_t[at(1), cut] = mm(q, dscore, NT)
-            dqkv_t[at(2), cut] = mm(do, probs_b, NT)
+    def heads(t, carry):
+        at = lambda i, h: pl.ds(pl.multiple_of(D * i + HD * (t * TOGETHER + h), 8), HD)
+        pairs = []
+        for h in range(TOGETHER):
+            q_t, k_t, v_t = (qkv_t[at(i, h), :].astype(BF) for i in range(3))
+            d_t = do_t[at(0, h), :].astype(BF)
+            for p in range(2):
+                cut = slice(128 * p, 128 * (p + 1))
+                pairs.append((h, cut, q_t[:, cut], k_t[:, cut], v_t[:, cut], d_t[:, cut]))
+        scores = [mm(k, q, TN) * scale for h, cut, q, k, v, do in pairs]
+        dprobs = [mm(v, do, TN) for h, cut, q, k, v, do in pairs]
+        probs = []
+        for s in scores:
+            grown = jnp.exp(s - jnp.max(s, axis=0, keepdims=True))
+            probs.append(grown * (1.0 / jnp.sum(grown, axis=0, keepdims=True)))
+        probs_b = [p.astype(BF) for p in probs]
+        dscores = [(p * (d - jnp.sum(p * d, axis=0, keepdims=True)) * scale).astype(BF) for p, d in zip(probs, dprobs)]
+        for (h, cut, q, k, v, do), p in zip(pairs, probs_b):
+            attn_t[at(0, h), cut] = mm(v, p, NN)
+            dqkv_t[at(2, h), cut] = mm(do, p, NT)
+        for (h, cut, q, k, v, do), d in zip(pairs, dscores):
+            dqkv_t[at(0, h), cut] = mm(k, d, NN)
+            dqkv_t[at(1, h), cut] = mm(q, d, NT)
         return carry
 
-    lax.fori_loop(0, HEADS, head, 0, unroll=16)
+    lax.fori_loop(0, HEADS // TOGETHER, heads, 0, unroll=4)
 
     attn = attn_t[...].astype(BF)
     loads[4].wait()
@@ -284,11 +290,10 @@
     )
     part_a, part_b = parts[:4], parts[4:]
     got_a, got_b = [], []
-    for s in (2, 1, 3):
+    for i, s in enumerate((1, 2, 3)):
         got_a.append(flip(part_a[s], "x", s))
-        got_b.append(flip(part_b[s], Y, s))
-
-    dg_own, dg_other, _ = lax.optimization_barrier((dg_own, dg_other, got_a[0]))
+        got_b.append(flip(part_b[(2, 1, 3)[i]], Y, (2, 1, 3)[i]))
+
     grad_in = call(
         grad_in_kernel,
         shape(512, 640),
@@ -307,9 +312,9 @@
         got_b.append(flip(sum_b[s], "x", s))
     sum_a = total(sum_a[0, 0], got_a).reshape(4, 18, D)
     sum_b = total(sum_b[0], got_b).reshape(4, 18, D)
-    got = [flip(jnp.concatenate([sum_a[s], sum_b[s]]).astype(BF), "z", s) for s in (2, 1, 3)]
+    got = [flip(jnp.concatenate([sum_a[i], sum_b[i]]).astype(BF), "z", s) for i, s in ((2, 6), (3, 7), (1, 1))]
     near = total(sum_a[0], [g[:18] for g in got])
-    far = flip(total(sum_b[0], [g[18:] for g in got]).astype(BF), "z", 4)
+    far = flip(total(sum_b[0], [g[18:] for g in got]).astype(BF), "z", 2)
     grad_wqkv = total(near[:, :864], [far[:, :864]])
     grad_wout = total(near[:, 864:], [far[:, 864:]])
     grad_in = lax.all_to_all(grad_in, FRAME, split_axis=0, concat_axis=0, tiled=True)

time: 159 us -> 164 us (1.031)
  waiting for transfers between devices: 52.6 us -> 66.1 us
  Pallas kernels: 45.9 us -> 40.7 us
    ppermute x18, waiting for transfers between devices: 34 us -> 47.5 us  [flip(): return lax.ppermute(array, axes, [(i, i ^ step) for i in range(size)])]
    pallas_call x6, Pallas kernels: 45.9 us -> 40.7 us  [call(): pl.pallas_call(kernel, out_shape=outs, in_specs=specs or [VMEM] * len(ins...]
    all_to_all x1, starting transfers between devices: 8.2 us -> 5.3 us  [per_device(): lax.all_to_all(grad_in, FRAME, split_axis=0, concat_axis=0, tiled=True)]
  transfers between devices with their start and end apart: 20 -> 20, of which waited for: 12 -> 15; matrix products, arithmetic and copies ran while one was open for 4% -> 2% of each run, Pallas kernels for 11% -> 11%
where the time goes in v2:
time: 164 us; the launch traced here: 163 us
  waiting for transfers between devices  66.1 us (40%)
  starting transfers between devices  46.4 us (28%)
  Pallas kernels  40.7 us (25%)
  local copies, waits for them, and re-layouts  5.26 us (3%)
  other arithmetic  3.87 us (2%)
    ppermute x18, waiting for transfers between devices, flip(): return lax.ppermute(array, axes, [(i, i ^ step) for i in range(size)])  47.5 us
    pallas_call x6, Pallas kernels, call(): pl.pallas_call(kernel, out_shape=outs, in_specs=specs or [VMEM] * len(ins...  40.7 us
    ppermute x18, starting transfers between devices, flip(): return lax.ppermute(array, axes, [(i, i ^ step) for i in range(size)])  27.4 us
    all_to_all x1, waiting for transfers between devices, per_device(): both = lax.all_to_all(both, FRAME, split_axis=0, concat_axis=0, tiled=True)  18.6 us
    all_to_all x1, starting transfers between devices, per_device(): both = lax.all_to_all(both, FRAME, split_axis=0, concat_axis=0, tiled=True)  13.7 us
    all_to_all x1, starting transfers between devices, per_device(): lax.all_to_all(grad_in, FRAME, split_axis=0, concat_axis=0, tiled=True)  5.3 us
    unnamed x6, local copies, waits for them, and re-layouts  5.01 us
  transfers between devices with their start and end apart: 20, of which 15 were waited for; matrix products, arithmetic and copies ran while one was open for 2% of the time, Pallas kernels for 11%

profile of v2, /device:TPU:8, one launch (start us, length us, event | category | flops | bytes accessed | tf_op | source)
XLA Modules:
  0.0 163.1 jit_solution(16918141625464142813)
XLA Ops:
  0.6 3.2 %shard_map.67 = bf16[512,1152]{1,0:T(8,128)(2,1)} custom-call(bf16[256,1152]{1,0:T(8,128)(2,1)} %bitcast.30, bf16[256,1152]{1,0:T(8,128)(2,1)} %bitcast.31), custom_call_target="tpu_custom_call" | custom-call | flops 1000000000 | bytes 10000000 | tf_op jit(solution)/shard_map/pallas_call | solution.py:223
  3.8 13.7 %all-to-all-start = ((bf16[64,8,1152]{2,1,0:T(8,128)(2,1)}), bf16[64,8,1152]{2,1,0:T(8,128)(2,1)S(1)}, u32[]{:S(2)}, u32[]{:S(2)}) async-start(bf16[64,8,1152]{2,1,0:T(8,128)(2,1)} %bitcast.29), calls=%async_computation | async-start | bytes 2359296 | tf_op jit(solution)/shard_map/all_to_all | solution.py:280
  17.6 3.3 %copy-done = bf16[1152,3456]{1,0:T(8,128)(2,1)S(1)} copy-done((bf16[1152,3456]{1,0:T(8,128)(2,1)S(1)}, bf16[1152,3456]{1,0:T(8,128)(2,1)}, u32[]{:S(2)}) %copy-start) | copy-done | bytes 7962648
  20.9 1.7 %copy-done.1 = bf16[1152,1152]{1,0:T(8,128)(2,1)S(1)} copy-done((bf16[1152,1152]{1,0:T(8,128)(2,1)S(1)}, bf16[1152,1152]{1,0:T(8,128)(2,1)}, u32[]{:S(2)}) %copy-start.1) | copy-done | bytes 2654232
  22.6 9.5 %shard_map.68.prepared = bf16[16128,1152]{1,0:T(8,128)(2,1)} custom-call(s32[5]{0:T(128)S(1)} %stack.23.place.home, bf16[1152,3456]{1,0:T(8,128)(2,1)S(1)} %copy-done, bf16[1152,1152]{1,0:T(8,128)(2,1)S(1)} %copy-done.1), custom_call_target="tpu_custom_call" | custom-call | flops 1000000000 | bytes 10000000 | tf_op jit(solution)/shard_map/pallas_call | solution.py:223
  32.1 18.6 %all-to-all-done = bf16[64,8,1152]{2,1,0:T(8,128)(2,1)S(1)} async-done(((bf16[64,8,1152]{2,1,0:T(8,128)(2,1)}), bf16[64,8,1152]{2,1,0:T(8,128)(2,1)S(1)}, u32[]{:S(2)}, u32[]{:S(2)}) %all-to-all-start) | async-done | bytes 1179680 | tf_op jit(solution)/shard_map/all_to_all | solution.py:280
  50.7 13.5 %shard_map.69 = (bf16[2304,256]{1,0:T(8,128)(2,1)S(1)}, bf16[2,1152,256]{2,1,0:T(8,128)(2,1)S(1)}, bf16[2,1152,256]{2,1,0:T(8,128)(2,1)S(1)}) custom-call(s32[5]{0:T(128)S(1)} %stack.23.place.home, bf16[512,1152]{1,0:T(8,128)(2,1)S(1)} %bitcast.25, bf16[16128,1152]{1,0:T(8,128)(2,1)} %shard_map.68.prepared), custom_call_target="tpu_custom_call" | custom-call | flops 10000000000 | bytes 10000000 | tf_op jit(solution)/shard_map/pallas_call | solution.py:223
  64.9 2.3 %collective-permute-done.1.dg_oth = bf16[2,1152,256]{2,1,0:T(8,128)(2,1)S(1)} collective-permute-done((bf16[2,1152,256]{2,1,0:T(8,128)(2,1)S(1)}, bf16[2,1152,256]{2,1,0:T(8,128)(2,1)S(1)}, u32[]{:S(2)}, u32[]{:S(2)}) %collective-permute-start.1) | collective-permute-done | bytes 1179680 | tf_op jit(solution)/shard_map/ppermute | solution.py:26
  67.2 1.7 %collective-permute-done.x_oth = bf16[2304,256]{1,0:T(8,128)(2,1)S(1)} collective-permute-done((bf16[2304,256]{1,0:T(8,128)(2,1)S(1)}, bf16[2304,256]{1,0:T(8,128)(2,1)S(1)}, u32[]{:S(2)}, u32[]{:S(2)}) %collective-permute-start) | collective-permute-done | bytes 1179680 | tf_op jit(solution)/shard_map/ppermute | solution.py:26
  68.9 5.6 %shard_map.72 = (bf16[2,144,1152]{2,1,0:T(8,128)(2,1)S(1)}, bf16[2,144,1152]{2,1,0:T(8,128)(2,1)}, bf16[2,144,1152]{2,1,0:T(8,128)(2,1)}, bf16[2,144,1152]{2,1,0...) custom-call(bf16[2304,256]{1,0:T(8,128)(2,1)S(1)} %get-tuple-element, ...), custom_call_target="tpu_custom_call" | custom-call | flops 6000000000 | bytes 10000000 | tf_op jit(solution)/shard_map/pallas_call | solution.py:223
  75.2 1.8 %collective-permute-start.3 = (bf16[2,144,1152]{2,1,0:T(8,128)(2,1)}, bf16[2,144,1152]{2,1,0:T(8,128)(2,1)}, u32[]{:S(2)}, u32[]{:S(2)}) collective-permute-start(bf16[2,144,1152]{2,1,0:T(8,128)(2,1)} %get-tuple-element.19), channel_id=1, source_target_pairs={{0,128},{64,192},{128,0},{192,64},{1,129},{65,193},{129,1},{193,65... | collective-permute-start | bytes 1990664 | tf_op jit(solution)/shard_map/ppermute | solution.py:26
  77.0 2.2 %collective-permute-start.4 = (bf16[2,144,1152]{2,1,0:T(8,128)(2,1)}, bf16[2,144,1152]{2,1,0:T(8,128)(2,1)}, u32[]{:S(2)}, u32[]{:S(2)}) collective-permute-start(bf16[2,144,1152]{2,1,0:T(8,128)(2,1)} %get-tuple-element.20), channel_id=1, source_target_pairs={{0,192},{64,128},{128,64},{192,0},{1,193},{65,129},{129,65},{193,1... | collective-permute-start | bytes 1990664 | tf_op jit(solution)/shard_map/ppermute | solution.py:26
  79.2 7.5 %shard_map.70 = bf16[512,640]{1,0:T(8,128)(2,1)} custom-call(s32[5]{0:T(128)S(1)} %stack.23.place.home, bf16[2,1152,256]{2,1,0:T(8,128)(2,1)S(1)} %get-tuple-element.14.dg_own, bf16[2,1152,256]{2,1,0:T(8,128)(2,1)S(1)} %get-tuple-element.15.dg_other, bf16[16128,1152]{1,0:T(8,128)(2,1)} %shard_map.68.prepared), custom_call_target="tpu_custom_call" | custom-call | flops 3000000000 | bytes 10000000 | tf_op jit(solution)/shard_map/pallas_call | solution.py:223
  86.7 5.3 %all-to-all-start.1 = ((bf16[64,8,640]{2,1,0:T(8,128)(2,1)}), bf16[64,8,640]{2,1,0:T(8,128)(2,1)S(1)}, u32[]{:S(2)}, u32[]{:S(2)}) async-start(bf16[64,8,640]{2,1,0:T(8,128)(2,1)} %bitcast.9), calls=%async_computation.1 | async-start | bytes 1310720 | tf_op jit(solution)/shard_map/all_to_all | solution.py:320
  92.0 3.2 %collective-permute-start.8 = (bf16[288,1152]{1,0:T(8,128)(2,1)}, bf16[288,1152]{1,0:T(8,128)(2,1)S(1)}, u32[]{:S(2)}, u32[]{:S(2)}) collective-permute-start(bf16[288,1152]{1,0:T(8,128)(2,1)} %copy-done.2), channel_id=1, source_target_pairs={{0,4},{2,6},{4,0},{6,2},{1,5},{3,7},{5,1},{7,3},{8,12},{10,14},{12... | collective-permute-start | bytes 1990664 | tf_op jit(solution)/shard_map/ppermute | solution.py:26
  95.2 1.3 collective-permute-start.9
  96.5 16.6 %collective-permute-done.3 = bf16[2,144,1152]{2,1,0:T(8,128)(2,1)} collective-permute-done((bf16[2,144,1152]{2,1,0:T(8,128)(2,1)}, bf16[2,144,1152]{2,1,0:T(8,128)(2,1)}, u32[]{:S(2)}, u32[]{:S(2)}) %collective-permute-start.3) | collective-permute-done | bytes 663584 | tf_op jit(solution)/shard_map/ppermute | solution.py:26
  113.2 2.8 %collective-permute-done.4 = bf16[2,144,1152]{2,1,0:T(8,128)(2,1)} collective-permute-done((bf16[2,144,1152]{2,1,0:T(8,128)(2,1)}, bf16[2,144,1152]{2,1,0:T(8,128)(2,1)}, u32[]{:S(2)}, u32[]{:S(2)}) %collective-permute-start.4) | collective-permute-done | bytes 663584 | tf_op jit(solution)/shard_map/ppermute | solution.py:26
  116.0 1.9 %add_convert_fusion.1 = bf16[2,144,1152]{2,1,0:T(8,128)(2,1)S(1)} fusion(bf16[2,144,1152]{2,1,0:T(8,128)(2,1)} %collective-permute-done.4, bf16[2,144,1152]{2,1,0:T(8,128)(2,1)} %collective-permute-done.3, bf16[2,144,1152]{2,1,0:T(8,128)(2,1)} %collective-permute-done.2, bf16[2,144,1152]{2,1,0:T(8,128)(2,1)S(1)} %get-tuple-element.17), kind=kLoop, calls=%fused_computation.1 | loop fusion | flops 2654208 | bytes 3317760 | tf_op jit(solution)/shard_map/convert_element_type | solution.py:307
  117.9 2.4 %collective-permute-start.5 = (bf16[72,1152]{1,0:T(8,128)(2,1)S(1)}, bf16[72,1152]{1,0:T(8,128)(2,1)S(1)}, u32[]{:S(2)}, u32[]{:S(2)}) collective-permute-start(bf16[72,1152]{1,0:T(8,128)(2,1)S(1)} %get-tuple-element.32), channel_id=1, source_target_pairs={{0,4},{2,6},{4,0},{6,2},{1,5},{3,7},{5,1},{7,3},{8,12},{10,14},{12... | collective-permute-start | bytes 497672 | tf_op jit(solution)/shard_map/ppermute | solution.py:26
  120.8 1.9 %collective-permute-start.6 = (bf16[72,1152]{1,0:T(8,128)(2,1)S(1)}, bf16[72,1152]{1,0:T(8,128)(2,1)S(1)}, u32[]{:S(2)}, u32[]{:S(2)}) collective-permute-start(bf16[72,1152]{1,0:T(8,128)(2,1)S(1)} %get-tuple-element.34), channel_id=1, source_target_pairs={{0,2},{2,0},{4,6},{6,4},{1,3},{3,1},{5,7},{7,5},{8,10},{10,8},{12,... | collective-permute-start | bytes 497672 | tf_op jit(solution)/shard_map/ppermute | solution.py:26
  122.7 10.1 %collective-permute-done.9 = bf16[288,1152]{1,0:T(8,128)(2,1)S(1)} collective-permute-done((bf16[288,1152]{1,0:T(8,128)(2,1)S(1)}, bf16[288,1152]{1,0:T(8,128)(2,1)S(1)}, u32[]{:S(2)}, u32[]{:S(2)}) %collective-permute-start.9) | collective-permute-done | bytes 663584 | tf_op jit(solution)/shard_map/ppermute | solution.py:26
  133.2 2.8 %collective-permute-start.11 = (bf16[72,1152]{1,0:T(8,128)(2,1)S(1)}, bf16[72,1152]{1,0:T(8,128)(2,1)S(1)}, u32[]{:S(2)}, u32[]{:S(2)}) collective-permute-start(bf16[72,1152]{1,0:T(8,128)(2,1)S(1)} %get-tuple-element.29), channel_id=1, source_target_pairs={{0,128},{64,192},{128,0},{192,64},{1,129},{65,193},{129,1},{193,65... | collective-permute-start | bytes 497672 | tf_op jit(solution)/shard_map/ppermute | solution.py:26
  138.2 2.5 %collective-permute-done.11 = bf16[72,1152]{1,0:T(8,128)(2,1)S(1)} collective-permute-done((bf16[72,1152]{1,0:T(8,128)(2,1)S(1)}, bf16[72,1152]{1,0:T(8,128)(2,1)S(1)}, u32[]{:S(2)}, u32[]{:S(2)}) %collective-permute-start.11) | collective-permute-done | bytes 165920 | tf_op jit(solution)/shard_map/ppermute | solution.py:26
  140.7 3.2 %collective-permute-done.13 = bf16[72,1152]{1,0:T(8,128)(2,1)S(1)} collective-permute-done((bf16[72,1152]{1,0:T(8,128)(2,1)S(1)}, bf16[72,1152]{1,0:T(8,128)(2,1)S(1)}, u32[]{:S(2)}, u32[]{:S(2)}) %collective-permute-start.13) | collective-permute-done | bytes 165920 | tf_op jit(solution)/shard_map/ppermute | solution.py:26
  144.4 2.3 %collective-permute-start.15 = (bf16[36,1152]{1,0:T(8,128)(2,1)S(1)}, bf16[36,1152]{1,0:T(8,128)(2,1)S(1)}, u32[]{:S(2)}, u32[]{:S(2)}) collective-permute-start(bf16[36,1152]{1,0:T(8,128)(2,1)S(1)} %pad_maximum_fusion.1), channel_id=1, source_target_pairs={{0,56},{8,48},{16,40},{24,32},{32,24},{40,16},{48,8},{56,0},{1,57}... | collective-permute-start | bytes 248840 | tf_op jit(solution)/shard_map/ppermute | solution.py:26
  146.7 2.4 %collective-permute-start.16 = (bf16[36,1152]{1,0:T(8,128)(2,1)S(1)}, bf16[36,1152]{1,0:T(8,128)(2,1)S(1)}, u32[]{:S(2)}, u32[]{:S(2)}) collective-permute-start(bf16[36,1152]{1,0:T(8,128)(2,1)S(1)} %pad_maximum_fusion.2), channel_id=1, source_target_pairs={{0,8},{8,0},{16,24},{24,16},{32,40},{40,32},{48,56},{56,48},{1,9},... | collective-permute-start | bytes 248840 | tf_op jit(solution)/shard_map/ppermute | solution.py:26
  149.4 2.2 %collective-permute-done.15 = bf16[36,1152]{1,0:T(8,128)(2,1)S(1)} collective-permute-done((bf16[36,1152]{1,0:T(8,128)(2,1)S(1)}, bf16[36,1152]{1,0:T(8,128)(2,1)S(1)}, u32[]{:S(2)}, u32[]{:S(2)}) %collective-permute-start.15) | collective-permute-done | bytes 82976 | tf_op jit(solution)/shard_map/ppermute | solution.py:26
  151.6 2.9 %collective-permute-done.16 = bf16[36,1152]{1,0:T(8,128)(2,1)S(1)} collective-permute-done((bf16[36,1152]{1,0:T(8,128)(2,1)S(1)}, bf16[36,1152]{1,0:T(8,128)(2,1)S(1)}, u32[]{:S(2)}, u32[]{:S(2)}) %collective-permute-start.16) | collective-permute-done | bytes 82976 | tf_op jit(solution)/shard_map/ppermute | solution.py:26
  154.5 1.4 collective-permute-done.14
  156.0 3.6 %collective-permute-start.17 = (bf16[18,1152]{1,0:T(8,128)(2,1)S(1)}, bf16[18,1152]{1,0:T(8,128)(2,1)S(1)}, u32[]{:S(2)}, u32[]{:S(2)}) collective-permute-start(bf16[18,1152]{1,0:T(8,128)(2,1)S(1)} %get-tuple-element.35), channel_id=1, source_target_pairs={{0,16},{8,24},{16,0},{24,8},{32,48},{40,56},{48,32},{56,40},{1,17}... | collective-permute-start | bytes 124424 | tf_op jit(solution)/shard_map/ppermute | solution.py:26
  159.6 1.3 shard_map.71
  (34 shorter events, 7.4 us)
Async XLA Ops:
  3.8 46.9 %all-to-all-start = ((bf16[64,8,1152]{2,1,0:T(8,128)(2,1)}), bf16[64,8,1152]{2,1,0:T(8,128)(2,1)S(1)}, u32[]{:S(2)}, u32[]{:S(2)}) async-start(bf16[64,8,1152]{2,1,0:T(8,128)(2,1)} %bitcast.29), calls=%async_computation | async-start | bytes 2359296 | tf_op jit(solution)/shard_map/all_to_all | solution.py:280
  17.6 3.3 %copy-start = (bf16[1152,3456]{1,0:T(8,128)(2,1)S(1)}, bf16[1152,3456]{1,0:T(8,128)(2,1)}, u32[]{:S(2)}) copy-start(bf16[1152,3456]{1,0:T(8,128)(2,1)} %w_qkv.1) | copy-start | bytes 23887876
  20.9 1.7 %copy-start.1 = (bf16[1152,1152]{1,0:T(8,128)(2,1)S(1)}, bf16[1152,1152]{1,0:T(8,128)(2,1)}, u32[]{:S(2)}) copy-start(bf16[1152,1152]{1,0:T(8,128)(2,1)} %w_out.1) | copy-start | bytes 7962628
  64.3 2.9 %collective-permute-start.1 = (bf16[2,1152,256]{2,1,0:T(8,128)(2,1)S(1)}, bf16[2,1152,256]{2,1,0:T(8,128)(2,1)S(1)}, u32[]{:S(2)}, u32[]{:S(2)}) collective-permute-start(bf16[2,1152,256]{2,1,0:T(8,128)(2,1)S(1)} %get-tuple-element.15.dg_other), channel_id=1, source_target_pairs={{0,1},{1,0},{2,3},{3,2},{4,5},{5,4},{6,7},{7,6},{8,9},{9,8},{10,11... | collective-permute-start | bytes 3538952 | tf_op jit(solution)/shard_map/ppermute | solution.py:26
  64.4 4.5 %collective-permute-start = (bf16[2304,256]{1,0:T(8,128)(2,1)S(1)}, bf16[2304,256]{1,0:T(8,128)(2,1)S(1)}, u32[]{:S(2)}, u32[]{:S(2)}) collective-permute-start(bf16[2304,256]{1,0:T(8,128)(2,1)S(1)} %get-tuple-element.16.x_own), channel_id=1, source_target_pairs={{0,1},{1,0},{2,3},{3,2},{4,5},{5,4},{6,7},{7,6},{8,9},{9,8},{10,11... | collective-permute-start | bytes 3538952 | tf_op jit(solution)/shard_map/ppermute | solution.py:26
  74.5 12.2 %copy-start.2 = (bf16[288,1152]{1,0:T(8,128)(2,1)}, bf16[288,1152]{1,0:T(8,128)(2,1)S(1)}, u32[]{:S(2)}) copy-start(bf16[288,1152]{1,0:T(8,128)(2,1)S(1)} %get-tuple-element.22) | copy-start | bytes 1990660
  74.5 22.0 %collective-permute-start.2 = (bf16[2,144,1152]{2,1,0:T(8,128)(2,1)}, bf16[2,144,1152]{2,1,0:T(8,128)(2,1)}, u32[]{:S(2)}, u32[]{:S(2)}) collective-permute-start(bf16[2,144,1152]{2,1,0:T(8,128)(2,1)} %get-tuple-element.18), channel_id=1, source_target_pairs={{0,64},{64,0},{128,192},{192,128},{1,65},{65,1},{129,193},{193,129... | collective-permute-start | bytes 1990664 | tf_op jit(solution)/shard_map/ppermute | solution.py:26
  75.2 38.0 %collective-permute-start.3 = (bf16[2,144,1152]{2,1,0:T(8,128)(2,1)}, bf16[2,144,1152]{2,1,0:T(8,128)(2,1)}, u32[]{:S(2)}, u32[]{:S(2)}) collective-permute-start(bf16[2,144,1152]{2,1,0:T(8,128)(2,1)} %get-tuple-element.19), channel_id=1, source_target_pairs={{0,128},{64,192},{128,0},{192,64},{1,129},{65,193},{129,1},{193,65... | collective-permute-start | bytes 1990664 | tf_op jit(solution)/shard_map/ppermute | solution.py:26
  77.0 38.9 %collective-permute-start.4 = (bf16[2,144,1152]{2,1,0:T(8,128)(2,1)}, bf16[2,144,1152]{2,1,0:T(8,128)(2,1)}, u32[]{:S(2)}, u32[]{:S(2)}) collective-permute-start(bf16[2,144,1152]{2,1,0:T(8,128)(2,1)} %get-tuple-element.20), channel_id=1, source_target_pairs={{0,192},{64,128},{128,64},{192,0},{1,193},{65,129},{129,65},{193,1... | collective-permute-start | bytes 1990664 | tf_op jit(solution)/shard_map/ppermute | solution.py:26
  86.7 72.9 %all-to-all-start.1 = ((bf16[64,8,640]{2,1,0:T(8,128)(2,1)}), bf16[64,8,640]{2,1,0:T(8,128)(2,1)S(1)}, u32[]{:S(2)}, u32[]{:S(2)}) async-start(bf16[64,8,640]{2,1,0:T(8,128)(2,1)} %bitcast.9), calls=%async_computation.1 | async-start | bytes 1310720 | tf_op jit(solution)/shard_map/all_to_all | solution.py:320
  92.0 28.7 %collective-permute-start.8 = (bf16[288,1152]{1,0:T(8,128)(2,1)}, bf16[288,1152]{1,0:T(8,128)(2,1)S(1)}, u32[]{:S(2)}, u32[]{:S(2)}) collective-permute-start(bf16[288,1152]{1,0:T(8,128)(2,1)} %copy-done.2), channel_id=1, source_target_pairs={{0,4},{2,6},{4,0},{6,2},{1,5},{3,7},{5,1},{7,3},{8,12},{10,14},{12... | collective-permute-start | bytes 1990664 | tf_op jit(solution)/shard_map/ppermute | solution.py:26
  95.2 37.6 %collective-permute-start.9 = (bf16[288,1152]{1,0:T(8,128)(2,1)S(1)}, bf16[288,1152]{1,0:T(8,128)(2,1)S(1)}, u32[]{:S(2)}, u32[]{:S(2)}) collective-permute-start(bf16[288,1152]{1,0:T(8,128)(2,1)S(1)} %get-tuple-element.23), channel_id=1, source_target_pairs={{0,2},{2,0},{4,6},{6,4},{1,3},{3,1},{5,7},{7,5},{8,10},{10,8},{12,... | collective-permute-start | bytes 1990664 | tf_op jit(solution)/shard_map/ppermute | solution.py:26
  96.5 36.3 %collective-permute-start.10 = (bf16[288,1152]{1,0:T(8,128)(2,1)S(1)}, bf16[288,1152]{1,0:T(8,128)(2,1)S(1)}, u32[]{:S(2)}, u32[]{:S(2)}) collective-permute-start(bf16[288,1152]{1,0:T(8,128)(2,1)S(1)} %get-tuple-element.24), channel_id=1, source_target_pairs={{0,6},{2,4},{4,2},{6,0},{1,7},{3,5},{5,3},{7,1},{8,14},{10,12},{12... | collective-permute-start | bytes 1990664 | tf_op jit(solution)/shard_map/ppermute | solution.py:26
  117.9 19.2 %collective-permute-start.5 = (bf16[72,1152]{1,0:T(8,128)(2,1)S(1)}, bf16[72,1152]{1,0:T(8,128)(2,1)S(1)}, u32[]{:S(2)}, u32[]{:S(2)}) collective-permute-start(bf16[72,1152]{1,0:T(8,128)(2,1)S(1)} %get-tuple-element.32), channel_id=1, source_target_pairs={{0,4},{2,6},{4,0},{6,2},{1,5},{3,7},{5,1},{7,3},{8,12},{10,14},{12... | collective-permute-start | bytes 497672 | tf_op jit(solution)/shard_map/ppermute | solution.py:26
  120.3 17.6 %collective-permute-start.7 = (bf16[72,1152]{1,0:T(8,128)(2,1)S(1)}, bf16[72,1152]{1,0:T(8,128)(2,1)S(1)}, u32[]{:S(2)}, u32[]{:S(2)}) collective-permute-start(bf16[72,1152]{1,0:T(8,128)(2,1)S(1)} %get-tuple-element.33), channel_id=1, source_target_pairs={{0,6},{2,4},{4,2},{6,0},{1,7},{3,5},{5,3},{7,1},{8,14},{10,12},{12... | collective-permute-start | bytes 497672 | tf_op jit(solution)/shard_map/ppermute | solution.py:26
  120.8 17.3 %collective-permute-start.6 = (bf16[72,1152]{1,0:T(8,128)(2,1)S(1)}, bf16[72,1152]{1,0:T(8,128)(2,1)S(1)}, u32[]{:S(2)}, u32[]{:S(2)}) collective-permute-start(bf16[72,1152]{1,0:T(8,128)(2,1)S(1)} %get-tuple-element.34), channel_id=1, source_target_pairs={{0,2},{2,0},{4,6},{6,4},{1,3},{3,1},{5,7},{7,5},{8,10},{10,8},{12,... | collective-permute-start | bytes 497672 | tf_op jit(solution)/shard_map/ppermute | solution.py:26
  133.2 7.5 %collective-permute-start.11 = (bf16[72,1152]{1,0:T(8,128)(2,1)S(1)}, bf16[72,1152]{1,0:T(8,128)(2,1)S(1)}, u32[]{:S(2)}, u32[]{:S(2)}) collective-permute-start(bf16[72,1152]{1,0:T(8,128)(2,1)S(1)} %get-tuple-element.29), channel_id=1, source_target_pairs={{0,128},{64,192},{128,0},{192,64},{1,129},{65,193},{129,1},{193,65... | collective-permute-start | bytes 497672 | tf_op jit(solution)/shard_map/ppermute | solution.py:26
  136.0 7.9 %collective-permute-start.13 = (bf16[72,1152]{1,0:T(8,128)(2,1)S(1)}, bf16[72,1152]{1,0:T(8,128)(2,1)S(1)}, u32[]{:S(2)}, u32[]{:S(2)}) collective-permute-start(bf16[72,1152]{1,0:T(8,128)(2,1)S(1)} %get-tuple-element.30), channel_id=1, source_target_pairs={{0,192},{64,128},{128,64},{192,0},{1,193},{65,129},{129,65},{193,1... | collective-permute-start | bytes 497672 | tf_op jit(solution)/shard_map/ppermute | solution.py:26
  137.1 7.0 %collective-permute-start.12 = (bf16[72,1152]{1,0:T(8,128)(2,1)S(1)}, bf16[72,1152]{1,0:T(8,128)(2,1)S(1)}, u32[]{:S(2)}, u32[]{:S(2)}) collective-permute-start(bf16[72,1152]{1,0:T(8,128)(2,1)S(1)} %get-tuple-element.31), channel_id=1, source_target_pairs={{0,64},{64,0},{128,192},{192,128},{1,65},{65,1},{129,193},{193,129... | collective-permute-start | bytes 497672 | tf_op jit(solution)/shard_map/ppermute | solution.py:26
  144.4 7.3 %collective-permute-start.15 = (bf16[36,1152]{1,0:T(8,128)(2,1)S(1)}, bf16[36,1152]{1,0:T(8,128)(2,1)S(1)}, u32[]{:S(2)}, u32[]{:S(2)}) collective-permute-start(bf16[36,1152]{1,0:T(8,128)(2,1)S(1)} %pad_maximum_fusion.1), channel_id=1, source_target_pairs={{0,56},{8,48},{16,40},{24,32},{32,24},{40,16},{48,8},{56,0},{1,57}... | collective-permute-start | bytes 248840 | tf_op jit(solution)/shard_map/ppermute | solution.py:26
  146.7 7.8 %collective-permute-start.16 = (bf16[36,1152]{1,0:T(8,128)(2,1)S(1)}, bf16[36,1152]{1,0:T(8,128)(2,1)S(1)}, u32[]{:S(2)}, u32[]{:S(2)}) collective-permute-start(bf16[36,1152]{1,0:T(8,128)(2,1)S(1)} %pad_maximum_fusion.2), channel_id=1, source_target_pairs={{0,8},{8,0},{16,24},{24,16},{32,40},{40,32},{48,56},{56,48},{1,9},... | collective-permute-start | bytes 248840 | tf_op jit(solution)/shard_map/ppermute | solution.py:26
  149.2 6.7 %collective-permute-start.14 = (bf16[36,1152]{1,0:T(8,128)(2,1)S(1)}, bf16[36,1152]{1,0:T(8,128)(2,1)S(1)}, u32[]{:S(2)}, u32[]{:S(2)}) collective-permute-start(bf16[36,1152]{1,0:T(8,128)(2,1)S(1)} %pad_maximum_fusion), channel_id=1, source_target_pairs={{0,48},{8,56},{16,32},{24,40},{32,16},{40,24},{48,0},{56,8},{1,49}... | collective-permute-start | bytes 248840 | tf_op jit(solution)/shard_map/ppermute | solution.py:26
  156.0 5.7 %collective-permute-start.17 = (bf16[18,1152]{1,0:T(8,128)(2,1)S(1)}, bf16[18,1152]{1,0:T(8,128)(2,1)S(1)}, u32[]{:S(2)}, u32[]{:S(2)}) collective-permute-start(bf16[18,1152]{1,0:T(8,128)(2,1)S(1)} %get-tuple-element.35), channel_id=1, source_target_pairs={{0,16},{8,24},{16,0},{24,8},{32,48},{40,56},{48,32},{56,40},{1,17}... | collective-permute-start | bytes 124424 | tf_op jit(solution)/shard_map/ppermute | solution.py:26

commit v3 on v2

--- a/solution.py
+++ b/solution.py
@@ -294,6 +294,7 @@
         got_a.append(flip(part_a[s], "x", s))
         got_b.append(flip(part_b[(2, 1, 3)[i]], Y, (2, 1, 3)[i]))
 
+    dg_own, dg_other, _ = lax.optimization_barrier((dg_own, dg_other, got_a[0]))
     grad_in = call(
         grad_in_kernel,
         shape(512, 640),

time: 164 us -> 150 us (0.915)
  waiting for transfers between devices: 66.1 us -> 52.8 us
  starting transfers between devices: 46.4 us -> 44.5 us
    ppermute x18, waiting for transfers between devices: 47.5 us -> 34.2 us  [flip(): return lax.ppermute(array, axes, [(i, i ^ step) for i in range(size)])]
    ppermute x18, starting transfers between devices: 27.4 us -> 22.6 us  [flip(): return lax.ppermute(array, axes, [(i, i ^ step) for i in range(size)])]
    all_to_all x1, starting transfers between devices: 5.3 us -> 8.2 us  [per_device(): lax.all_to_all(grad_in, FRAME, split_axis=0, concat_axis=0, tiled=True)]
  transfers between devices with their start and end apart: 20 -> 20, of which waited for: 15 -> 13; matrix products, arithmetic and copies ran while one was open for 2% -> 4% of each run, Pallas kernels for 11% -> 11%
where the time goes in v3:
time: 150 us; the launch traced here: 149 us
  waiting for transfers between devices  52.8 us (35%)
  starting transfers between devices  44.5 us (30%)
  Pallas kernels  40.7 us (27%)
  other arithmetic  5.34 us (4%)
  local copies, waits for them, and re-layouts  5.26 us (4%)
    pallas_call x6, Pallas kernels, call(): pl.pallas_call(kernel, out_shape=outs, in_specs=specs or [VMEM] * len(ins...  40.7 us
    ppermute x18, waiting for transfers between devices, flip(): return lax.ppermute(array, axes, [(i, i ^ step) for i in range(size)])  34.2 us
    ppermute x18, starting transfers between devices, flip(): return lax.ppermute(array, axes, [(i, i ^ step) for i in range(size)])  22.6 us
    all_to_all x1, waiting for transfers between devices, per_device(): both = lax.all_to_all(both, FRAME, split_axis=0, concat_axis=0, tiled=True)  18.6 us
    all_to_all x1, starting transfers between devices, per_device(): both = lax.all_to_all(both, FRAME, split_axis=0, concat_axis=0, tiled=True)  13.7 us
    all_to_all x1, starting transfers between devices, per_device(): lax.all_to_all(grad_in, FRAME, split_axis=0, concat_axis=0, tiled=True)  8.2 us
    unnamed x6, local copies, waits for them, and re-layouts  5.01 us
  transfers between devices with their start and end apart: 20, of which 13 were waited for; matrix products, arithmetic and copies ran while one was open for 4% of the time, Pallas kernels for 11%

profile of v3, /device:TPU:8, one launch (start us, length us, event | category | flops | bytes accessed | tf_op | source)
XLA Modules:
  0.0 149.4 jit_solution(9099556789463219779)
XLA Ops:
  0.6 3.2 %shard_map.67 = bf16[512,1152]{1,0:T(8,128)(2,1)} custom-call(bf16[256,1152]{1,0:T(8,128)(2,1)} %bitcast.30, bf16[256,1152]{1,0:T(8,128)(2,1)} %bitcast.31), custom_call_target="tpu_custom_call" | custom-call | flops 1000000000 | bytes 10000000 | tf_op jit(solution)/shard_map/pallas_call | solution.py:223
  3.8 13.7 %all-to-all-start = ((bf16[64,8,1152]{2,1,0:T(8,128)(2,1)}), bf16[64,8,1152]{2,1,0:T(8,128)(2,1)S(1)}, u32[]{:S(2)}, u32[]{:S(2)}) async-start(bf16[64,8,1152]{2,1,0:T(8,128)(2,1)} %bitcast.29), calls=%async_computation | async-start | bytes 2359296 | tf_op jit(solution)/shard_map/all_to_all | solution.py:280
  17.6 3.3 %copy-done = bf16[1152,3456]{1,0:T(8,128)(2,1)S(1)} copy-done((bf16[1152,3456]{1,0:T(8,128)(2,1)S(1)}, bf16[1152,3456]{1,0:T(8,128)(2,1)}, u32[]{:S(2)}) %copy-start) | copy-done | bytes 7962648
  20.9 1.7 %copy-done.1 = bf16[1152,1152]{1,0:T(8,128)(2,1)S(1)} copy-done((bf16[1152,1152]{1,0:T(8,128)(2,1)S(1)}, bf16[1152,1152]{1,0:T(8,128)(2,1)}, u32[]{:S(2)}) %copy-start.1) | copy-done | bytes 2654232
  22.6 9.5 %shard_map.68.prepared = bf16[16128,1152]{1,0:T(8,128)(2,1)} custom-call(s32[5]{0:T(128)S(1)} %stack.23.place.home, bf16[1152,3456]{1,0:T(8,128)(2,1)S(1)} %copy-done, bf16[1152,1152]{1,0:T(8,128)(2,1)S(1)} %copy-done.1), custom_call_target="tpu_custom_call" | custom-call | flops 1000000000 | bytes 10000000 | tf_op jit(solution)/shard_map/pallas_call | solution.py:223
  32.1 18.6 %all-to-all-done = bf16[64,8,1152]{2,1,0:T(8,128)(2,1)S(1)} async-done(((bf16[64,8,1152]{2,1,0:T(8,128)(2,1)}), bf16[64,8,1152]{2,1,0:T(8,128)(2,1)S(1)}, u32[]{:S(2)}, u32[]{:S(2)}) %all-to-all-start) | async-done | bytes 1179680 | tf_op jit(solution)/shard_map/all_to_all | solution.py:280
  50.7 13.5 %shard_map.69 = (bf16[2304,256]{1,0:T(8,128)(2,1)S(1)}, bf16[2,1152,256]{2,1,0:T(8,128)(2,1)S(1)}, bf16[2,1152,256]{2,1,0:T(8,128)(2,1)S(1)}) custom-call(s32[5]{0:T(128)S(1)} %stack.23.place.home, bf16[512,1152]{1,0:T(8,128)(2,1)S(1)} %bitcast.25, bf16[16128,1152]{1,0:T(8,128)(2,1)} %shard_map.68.prepared), custom_call_target="tpu_custom_call" | custom-call | flops 10000000000 | bytes 10000000 | tf_op jit(solution)/shard_map/pallas_call | solution.py:223
  64.9 2.3 %collective-permute-done.1.dg_oth = bf16[2,1152,256]{2,1,0:T(8,128)(2,1)S(1)} collective-permute-done((bf16[2,1152,256]{2,1,0:T(8,128)(2,1)S(1)}, bf16[2,1152,256]{2,1,0:T(8,128)(2,1)S(1)}, u32[]{:S(2)}, u32[]{:S(2)}) %collective-permute-start.1) | collective-permute-done | bytes 1179680 | tf_op jit(solution)/shard_map/ppermute | solution.py:26
  67.2 1.7 %collective-permute-done.x_oth = bf16[2304,256]{1,0:T(8,128)(2,1)S(1)} collective-permute-done((bf16[2304,256]{1,0:T(8,128)(2,1)S(1)}, bf16[2304,256]{1,0:T(8,128)(2,1)S(1)}, u32[]{:S(2)}, u32[]{:S(2)}) %collective-permute-start) | collective-permute-done | bytes 1179680 | tf_op jit(solution)/shard_map/ppermute | solution.py:26
  68.9 5.6 %shard_map.70 = (bf16[2,144,1152]{2,1,0:T(8,128)(2,1)S(1)}, bf16[2,144,1152]{2,1,0:T(8,128)(2,1)S(1)}, bf16[2,144,1152]{2,1,0:T(8,128)(2,1)}, bf16[2,144,1152]{2...) custom-call(bf16[2304,256]{1,0:T(8,128)(2,1)S(1)} %get-tuple-element, ...), custom_call_target="tpu_custom_call" | custom-call | flops 6000000000 | bytes 10000000 | tf_op jit(solution)/shard_map/pallas_call | solution.py:223
  75.2 1.8 %collective-permute-start.3 = (bf16[2,144,1152]{2,1,0:T(8,128)(2,1)}, bf16[2,144,1152]{2,1,0:T(8,128)(2,1)}, u32[]{:S(2)}, u32[]{:S(2)}) collective-permute-start(bf16[2,144,1152]{2,1,0:T(8,128)(2,1)} %get-tuple-element.23), channel_id=1, source_target_pairs={{0,128},{64,192},{128,0},{192,64},{1,129},{65,193},{129,1},{193,65... | collective-permute-start | bytes 1990664 | tf_op jit(solution)/shard_map/ppermute | solution.py:26
  77.0 2.2 %collective-permute-start.4 = (bf16[2,144,1152]{2,1,0:T(8,128)(2,1)}, bf16[2,144,1152]{2,1,0:T(8,128)(2,1)}, u32[]{:S(2)}, u32[]{:S(2)}) collective-permute-start(bf16[2,144,1152]{2,1,0:T(8,128)(2,1)} %get-tuple-element.24), channel_id=1, source_target_pairs={{0,192},{64,128},{128,64},{192,0},{1,193},{65,129},{129,65},{193,1... | collective-permute-start | bytes 1990664 | tf_op jit(solution)/shard_map/ppermute | solution.py:26
  79.5 1.3 collective-permute-start.9
  80.8 11.5 %collective-permute-done.2 = bf16[2,144,1152]{2,1,0:T(8,128)(2,1)S(1)} collective-permute-done((bf16[2,144,1152]{2,1,0:T(8,128)(2,1)S(1)}, bf16[2,144,1152]{2,1,0:T(8,128)(2,1)S(1)}, u32[]{:S(2)}, u32[]{:S(2)}) %collective-permute-start.2) | collective-permute-done | bytes 663584 | tf_op jit(solution)/shard_map/ppermute | solution.py:26
  92.3 7.5 %shard_map.71 = bf16[512,640]{1,0:T(8,128)(2,1)} custom-call(s32[5]{0:T(128)S(1)} %stack.23.place.home, bf16[2,1152,256]{2,1,0:T(8,128)(2,1)S(1)} %get-tuple-element.20.dg_own, bf16[2,1152,256]{2,1,0:T(8,128)(2,1)S(1)} %get-tuple-element.21.dg_other, bf16[16128,1152]{1,0:T(8,128)(2,1)} %shard_map.68.prepared), custom_call_target="tpu_custom_call" | custom-call | flops 3000000000 | bytes 10000000 | tf_op jit(solution)/shard_map/pallas_call | solution.py:223
  99.8 8.2 %all-to-all-start.1 = ((bf16[64,8,640]{2,1,0:T(8,128)(2,1)}), bf16[64,8,640]{2,1,0:T(8,128)(2,1)S(1)}, u32[]{:S(2)}, u32[]{:S(2)}) async-start(bf16[64,8,640]{2,1,0:T(8,128)(2,1)} %bitcast.9), calls=%async_computation.1 | async-start | bytes 1310720 | tf_op jit(solution)/shard_map/all_to_all | solution.py:321
  108.0 1.1 collective-permute-done.4
  109.2 1.8 %add_convert_fusion.1 = bf16[2,144,1152]{2,1,0:T(8,128)(2,1)S(1)} fusion(bf16[2,144,1152]{2,1,0:T(8,128)(2,1)} %collective-permute-done.4, bf16[2,144,1152]{2,1,0:T(8,128)(2,1)} %collective-permute-done.3, bf16[2,144,1152]{2,1,0:T(8,128)(2,1)} %copy-done.2, bf16[2,144,1152]{2,1,0:T(8,128)(2,1)S(1)} %get-tuple-element.22), kind=kLoop, calls=%fused_computation.1 | loop fusion | flops 2654208 | bytes 3317760 | tf_op jit(solution)/shard_map/convert_element_type | solution.py:308
  111.1 2.4 %collective-permute-start.5 = (bf16[72,1152]{1,0:T(8,128)(2,1)S(1)}, bf16[72,1152]{1,0:T(8,128)(2,1)S(1)}, u32[]{:S(2)}, u32[]{:S(2)}) collective-permute-start(bf16[72,1152]{1,0:T(8,128)(2,1)S(1)} %get-tuple-element.36), channel_id=1, source_target_pairs={{0,4},{2,6},{4,0},{6,2},{1,5},{3,7},{5,1},{7,3},{8,12},{10,14},{12... | collective-permute-start | bytes 497672 | tf_op jit(solution)/shard_map/ppermute | solution.py:26
  114.0 1.9 %collective-permute-start.6 = (bf16[72,1152]{1,0:T(8,128)(2,1)S(1)}, bf16[72,1152]{1,0:T(8,128)(2,1)S(1)}, u32[]{:S(2)}, u32[]{:S(2)}) collective-permute-start(bf16[72,1152]{1,0:T(8,128)(2,1)S(1)} %get-tuple-element.38), channel_id=1, source_target_pairs={{0,2},{2,0},{4,6},{6,4},{1,3},{3,1},{5,7},{7,5},{8,10},{10,8},{12,... | collective-permute-start | bytes 497672 | tf_op jit(solution)/shard_map/ppermute | solution.py:26
  115.9 1.8 %add_convert_fusion = bf16[288,1152]{1,0:T(8,128)(2,1)S(1)} fusion(bf16[288,1152]{1,0:T(8,128)(2,1)} %collective-permute-done.10, bf16[288,1152]{1,0:T(8,128)(2,1)} %collective-permute-done.9, bf16[288,1152]{1,0:T(8,128)(2,1)} %collective-permute-done.8, bf16[288,1152]{1,0:T(8,128)(2,1)S(1)} %get-tuple-element.25), kind=kLoop, calls=%fused_computation | loop fusion | flops 2654208 | bytes 3317760 | tf_op jit(solution)/shard_map/convert_element_type | solution.py:309
  117.7 2.1 %collective-permute-start.11 = (bf16[72,1152]{1,0:T(8,128)(2,1)S(1)}, bf16[72,1152]{1,0:T(8,128)(2,1)S(1)}, u32[]{:S(2)}, u32[]{:S(2)}) collective-permute-start(bf16[72,1152]{1,0:T(8,128)(2,1)S(1)} %get-tuple-element.33), channel_id=1, source_target_pairs={{0,128},{64,192},{128,0},{192,64},{1,129},{65,193},{129,1},{193,65... | collective-permute-start | bytes 497672 | tf_op jit(solution)/shard_map/ppermute | solution.py:26
  121.0 1.9 %collective-permute-done.5 = bf16[72,1152]{1,0:T(8,128)(2,1)S(1)} collective-permute-done((bf16[72,1152]{1,0:T(8,128)(2,1)S(1)}, bf16[72,1152]{1,0:T(8,128)(2,1)S(1)}, u32[]{:S(2)}, u32[]{:S(2)}) %collective-permute-start.5) | collective-permute-done | bytes 165920 | tf_op jit(solution)/shard_map/ppermute | solution.py:26
  123.2 3.2 %collective-permute-done.7 = bf16[72,1152]{1,0:T(8,128)(2,1)S(1)} collective-permute-done((bf16[72,1152]{1,0:T(8,128)(2,1)S(1)}, bf16[72,1152]{1,0:T(8,128)(2,1)S(1)}, u32[]{:S(2)}, u32[]{:S(2)}) %collective-permute-start.7) | collective-permute-done | bytes 165920 | tf_op jit(solution)/shard_map/ppermute | solution.py:26
  127.4 2.2 %collective-permute-done.13 = bf16[72,1152]{1,0:T(8,128)(2,1)S(1)} collective-permute-done((bf16[72,1152]{1,0:T(8,128)(2,1)S(1)}, bf16[72,1152]{1,0:T(8,128)(2,1)S(1)}, u32[]{:S(2)}, u32[]{:S(2)}) %collective-permute-start.13) | collective-permute-done | bytes 165920 | tf_op jit(solution)/shard_map/ppermute | solution.py:26
  130.9 3.2 %collective-permute-start.16 = (bf16[36,1152]{1,0:T(8,128)(2,1)S(1)}, bf16[36,1152]{1,0:T(8,128)(2,1)S(1)}, u32[]{:S(2)}, u32[]{:S(2)}) collective-permute-start(bf16[36,1152]{1,0:T(8,128)(2,1)S(1)} %pad_maximum_fusion.2), channel_id=1, source_target_pairs={{0,8},{8,0},{16,24},{24,16},{32,40},{40,32},{48,56},{56,48},{1,9},... | collective-permute-start | bytes 248840 | tf_op jit(solution)/shard_map/ppermute | solution.py:26
  135.0 2.5 %collective-permute-done.15 = bf16[36,1152]{1,0:T(8,128)(2,1)S(1)} collective-permute-done((bf16[36,1152]{1,0:T(8,128)(2,1)S(1)}, bf16[36,1152]{1,0:T(8,128)(2,1)S(1)}, u32[]{:S(2)}, u32[]{:S(2)}) %collective-permute-start.15) | collective-permute-done | bytes 82976 | tf_op jit(solution)/shard_map/ppermute | solution.py:26
  137.5 1.6 %collective-permute-done.16 = bf16[36,1152]{1,0:T(8,128)(2,1)S(1)} collective-permute-done((bf16[36,1152]{1,0:T(8,128)(2,1)S(1)}, bf16[36,1152]{1,0:T(8,128)(2,1)S(1)}, u32[]{:S(2)}, u32[]{:S(2)}) %collective-permute-start.16) | collective-permute-done | bytes 82976 | tf_op jit(solution)/shard_map/ppermute | solution.py:26
  139.1 1.9 %collective-permute-done.14 = bf16[36,1152]{1,0:T(8,128)(2,1)S(1)} collective-permute-done((bf16[36,1152]{1,0:T(8,128)(2,1)S(1)}, bf16[36,1152]{1,0:T(8,128)(2,1)S(1)}, u32[]{:S(2)}, u32[]{:S(2)}) %collective-permute-start.14) | collective-permute-done | bytes 82976 | tf_op jit(solution)/shard_map/ppermute | solution.py:26
  141.0 2.3 %collective-permute-start.17 = (bf16[18,1152]{1,0:T(8,128)(2,1)S(1)}, bf16[18,1152]{1,0:T(8,128)(2,1)S(1)}, u32[]{:S(2)}, u32[]{:S(2)}) collective-permute-start(bf16[18,1152]{1,0:T(8,128)(2,1)S(1)} %get-tuple-element.39), channel_id=1, source_target_pairs={{0,16},{8,24},{16,0},{24,8},{32,48},{40,56},{48,32},{56,40},{1,17}... | collective-permute-start | bytes 124424 | tf_op jit(solution)/shard_map/ppermute | solution.py:26
  143.3 3.4 %collective-permute-done.17 = bf16[18,1152]{1,0:T(8,128)(2,1)S(1)} collective-permute-done((bf16[18,1152]{1,0:T(8,128)(2,1)S(1)}, bf16[18,1152]{1,0:T(8,128)(2,1)S(1)}, u32[]{:S(2)}, u32[]{:S(2)}) %collective-permute-start.17) | collective-permute-done | bytes 41504 | tf_op jit(solution)/shard_map/ppermute | solution.py:26
  148.1 1.3 shard_map.72
  (34 shorter events, 8.1 us)
Async XLA Ops:
  3.8 46.9 %all-to-all-start = ((bf16[64,8,1152]{2,1,0:T(8,128)(2,1)}), bf16[64,8,1152]{2,1,0:T(8,128)(2,1)S(1)}, u32[]{:S(2)}, u32[]{:S(2)}) async-start(bf16[64,8,1152]{2,1,0:T(8,128)(2,1)} %bitcast.29), calls=%async_computation | async-start | bytes 2359296 | tf_op jit(solution)/shard_map/all_to_all | solution.py:280
  17.6 3.3 %copy-start = (bf16[1152,3456]{1,0:T(8,128)(2,1)S(1)}, bf16[1152,3456]{1,0:T(8,128)(2,1)}, u32[]{:S(2)}) copy-start(bf16[1152,3456]{1,0:T(8,128)(2,1)} %w_qkv.1) | copy-start | bytes 23887876
  20.9 1.7 %copy-start.1 = (bf16[1152,1152]{1,0:T(8,128)(2,1)S(1)}, bf16[1152,1152]{1,0:T(8,128)(2,1)}, u32[]{:S(2)}) copy-start(bf16[1152,1152]{1,0:T(8,128)(2,1)} %w_out.1) | copy-start | bytes 7962628
  64.3 2.9 %collective-permute-start.1 = (bf16[2,1152,256]{2,1,0:T(8,128)(2,1)S(1)}, bf16[2,1152,256]{2,1,0:T(8,128)(2,1)S(1)}, u32[]{:S(2)}, u32[]{:S(2)}) collective-permute-start(bf16[2,1152,256]{2,1,0:T(8,128)(2,1)S(1)} %get-tuple-element.21.dg_other), channel_id=1, source_target_pairs={{0,1},{1,0},{2,3},{3,2},{4,5},{5,4},{6,7},{7,6},{8,9},{9,8},{10,11... | collective-permute-start | bytes 3538952 | tf_op jit(solution)/shard_map/ppermute | solution.py:26
  64.4 4.5 %collective-permute-start = (bf16[2304,256]{1,0:T(8,128)(2,1)S(1)}, bf16[2304,256]{1,0:T(8,128)(2,1)S(1)}, u32[]{:S(2)}, u32[]{:S(2)}) collective-permute-start(bf16[2304,256]{1,0:T(8,128)(2,1)S(1)} %get-tuple-element.18.x_own), channel_id=1, source_target_pairs={{0,1},{1,0},{2,3},{3,2},{4,5},{5,4},{6,7},{7,6},{8,9},{9,8},{10,11... | collective-permute-start | bytes 3538952 | tf_op jit(solution)/shard_map/ppermute | solution.py:26
  74.5 17.8 %collective-permute-start.2 = (bf16[2,144,1152]{2,1,0:T(8,128)(2,1)S(1)}, bf16[2,144,1152]{2,1,0:T(8,128)(2,1)S(1)}, u32[]{:S(2)}, u32[]{:S(2)}) collective-permute-start(bf16[2,144,1152]{2,1,0:T(8,128)(2,1)S(1)} %get-tuple-element.19), channel_id=1, source_target_pairs={{0,64},{64,0},{128,192},{192,128},{1,65},{65,1},{129,193},{193,129... | collective-permute-start | bytes 1990664 | tf_op jit(solution)/shard_map/ppermute | solution.py:26
  75.2 32.8 %collective-permute-start.3 = (bf16[2,144,1152]{2,1,0:T(8,128)(2,1)}, bf16[2,144,1152]{2,1,0:T(8,128)(2,1)}, u32[]{:S(2)}, u32[]{:S(2)}) collective-permute-start(bf16[2,144,1152]{2,1,0:T(8,128)(2,1)} %get-tuple-element.23), channel_id=1, source_target_pairs={{0,128},{64,192},{128,0},{192,64},{1,129},{65,193},{129,1},{193,65... | collective-permute-start | bytes 1990664 | tf_op jit(solution)/shard_map/ppermute | solution.py:26
  77.0 32.1 %collective-permute-start.4 = (bf16[2,144,1152]{2,1,0:T(8,128)(2,1)}, bf16[2,144,1152]{2,1,0:T(8,128)(2,1)}, u32[]{:S(2)}, u32[]{:S(2)}) collective-permute-start(bf16[2,144,1152]{2,1,0:T(8,128)(2,1)} %get-tuple-element.24), channel_id=1, source_target_pairs={{0,192},{64,128},{128,64},{192,0},{1,193},{65,129},{129,65},{193,1... | collective-permute-start | bytes 1990664 | tf_op jit(solution)/shard_map/ppermute | solution.py:26
  79.2 34.8 %collective-permute-start.8 = (bf16[288,1152]{1,0:T(8,128)(2,1)}, bf16[288,1152]{1,0:T(8,128)(2,1)}, u32[]{:S(2)}, u32[]{:S(2)}) collective-permute-start(bf16[288,1152]{1,0:T(8,128)(2,1)} %get-tuple-element.26), channel_id=1, source_target_pairs={{0,4},{2,6},{4,0},{6,2},{1,5},{3,7},{5,1},{7,3},{8,12},{10,14},{12... | collective-permute-start | bytes 1990664 | tf_op jit(solution)/shard_map/ppermute | solution.py:26
  79.5 36.4 %collective-permute-start.9 = (bf16[288,1152]{1,0:T(8,128)(2,1)S(1)}, bf16[288,1152]{1,0:T(8,128)(2,1)}, u32[]{:S(2)}, u32[]{:S(2)}) collective-permute-start(bf16[288,1152]{1,0:T(8,128)(2,1)S(1)} %get-tuple-element.27), channel_id=1, source_target_pairs={{0,2},{2,0},{4,6},{6,4},{1,3},{3,1},{5,7},{7,5},{8,10},{10,8},{12,... | collective-permute-start | bytes 1990664 | tf_op jit(solution)/shard_map/ppermute | solution.py:26
  92.3 7.5 %copy-start.2 = (bf16[2,144,1152]{2,1,0:T(8,128)(2,1)}, bf16[2,144,1152]{2,1,0:T(8,128)(2,1)S(1)}, u32[]{:S(2)}) copy-start(bf16[2,144,1152]{2,1,0:T(8,128)(2,1)S(1)} %collective-permute-done.2) | copy-start | bytes 1990660
  92.3 23.6 %collective-permute-start.10 = (bf16[288,1152]{1,0:T(8,128)(2,1)S(1)}, bf16[288,1152]{1,0:T(8,128)(2,1)}, u32[]{:S(2)}, u32[]{:S(2)}) collective-permute-start(bf16[288,1152]{1,0:T(8,128)(2,1)S(1)} %get-tuple-element.28), channel_id=1, source_target_pairs={{0,6},{2,4},{4,2},{6,0},{1,7},{3,5},{5,3},{7,1},{8,14},{10,12},{12... | collective-permute-start | bytes 1990664 | tf_op jit(solution)/shard_map/ppermute | solution.py:26
  99.8 48.2 %all-to-all-start.1 = ((bf16[64,8,640]{2,1,0:T(8,128)(2,1)}), bf16[64,8,640]{2,1,0:T(8,128)(2,1)S(1)}, u32[]{:S(2)}, u32[]{:S(2)}) async-start(bf16[64,8,640]{2,1,0:T(8,128)(2,1)} %bitcast.9), calls=%async_computation.1 | async-start | bytes 1310720 | tf_op jit(solution)/shard_map/all_to_all | solution.py:321
  111.1 11.8 %collective-permute-start.5 = (bf16[72,1152]{1,0:T(8,128)(2,1)S(1)}, bf16[72,1152]{1,0:T(8,128)(2,1)S(1)}, u32[]{:S(2)}, u32[]{:S(2)}) collective-permute-start(bf16[72,1152]{1,0:T(8,128)(2,1)S(1)} %get-tuple-element.36), channel_id=1, source_target_pairs={{0,4},{2,6},{4,0},{6,2},{1,5},{3,7},{5,1},{7,3},{8,12},{10,14},{12... | collective-permute-start | bytes 497672 | tf_op jit(solution)/shard_map/ppermute | solution.py:26
  113.5 12.9 %collective-permute-start.7 = (bf16[72,1152]{1,0:T(8,128)(2,1)S(1)}, bf16[72,1152]{1,0:T(8,128)(2,1)S(1)}, u32[]{:S(2)}, u32[]{:S(2)}) collective-permute-start(bf16[72,1152]{1,0:T(8,128)(2,1)S(1)} %get-tuple-element.37), channel_id=1, source_target_pairs={{0,6},{2,4},{4,2},{6,0},{1,7},{3,5},{5,3},{7,1},{8,14},{10,12},{12... | collective-permute-start | bytes 497672 | tf_op jit(solution)/shard_map/ppermute | solution.py:26
  114.0 12.4 %collective-permute-start.6 = (bf16[72,1152]{1,0:T(8,128)(2,1)S(1)}, bf16[72,1152]{1,0:T(8,128)(2,1)S(1)}, u32[]{:S(2)}, u32[]{:S(2)}) collective-permute-start(bf16[72,1152]{1,0:T(8,128)(2,1)S(1)} %get-tuple-element.38), channel_id=1, source_target_pairs={{0,2},{2,0},{4,6},{6,4},{1,3},{3,1},{5,7},{7,5},{8,10},{10,8},{12,... | collective-permute-start | bytes 497672 | tf_op jit(solution)/shard_map/ppermute | solution.py:26
  117.7 9.7 %collective-permute-start.11 = (bf16[72,1152]{1,0:T(8,128)(2,1)S(1)}, bf16[72,1152]{1,0:T(8,128)(2,1)S(1)}, u32[]{:S(2)}, u32[]{:S(2)}) collective-permute-start(bf16[72,1152]{1,0:T(8,128)(2,1)S(1)} %get-tuple-element.33), channel_id=1, source_target_pairs={{0,128},{64,192},{128,0},{192,64},{1,129},{65,193},{129,1},{193,65... | collective-permute-start | bytes 497672 | tf_op jit(solution)/shard_map/ppermute | solution.py:26
  119.9 9.7 %collective-permute-start.13 = (bf16[72,1152]{1,0:T(8,128)(2,1)S(1)}, bf16[72,1152]{1,0:T(8,128)(2,1)S(1)}, u32[]{:S(2)}, u32[]{:S(2)}) collective-permute-start(bf16[72,1152]{1,0:T(8,128)(2,1)S(1)} %get-tuple-element.34), channel_id=1, source_target_pairs={{0,192},{64,128},{128,64},{192,0},{1,193},{65,129},{129,65},{193,1... | collective-permute-start | bytes 497672 | tf_op jit(solution)/shard_map/ppermute | solution.py:26
  122.9 6.7 %collective-permute-start.12 = (bf16[72,1152]{1,0:T(8,128)(2,1)S(1)}, bf16[72,1152]{1,0:T(8,128)(2,1)S(1)}, u32[]{:S(2)}, u32[]{:S(2)}) collective-permute-start(bf16[72,1152]{1,0:T(8,128)(2,1)S(1)} %get-tuple-element.35), channel_id=1, source_target_pairs={{0,64},{64,0},{128,192},{192,128},{1,65},{65,1},{129,193},{193,129... | collective-permute-start | bytes 497672 | tf_op jit(solution)/shard_map/ppermute | solution.py:26
  129.8 7.6 %collective-permute-start.15 = (bf16[36,1152]{1,0:T(8,128)(2,1)S(1)}, bf16[36,1152]{1,0:T(8,128)(2,1)S(1)}, u32[]{:S(2)}, u32[]{:S(2)}) collective-permute-start(bf16[36,1152]{1,0:T(8,128)(2,1)S(1)} %pad_maximum_fusion.1), channel_id=1, source_target_pairs={{0,56},{8,48},{16,40},{24,32},{32,24},{40,16},{48,8},{56,0},{1,57}... | collective-permute-start | bytes 248840 | tf_op jit(solution)/shard_map/ppermute | solution.py:26
  130.9 8.1 %collective-permute-start.16 = (bf16[36,1152]{1,0:T(8,128)(2,1)S(1)}, bf16[36,1152]{1,0:T(8,128)(2,1)S(1)}, u32[]{:S(2)}, u32[]{:S(2)}) collective-permute-start(bf16[36,1152]{1,0:T(8,128)(2,1)S(1)} %pad_maximum_fusion.2), channel_id=1, source_target_pairs={{0,8},{8,0},{16,24},{24,16},{32,40},{40,32},{48,56},{56,48},{1,9},... | collective-permute-start | bytes 248840 | tf_op jit(solution)/shard_map/ppermute | solution.py:26
  134.2 6.7 %collective-permute-start.14 = (bf16[36,1152]{1,0:T(8,128)(2,1)S(1)}, bf16[36,1152]{1,0:T(8,128)(2,1)S(1)}, u32[]{:S(2)}, u32[]{:S(2)}) collective-permute-start(bf16[36,1152]{1,0:T(8,128)(2,1)S(1)} %pad_maximum_fusion), channel_id=1, source_target_pairs={{0,48},{8,56},{16,32},{24,40},{32,16},{40,24},{48,0},{56,8},{1,49}... | collective-permute-start | bytes 248840 | tf_op jit(solution)/shard_map/ppermute | solution.py:26
  141.0 5.7 %collective-permute-start.17 = (bf16[18,1152]{1,0:T(8,128)(2,1)S(1)}, bf16[18,1152]{1,0:T(8,128)(2,1)S(1)}, u32[]{:S(2)}, u32[]{:S(2)}) collective-permute-start(bf16[18,1152]{1,0:T(8,128)(2,1)S(1)} %get-tuple-element.39), channel_id=1, source_target_pairs={{0,16},{8,24},{16,0},{24,8},{32,48},{40,56},{48,32},{56,40},{1,17}... | collective-permute-start | bytes 124424 | tf_op jit(solution)/shard_map/ppermute | solution.py:26

commit v4 on v3

--- a/solution.py
+++ b/solution.py
@@ -40,15 +40,19 @@
     loads = [pltpu.make_async_copy(array, held.at[i], sems.at[i]) for i, array in enumerate((hidden, grad))]
     for load in loads:
         load.start()
-    at = lambda a: pick(
-        512, ROWS, lambda i: jnp.where(((i >> 2) & 1) == a, ((i >> 1) & 1) * 128 + (i >> 3) * 2 + (i & 1), -1)
-    )
+    from_row = lambda i: ((i >> 2) & 1) * 256 + ((i >> 1) & 1) * 128 + (i >> 3) * 2 + (i & 1)
+    chosen = [pick(ROWS, 512, lambda i: from_row(i + ROWS * half)) for half in range(2)]
     for load in loads:
         load.wait()
-    sent[...] = (mm(at(0), held[0], NN) + mm(at(1), held[1], NN)).astype(BF)
-    store = pltpu.make_async_copy(sent, out, sems.at[2])
-    store.start()
-    store.wait()
+    rows = jnp.concatenate([held[0], held[1]], axis=0)
+    stores = []
+    for half in range(2):
+        cut = pl.ds(ROWS * half, ROWS)
+        sent[cut, :] = mm(chosen[half], rows, NN).astype(BF)
+        stores.append(pltpu.make_async_copy(sent.at[cut], out.at[cut], sems.at[2 + half]))
+        stores[half].start()
+    for store in stores:
+        store.wait()
 
 
 def column_order(place, start, count):
@@ -91,9 +95,9 @@
     loads = [pltpu.make_async_copy(prepared.at[pl.ds(D * i, D)], weights.at[i], sems.at[i]) for i in order]
     for load in loads:
         load.start()
-    place = lambda a: lambda i: ((i >> 1) & 63) * 8 + a * 4 + (i & 1) * 2 + (i >> 7)
-    gout = mm(pick(ROWS, 512, place(1)), got[...], NN).astype(BF)
-    hid = mm(pick(ROWS, 512, place(0)), got[...], NN).astype(BF)
+    from_row = lambda i: ((i >> 1) & 63) * 8 + (i >> 8) * 4 + (i & 1) * 2 + ((i >> 7) & 1)
+    moved = mm(pick(512, 512, from_row), got[...], NN).astype(BF)
+    hid, gout = moved[:ROWS], moved[ROWS:]
     loads[0].wait()
     for i in range(3):
         cut = slice(384 * i, 384 * (i + 1))
@@ -169,10 +173,9 @@
         part = mm(rows, w_t[b], TN)
         total = part if total is None else total + part
     total = total.astype(BF)
-    at = lambda a: pick(
-        512, ROWS, lambda i: jnp.where(((i >> 2) & 1) == a, (i & 1) * 128 + (i >> 3) * 2 + ((i >> 1) & 1), -1)
-    )
-    sent[...] = (mm(at(0), total[:, :640], NN) + mm(at(1), total[:, 512:], NN)).astype(BF)
+    from_row = lambda i: ((i >> 2) & 1) * 256 + (i & 1) * 128 + (i >> 3) * 2 + ((i >> 1) & 1)
+    columns = jnp.concatenate([total[:, :640], total[:, 512:]], axis=0)
+    sent[...] = mm(pick(512, 512, from_row), columns, NN).astype(BF)
     store = pltpu.make_async_copy(sent, out, sems.at[4])
     store.start()
     store.wait()
@@ -274,7 +277,7 @@
         (hidden_in.reshape(ROWS, D), grad_out.reshape(ROWS, D)),
         10**9,
         58,
-        scratch=[pltpu.VMEM((2, ROWS, D), BF), pltpu.VMEM((512, D), BF), pltpu.SemaphoreType.DMA((3,))],
+        scratch=[pltpu.VMEM((2, ROWS, D), BF), pltpu.VMEM((512, D), BF), pltpu.SemaphoreType.DMA((4,))],
         specs=[ANY, ANY],
     )
     both = lax.all_to_all(both, FRAME, split_axis=0, concat_axis=0, tiled=True)
@@ -315,11 +318,12 @@
     sum_b = total(sum_b[0], got_b).reshape(4, 18, D)
     got = [flip(jnp.concatenate([sum_a[i], sum_b[i]]).astype(BF), "z", s) for i, s in ((2, 6), (3, 7), (1, 1))]
     near = total(sum_a[0], [g[:18] for g in got])
+    grad_in = lax.all_to_all(grad_in, FRAME, split_axis=0, concat_axis=0, tiled=True)
+    (grad_in,) = call(unpack_kernel, [shape(ROWS, D)], (grad_in,), 10**9, 16)
+    near, grad_in = lax.optimization_barrier((near, grad_in))
     far = flip(total(sum_b[0], [g[18:] for g in got]).astype(BF), "z", 2)
     grad_wqkv = total(near[:, :864], [far[:, :864]])
     grad_wout = total(near[:, 864:], [far[:, 864:]])
-    grad_in = lax.all_to_all(grad_in, FRAME, split_axis=0, concat_axis=0, tiled=True)
-    (grad_in,) = call(unpack_kernel, [shape(ROWS, D)], (grad_in,), 10**9, 16)
     return grad_in.reshape(2, 128, D), grad_wqkv, grad_wout
 
 

time: 150 us -> 147 us (0.980)
  transfers between devices with their start and end apart: 20 -> 20, of which waited for: 13 -> 13; matrix products, arithmetic and copies ran while one was open for 4% -> 3% of each run, Pallas kernels for 11% -> 12%
where the time goes in v4:
time: 147 us
  waiting for transfers between devices  51.5 us (35%)
  starting transfers between devices  44.5 us (30%)
  Pallas kernels  39.6 us (27%)
  other arithmetic  5.34 us (4%)
  local copies, waits for them, and re-layouts  5.26 us (4%)
    pallas_call x6, Pallas kernels, call(): pl.pallas_call(kernel, out_shape=outs, in_specs=specs or [VMEM] * len(ins...  39.6 us
    ppermute x18, waiting for transfers between devices, flip(): return lax.ppermute(array, axes, [(i, i ^ step) for i in range(size)])  32.9 us
    ppermute x18, starting transfers between devices, flip(): return lax.ppermute(array, axes, [(i, i ^ step) for i in range(size)])  22.6 us
    all_to_all x1, waiting for transfers between devices, per_device(): both = lax.all_to_all(both, FRAME, split_axis=0, concat_axis=0, tiled=True)  18.6 us
    all_to_all x1, starting transfers between devices, per_device(): both = lax.all_to_all(both, FRAME, split_axis=0, concat_axis=0, tiled=True)  13.7 us
    all_to_all x1, starting transfers between devices, per_device(): lax.all_to_all(grad_in, FRAME, split_axis=0, concat_axis=0, tiled=True)  8.18 us
    unnamed x6, local copies, waits for them, and re-layouts  5.01 us
  transfers between devices with their start and end apart: 20, of which 13 were waited for; matrix products, arithmetic and copies ran while one was open for 3% of the time, Pallas kernels for 12%

profile of v4, /device:TPU:8, one launch (start us, length us, event | category | flops | bytes accessed | tf_op | source)
XLA Modules:
  0.0 147.0 jit_solution(633474286884615204)
XLA Ops:
  0.6 3.0 %shard_map.67 = bf16[512,1152]{1,0:T(8,128)(2,1)} custom-call(bf16[256,1152]{1,0:T(8,128)(2,1)} %bitcast.30, bf16[256,1152]{1,0:T(8,128)(2,1)} %bitcast.31), custom_call_target="tpu_custom_call" | custom-call | flops 1000000000 | bytes 10000000 | tf_op jit(solution)/shard_map/pallas_call | solution.py:226
  3.6 13.7 %all-to-all-start = ((bf16[64,8,1152]{2,1,0:T(8,128)(2,1)}), bf16[64,8,1152]{2,1,0:T(8,128)(2,1)S(1)}, u32[]{:S(2)}, u32[]{:S(2)}) async-start(bf16[64,8,1152]{2,1,0:T(8,128)(2,1)} %bitcast.29), calls=%async_computation | async-start | bytes 2359296 | tf_op jit(solution)/shard_map/all_to_all | solution.py:283
  17.4 3.3 %copy-done = bf16[1152,3456]{1,0:T(8,128)(2,1)S(1)} copy-done((bf16[1152,3456]{1,0:T(8,128)(2,1)S(1)}, bf16[1152,3456]{1,0:T(8,128)(2,1)}, u32[]{:S(2)}) %copy-start) | copy-done | bytes 7962648
  20.6 1.7 %copy-done.1 = bf16[1152,1152]{1,0:T(8,128)(2,1)S(1)} copy-done((bf16[1152,1152]{1,0:T(8,128)(2,1)S(1)}, bf16[1152,1152]{1,0:T(8,128)(2,1)}, u32[]{:S(2)}) %copy-start.1) | copy-done | bytes 2654232
  22.4 9.5 %shard_map.68.prepared = bf16[16128,1152]{1,0:T(8,128)(2,1)} custom-call(s32[5]{0:T(128)S(1)} %stack.23.place.home, bf16[1152,3456]{1,0:T(8,128)(2,1)S(1)} %copy-done, bf16[1152,1152]{1,0:T(8,128)(2,1)S(1)} %copy-done.1), custom_call_target="tpu_custom_call" | custom-call | flops 1000000000 | bytes 10000000 | tf_op jit(solution)/shard_map/pallas_call | solution.py:226
  31.9 18.6 %all-to-all-done = bf16[64,8,1152]{2,1,0:T(8,128)(2,1)S(1)} async-done(((bf16[64,8,1152]{2,1,0:T(8,128)(2,1)}), bf16[64,8,1152]{2,1,0:T(8,128)(2,1)S(1)}, u32[]{:S(2)}, u32[]{:S(2)}) %all-to-all-start) | async-done | bytes 1179680 | tf_op jit(solution)/shard_map/all_to_all | solution.py:283
  50.5 12.7 %shard_map.69 = (bf16[2304,256]{1,0:T(8,128)(2,1)S(1)}, bf16[2,1152,256]{2,1,0:T(8,128)(2,1)S(1)}, bf16[2,1152,256]{2,1,0:T(8,128)(2,1)S(1)}) custom-call(s32[5]{0:T(128)S(1)} %stack.23.place.home, bf16[512,1152]{1,0:T(8,128)(2,1)S(1)} %bitcast.25, bf16[16128,1152]{1,0:T(8,128)(2,1)} %shard_map.68.prepared), custom_call_target="tpu_custom_call" | custom-call | flops 10000000000 | bytes 10000000 | tf_op jit(solution)/shard_map/pallas_call | solution.py:226
  63.8 2.3 %collective-permute-done.x_oth = bf16[2304,256]{1,0:T(8,128)(2,1)S(1)} collective-permute-done((bf16[2304,256]{1,0:T(8,128)(2,1)S(1)}, bf16[2304,256]{1,0:T(8,128)(2,1)S(1)}, u32[]{:S(2)}, u32[]{:S(2)}) %collective-permute-start) | collective-permute-done | bytes 1179680 | tf_op jit(solution)/shard_map/ppermute | solution.py:26
  66.1 1.7 %collective-permute-done.1.dg_oth = bf16[2,1152,256]{2,1,0:T(8,128)(2,1)S(1)} collective-permute-done((bf16[2,1152,256]{2,1,0:T(8,128)(2,1)S(1)}, bf16[2,1152,256]{2,1,0:T(8,128)(2,1)S(1)}, u32[]{:S(2)}, u32[]{:S(2)}) %collective-permute-start.1) | collective-permute-done | bytes 1179680 | tf_op jit(solution)/shard_map/ppermute | solution.py:26
  67.8 5.6 %shard_map.70 = (bf16[2,144,1152]{2,1,0:T(8,128)(2,1)S(1)}, bf16[2,144,1152]{2,1,0:T(8,128)(2,1)S(1)}, bf16[2,144,1152]{2,1,0:T(8,128)(2,1)}, bf16[2,144,1152]{2...) custom-call(bf16[2304,256]{1,0:T(8,128)(2,1)S(1)} %get-tuple-element, ...), custom_call_target="tpu_custom_call" | custom-call | flops 6000000000 | bytes 10000000 | tf_op jit(solution)/shard_map/pallas_call | solution.py:226
  74.1 1.8 %collective-permute-start.3 = (bf16[2,144,1152]{2,1,0:T(8,128)(2,1)}, bf16[2,144,1152]{2,1,0:T(8,128)(2,1)}, u32[]{:S(2)}, u32[]{:S(2)}) collective-permute-start(bf16[2,144,1152]{2,1,0:T(8,128)(2,1)} %get-tuple-element.23), channel_id=1, source_target_pairs={{0,128},{64,192},{128,0},{192,64},{1,129},{65,193},{129,1},{193,65... | collective-permute-start | bytes 1990664 | tf_op jit(solution)/shard_map/ppermute | solution.py:26
  76.0 2.2 %collective-permute-start.4 = (bf16[2,144,1152]{2,1,0:T(8,128)(2,1)}, bf16[2,144,1152]{2,1,0:T(8,128)(2,1)}, u32[]{:S(2)}, u32[]{:S(2)}) collective-permute-start(bf16[2,144,1152]{2,1,0:T(8,128)(2,1)} %get-tuple-element.24), channel_id=1, source_target_pairs={{0,192},{64,128},{128,64},{192,0},{1,193},{65,129},{129,65},{193,1... | collective-permute-start | bytes 1990664 | tf_op jit(solution)/shard_map/ppermute | solution.py:26
  78.4 1.3 collective-permute-start.9
  79.8 11.4 %collective-permute-done.2 = bf16[2,144,1152]{2,1,0:T(8,128)(2,1)S(1)} collective-permute-done((bf16[2,144,1152]{2,1,0:T(8,128)(2,1)S(1)}, bf16[2,144,1152]{2,1,0:T(8,128)(2,1)S(1)}, u32[]{:S(2)}, u32[]{:S(2)}) %collective-permute-start.2) | collective-permute-done | bytes 663584 | tf_op jit(solution)/shard_map/ppermute | solution.py:26
  91.2 7.5 %shard_map.71 = bf16[512,640]{1,0:T(8,128)(2,1)} custom-call(s32[5]{0:T(128)S(1)} %stack.23.place.home, bf16[2,1152,256]{2,1,0:T(8,128)(2,1)S(1)} %get-tuple-element.29.dg_own, bf16[2,1152,256]{2,1,0:T(8,128)(2,1)S(1)} %get-tuple-element.30.dg_other, bf16[16128,1152]{1,0:T(8,128)(2,1)} %shard_map.68.prepared), custom_call_target="tpu_custom_call" | custom-call | flops 3000000000 | bytes 10000000 | tf_op jit(solution)/shard_map/pallas_call | solution.py:226
  98.7 8.2 %all-to-all-start.1 = ((bf16[64,8,640]{2,1,0:T(8,128)(2,1)}), bf16[64,8,640]{2,1,0:T(8,128)(2,1)S(1)}, u32[]{:S(2)}, u32[]{:S(2)}) async-start(bf16[64,8,640]{2,1,0:T(8,128)(2,1)} %bitcast.14), calls=%async_computation.1 | async-start | bytes 1310720 | tf_op jit(solution)/shard_map/all_to_all | solution.py:321
  106.9 1.2 collective-permute-done.4
  108.1 1.8 %add_convert_fusion.1 = bf16[2,144,1152]{2,1,0:T(8,128)(2,1)S(1)} fusion(bf16[2,144,1152]{2,1,0:T(8,128)(2,1)} %collective-permute-done.4, bf16[2,144,1152]{2,1,0:T(8,128)(2,1)} %collective-permute-done.3, bf16[2,144,1152]{2,1,0:T(8,128)(2,1)} %copy-done.2, bf16[2,144,1152]{2,1,0:T(8,128)(2,1)S(1)} %get-tuple-element.21), kind=kLoop, calls=%fused_computation.1 | loop fusion | flops 2654208 | bytes 3317760 | tf_op jit(solution)/shard_map/convert_element_type | solution.py:311
  110.0 2.4 %collective-permute-start.5 = (bf16[72,1152]{1,0:T(8,128)(2,1)S(1)}, bf16[72,1152]{1,0:T(8,128)(2,1)S(1)}, u32[]{:S(2)}, u32[]{:S(2)}) collective-permute-start(bf16[72,1152]{1,0:T(8,128)(2,1)S(1)} %get-tuple-element.40), channel_id=1, source_target_pairs={{0,4},{2,6},{4,0},{6,2},{1,5},{3,7},{5,1},{7,3},{8,12},{10,14},{12... | collective-permute-start | bytes 497672 | tf_op jit(solution)/shard_map/ppermute | solution.py:26
  113.1 1.7 %collective-permute-start.6 = (bf16[72,1152]{1,0:T(8,128)(2,1)S(1)}, bf16[72,1152]{1,0:T(8,128)(2,1)S(1)}, u32[]{:S(2)}, u32[]{:S(2)}) collective-permute-start(bf16[72,1152]{1,0:T(8,128)(2,1)S(1)} %get-tuple-element.42), channel_id=1, source_target_pairs={{0,2},{2,0},{4,6},{6,4},{1,3},{3,1},{5,7},{7,5},{8,10},{10,8},{12,... | collective-permute-start | bytes 497672 | tf_op jit(solution)/shard_map/ppermute | solution.py:26
  114.8 1.8 %add_convert_fusion = bf16[288,1152]{1,0:T(8,128)(2,1)S(1)} fusion(bf16[288,1152]{1,0:T(8,128)(2,1)} %collective-permute-done.10, bf16[288,1152]{1,0:T(8,128)(2,1)} %collective-permute-done.9, bf16[288,1152]{1,0:T(8,128)(2,1)} %collective-permute-done.8, bf16[288,1152]{1,0:T(8,128)(2,1)S(1)} %get-tuple-element.25), kind=kLoop, calls=%fused_computation | loop fusion | flops 2654208 | bytes 3317760 | tf_op jit(solution)/shard_map/convert_element_type | solution.py:312
  116.7 2.1 %collective-permute-start.11 = (bf16[72,1152]{1,0:T(8,128)(2,1)S(1)}, bf16[72,1152]{1,0:T(8,128)(2,1)S(1)}, u32[]{:S(2)}, u32[]{:S(2)}) collective-permute-start(bf16[72,1152]{1,0:T(8,128)(2,1)S(1)} %get-tuple-element.37), channel_id=1, source_target_pairs={{0,128},{64,192},{128,0},{192,64},{1,129},{65,193},{129,1},{193,65... | collective-permute-start | bytes 497672 | tf_op jit(solution)/shard_map/ppermute | solution.py:26
  119.8 1.9 %collective-permute-done.5 = bf16[72,1152]{1,0:T(8,128)(2,1)S(1)} collective-permute-done((bf16[72,1152]{1,0:T(8,128)(2,1)S(1)}, bf16[72,1152]{1,0:T(8,128)(2,1)S(1)}, u32[]{:S(2)}, u32[]{:S(2)}) %collective-permute-start.5) | collective-permute-done | bytes 165920 | tf_op jit(solution)/shard_map/ppermute | solution.py:26
  122.1 3.2 %collective-permute-done.7 = bf16[72,1152]{1,0:T(8,128)(2,1)S(1)} collective-permute-done((bf16[72,1152]{1,0:T(8,128)(2,1)S(1)}, bf16[72,1152]{1,0:T(8,128)(2,1)S(1)}, u32[]{:S(2)}, u32[]{:S(2)}) %collective-permute-start.7) | collective-permute-done | bytes 165920 | tf_op jit(solution)/shard_map/ppermute | solution.py:26
  126.4 2.2 %collective-permute-done.13 = bf16[72,1152]{1,0:T(8,128)(2,1)S(1)} collective-permute-done((bf16[72,1152]{1,0:T(8,128)(2,1)S(1)}, bf16[72,1152]{1,0:T(8,128)(2,1)S(1)}, u32[]{:S(2)}, u32[]{:S(2)}) %collective-permute-start.13) | collective-permute-done | bytes 165920 | tf_op jit(solution)/shard_map/ppermute | solution.py:26
  129.8 3.2 %collective-permute-start.16 = (bf16[36,1152]{1,0:T(8,128)(2,1)S(1)}, bf16[36,1152]{1,0:T(8,128)(2,1)S(1)}, u32[]{:S(2)}, u32[]{:S(2)}) collective-permute-start(bf16[36,1152]{1,0:T(8,128)(2,1)S(1)} %pad_maximum_fusion.2), channel_id=1, source_target_pairs={{0,8},{8,0},{16,24},{24,16},{32,40},{40,32},{48,56},{56,48},{1,9},... | collective-permute-start | bytes 248840 | tf_op jit(solution)/shard_map/ppermute | solution.py:26
  133.9 2.4 %collective-permute-done.15 = bf16[36,1152]{1,0:T(8,128)(2,1)S(1)} collective-permute-done((bf16[36,1152]{1,0:T(8,128)(2,1)S(1)}, bf16[36,1152]{1,0:T(8,128)(2,1)S(1)}, u32[]{:S(2)}, u32[]{:S(2)}) %collective-permute-start.15) | collective-permute-done | bytes 82976 | tf_op jit(solution)/shard_map/ppermute | solution.py:26
  136.3 1.7 %collective-permute-done.16 = bf16[36,1152]{1,0:T(8,128)(2,1)S(1)} collective-permute-done((bf16[36,1152]{1,0:T(8,128)(2,1)S(1)}, bf16[36,1152]{1,0:T(8,128)(2,1)S(1)}, u32[]{:S(2)}, u32[]{:S(2)}) %collective-permute-start.16) | collective-permute-done | bytes 82976 | tf_op jit(solution)/shard_map/ppermute | solution.py:26
  137.9 1.9 %collective-permute-done.14 = bf16[36,1152]{1,0:T(8,128)(2,1)S(1)} collective-permute-done((bf16[36,1152]{1,0:T(8,128)(2,1)S(1)}, bf16[36,1152]{1,0:T(8,128)(2,1)S(1)}, u32[]{:S(2)}, u32[]{:S(2)}) %collective-permute-start.14) | collective-permute-done | bytes 82976 | tf_op jit(solution)/shard_map/ppermute | solution.py:26
  139.9 2.4 %collective-permute-start.17 = (bf16[18,1152]{1,0:T(8,128)(2,1)S(1)}, bf16[18,1152]{1,0:T(8,128)(2,1)S(1)}, u32[]{:S(2)}, u32[]{:S(2)}) collective-permute-start(bf16[18,1152]{1,0:T(8,128)(2,1)S(1)} %get-tuple-element.43), channel_id=1, source_target_pairs={{0,16},{8,24},{16,0},{24,8},{32,48},{40,56},{48,32},{56,40},{1,17}... | collective-permute-start | bytes 124424 | tf_op jit(solution)/shard_map/ppermute | solution.py:26
  142.3 1.3 shard_map.72
  143.6 2.0 %collective-permute-done.17 = bf16[18,1152]{1,0:T(8,128)(2,1)S(1)} collective-permute-done((bf16[18,1152]{1,0:T(8,128)(2,1)S(1)}, bf16[18,1152]{1,0:T(8,128)(2,1)S(1)}, u32[]{:S(2)}, u32[]{:S(2)}) %collective-permute-start.17) | collective-permute-done | bytes 41504 | tf_op jit(solution)/shard_map/ppermute | solution.py:26
  (34 shorter events, 8.3 us)
Async XLA Ops:
  3.6 46.9 %all-to-all-start = ((bf16[64,8,1152]{2,1,0:T(8,128)(2,1)}), bf16[64,8,1152]{2,1,0:T(8,128)(2,1)S(1)}, u32[]{:S(2)}, u32[]{:S(2)}) async-start(bf16[64,8,1152]{2,1,0:T(8,128)(2,1)} %bitcast.29), calls=%async_computation | async-start | bytes 2359296 | tf_op jit(solution)/shard_map/all_to_all | solution.py:283
  17.4 3.3 %copy-start = (bf16[1152,3456]{1,0:T(8,128)(2,1)S(1)}, bf16[1152,3456]{1,0:T(8,128)(2,1)}, u32[]{:S(2)}) copy-start(bf16[1152,3456]{1,0:T(8,128)(2,1)} %w_qkv.1) | copy-start | bytes 23887876
  20.6 1.7 %copy-start.1 = (bf16[1152,1152]{1,0:T(8,128)(2,1)S(1)}, bf16[1152,1152]{1,0:T(8,128)(2,1)}, u32[]{:S(2)}) copy-start(bf16[1152,1152]{1,0:T(8,128)(2,1)} %w_out.1) | copy-start | bytes 7962628
  63.2 2.9 %collective-permute-start = (bf16[2304,256]{1,0:T(8,128)(2,1)S(1)}, bf16[2304,256]{1,0:T(8,128)(2,1)S(1)}, u32[]{:S(2)}, u32[]{:S(2)}) collective-permute-start(bf16[2304,256]{1,0:T(8,128)(2,1)S(1)} %get-tuple-element.18.x_own), channel_id=1, source_target_pairs={{0,1},{1,0},{2,3},{3,2},{4,5},{5,4},{6,7},{7,6},{8,9},{9,8},{10,11... | collective-permute-start | bytes 3538952 | tf_op jit(solution)/shard_map/ppermute | solution.py:26
  63.3 4.5 %collective-permute-start.1 = (bf16[2,1152,256]{2,1,0:T(8,128)(2,1)S(1)}, bf16[2,1152,256]{2,1,0:T(8,128)(2,1)S(1)}, u32[]{:S(2)}, u32[]{:S(2)}) collective-permute-start(bf16[2,1152,256]{2,1,0:T(8,128)(2,1)S(1)} %get-tuple-element.30.dg_other), channel_id=1, source_target_pairs={{0,1},{1,0},{2,3},{3,2},{4,5},{5,4},{6,7},{7,6},{8,9},{9,8},{10,11... | collective-permute-start | bytes 3538952 | tf_op jit(solution)/shard_map/ppermute | solution.py:26
  73.5 17.8 %collective-permute-start.2 = (bf16[2,144,1152]{2,1,0:T(8,128)(2,1)S(1)}, bf16[2,144,1152]{2,1,0:T(8,128)(2,1)S(1)}, u32[]{:S(2)}, u32[]{:S(2)}) collective-permute-start(bf16[2,144,1152]{2,1,0:T(8,128)(2,1)S(1)} %get-tuple-element.22), channel_id=1, source_target_pairs={{0,64},{64,0},{128,192},{192,128},{1,65},{65,1},{129,193},{193,129... | collective-permute-start | bytes 1990664 | tf_op jit(solution)/shard_map/ppermute | solution.py:26
  74.1 32.8 %collective-permute-start.3 = (bf16[2,144,1152]{2,1,0:T(8,128)(2,1)}, bf16[2,144,1152]{2,1,0:T(8,128)(2,1)}, u32[]{:S(2)}, u32[]{:S(2)}) collective-permute-start(bf16[2,144,1152]{2,1,0:T(8,128)(2,1)} %get-tuple-element.23), channel_id=1, source_target_pairs={{0,128},{64,192},{128,0},{192,64},{1,129},{65,193},{129,1},{193,65... | collective-permute-start | bytes 1990664 | tf_op jit(solution)/shard_map/ppermute | solution.py:26
  76.0 32.1 %collective-permute-start.4 = (bf16[2,144,1152]{2,1,0:T(8,128)(2,1)}, bf16[2,144,1152]{2,1,0:T(8,128)(2,1)}, u32[]{:S(2)}, u32[]{:S(2)}) collective-permute-start(bf16[2,144,1152]{2,1,0:T(8,128)(2,1)} %get-tuple-element.24), channel_id=1, source_target_pairs={{0,192},{64,128},{128,64},{192,0},{1,193},{65,129},{129,65},{193,1... | collective-permute-start | bytes 1990664 | tf_op jit(solution)/shard_map/ppermute | solution.py:26
  78.2 34.9 %collective-permute-start.8 = (bf16[288,1152]{1,0:T(8,128)(2,1)}, bf16[288,1152]{1,0:T(8,128)(2,1)}, u32[]{:S(2)}, u32[]{:S(2)}) collective-permute-start(bf16[288,1152]{1,0:T(8,128)(2,1)} %get-tuple-element.26), channel_id=1, source_target_pairs={{0,4},{2,6},{4,0},{6,2},{1,5},{3,7},{5,1},{7,3},{8,12},{10,14},{12... | collective-permute-start | bytes 1990664 | tf_op jit(solution)/shard_map/ppermute | solution.py:26
  78.4 36.4 %collective-permute-start.9 = (bf16[288,1152]{1,0:T(8,128)(2,1)S(1)}, bf16[288,1152]{1,0:T(8,128)(2,1)}, u32[]{:S(2)}, u32[]{:S(2)}) collective-permute-start(bf16[288,1152]{1,0:T(8,128)(2,1)S(1)} %get-tuple-element.27), channel_id=1, source_target_pairs={{0,2},{2,0},{4,6},{6,4},{1,3},{3,1},{5,7},{7,5},{8,10},{10,8},{12,... | collective-permute-start | bytes 1990664 | tf_op jit(solution)/shard_map/ppermute | solution.py:26
  91.2 7.5 %copy-start.2 = (bf16[2,144,1152]{2,1,0:T(8,128)(2,1)}, bf16[2,144,1152]{2,1,0:T(8,128)(2,1)S(1)}, u32[]{:S(2)}) copy-start(bf16[2,144,1152]{2,1,0:T(8,128)(2,1)S(1)} %collective-permute-done.2) | copy-start | bytes 1990660
  91.2 23.6 %collective-permute-start.10 = (bf16[288,1152]{1,0:T(8,128)(2,1)S(1)}, bf16[288,1152]{1,0:T(8,128)(2,1)}, u32[]{:S(2)}, u32[]{:S(2)}) collective-permute-start(bf16[288,1152]{1,0:T(8,128)(2,1)S(1)} %get-tuple-element.28), channel_id=1, source_target_pairs={{0,6},{2,4},{4,2},{6,0},{1,7},{3,5},{5,3},{7,1},{8,14},{10,12},{12... | collective-permute-start | bytes 1990664 | tf_op jit(solution)/shard_map/ppermute | solution.py:26
  98.7 43.5 %all-to-all-start.1 = ((bf16[64,8,640]{2,1,0:T(8,128)(2,1)}), bf16[64,8,640]{2,1,0:T(8,128)(2,1)S(1)}, u32[]{:S(2)}, u32[]{:S(2)}) async-start(bf16[64,8,640]{2,1,0:T(8,128)(2,1)} %bitcast.14), calls=%async_computation.1 | async-start | bytes 1310720 | tf_op jit(solution)/shard_map/all_to_all | solution.py:321
  110.0 11.8 %collective-permute-start.5 = (bf16[72,1152]{1,0:T(8,128)(2,1)S(1)}, bf16[72,1152]{1,0:T(8,128)(2,1)S(1)}, u32[]{:S(2)}, u32[]{:S(2)}) collective-permute-start(bf16[72,1152]{1,0:T(8,128)(2,1)S(1)} %get-tuple-element.40), channel_id=1, source_target_pairs={{0,4},{2,6},{4,0},{6,2},{1,5},{3,7},{5,1},{7,3},{8,12},{10,14},{12... | collective-permute-start | bytes 497672 | tf_op jit(solution)/shard_map/ppermute | solution.py:26
  112.4 12.9 %collective-permute-start.7 = (bf16[72,1152]{1,0:T(8,128)(2,1)S(1)}, bf16[72,1152]{1,0:T(8,128)(2,1)S(1)}, u32[]{:S(2)}, u32[]{:S(2)}) collective-permute-start(bf16[72,1152]{1,0:T(8,128)(2,1)S(1)} %get-tuple-element.41), channel_id=1, source_target_pairs={{0,6},{2,4},{4,2},{6,0},{1,7},{3,5},{5,3},{7,1},{8,14},{10,12},{12... | collective-permute-start | bytes 497672 | tf_op jit(solution)/shard_map/ppermute | solution.py:26
  113.1 12.3 %collective-permute-start.6 = (bf16[72,1152]{1,0:T(8,128)(2,1)S(1)}, bf16[72,1152]{1,0:T(8,128)(2,1)S(1)}, u32[]{:S(2)}, u32[]{:S(2)}) collective-permute-start(bf16[72,1152]{1,0:T(8,128)(2,1)S(1)} %get-tuple-element.42), channel_id=1, source_target_pairs={{0,2},{2,0},{4,6},{6,4},{1,3},{3,1},{5,7},{7,5},{8,10},{10,8},{12,... | collective-permute-start | bytes 497672 | tf_op jit(solution)/shard_map/ppermute | solution.py:26
  116.7 9.7 %collective-permute-start.11 = (bf16[72,1152]{1,0:T(8,128)(2,1)S(1)}, bf16[72,1152]{1,0:T(8,128)(2,1)S(1)}, u32[]{:S(2)}, u32[]{:S(2)}) collective-permute-start(bf16[72,1152]{1,0:T(8,128)(2,1)S(1)} %get-tuple-element.37), channel_id=1, source_target_pairs={{0,128},{64,192},{128,0},{192,64},{1,129},{65,193},{129,1},{193,65... | collective-permute-start | bytes 497672 | tf_op jit(solution)/shard_map/ppermute | solution.py:26
  118.8 9.7 %collective-permute-start.13 = (bf16[72,1152]{1,0:T(8,128)(2,1)S(1)}, bf16[72,1152]{1,0:T(8,128)(2,1)S(1)}, u32[]{:S(2)}, u32[]{:S(2)}) collective-permute-start(bf16[72,1152]{1,0:T(8,128)(2,1)S(1)} %get-tuple-element.38), channel_id=1, source_target_pairs={{0,192},{64,128},{128,64},{192,0},{1,193},{65,129},{129,65},{193,1... | collective-permute-start | bytes 497672 | tf_op jit(solution)/shard_map/ppermute | solution.py:26
  121.8 6.7 %collective-permute-start.12 = (bf16[72,1152]{1,0:T(8,128)(2,1)S(1)}, bf16[72,1152]{1,0:T(8,128)(2,1)S(1)}, u32[]{:S(2)}, u32[]{:S(2)}) collective-permute-start(bf16[72,1152]{1,0:T(8,128)(2,1)S(1)} %get-tuple-element.39), channel_id=1, source_target_pairs={{0,64},{64,0},{128,192},{192,128},{1,65},{65,1},{129,193},{193,129... | collective-permute-start | bytes 497672 | tf_op jit(solution)/shard_map/ppermute | solution.py:26
  128.7 7.5 %collective-permute-start.15 = (bf16[36,1152]{1,0:T(8,128)(2,1)S(1)}, bf16[36,1152]{1,0:T(8,128)(2,1)S(1)}, u32[]{:S(2)}, u32[]{:S(2)}) collective-permute-start(bf16[36,1152]{1,0:T(8,128)(2,1)S(1)} %pad_maximum_fusion.1), channel_id=1, source_target_pairs={{0,56},{8,48},{16,40},{24,32},{32,24},{40,16},{48,8},{56,0},{1,57}... | collective-permute-start | bytes 248840 | tf_op jit(solution)/shard_map/ppermute | solution.py:26
  129.8 8.1 %collective-permute-start.16 = (bf16[36,1152]{1,0:T(8,128)(2,1)S(1)}, bf16[36,1152]{1,0:T(8,128)(2,1)S(1)}, u32[]{:S(2)}, u32[]{:S(2)}) collective-permute-start(bf16[36,1152]{1,0:T(8,128)(2,1)S(1)} %pad_maximum_fusion.2), channel_id=1, source_target_pairs={{0,8},{8,0},{16,24},{24,16},{32,40},{40,32},{48,56},{56,48},{1,9},... | collective-permute-start | bytes 248840 | tf_op jit(solution)/shard_map/ppermute | solution.py:26
  133.0 6.7 %collective-permute-start.14 = (bf16[36,1152]{1,0:T(8,128)(2,1)S(1)}, bf16[36,1152]{1,0:T(8,128)(2,1)S(1)}, u32[]{:S(2)}, u32[]{:S(2)}) collective-permute-start(bf16[36,1152]{1,0:T(8,128)(2,1)S(1)} %pad_maximum_fusion), channel_id=1, source_target_pairs={{0,48},{8,56},{16,32},{24,40},{32,16},{40,24},{48,0},{56,8},{1,49}... | collective-permute-start | bytes 248840 | tf_op jit(solution)/shard_map/ppermute | solution.py:26
  139.9 5.7 %collective-permute-start.17 = (bf16[18,1152]{1,0:T(8,128)(2,1)S(1)}, bf16[18,1152]{1,0:T(8,128)(2,1)S(1)}, u32[]{:S(2)}, u32[]{:S(2)}) collective-permute-start(bf16[18,1152]{1,0:T(8,128)(2,1)S(1)} %get-tuple-element.43), channel_id=1, source_target_pairs={{0,16},{8,24},{16,0},{24,8},{32,48},{40,56},{48,32},{56,40},{1,17}... | collective-permute-start | bytes 124424 | tf_op jit(solution)/shard_map/ppermute | solution.py:26

commit v5 on v4

--- a/solution.py
+++ b/solution.py
@@ -17,7 +17,7 @@
 ANY = pl.BlockSpec(memory_space=pl.ANY)
 SMEM = pl.BlockSpec(memory_space=pltpu.SMEM)
 MIB = 1024 * 1024
-CUTS = 2
+CUTS = 1
 TOGETHER = 4
 
 

time: 147 us -> 147 us (level)
  no operation moved by 1% of the time
where the time goes in v5:
time: 147 us
  waiting for transfers between devices  51.4 us (35%)
  starting transfers between devices  44.5 us (30%)
  Pallas kernels  39.6 us (27%)
  other arithmetic  5.34 us (4%)
  local copies, waits for them, and re-layouts  5.26 us (4%)
    pallas_call x6, Pallas kernels, call(): pl.pallas_call(kernel, out_shape=outs, in_specs=specs or [VMEM] * len(ins...  39.6 us
    ppermute x18, waiting for transfers between devices, flip(): return lax.ppermute(array, axes, [(i, i ^ step) for i in range(size)])  32.8 us
    ppermute x18, starting transfers between devices, flip(): return lax.ppermute(array, axes, [(i, i ^ step) for i in range(size)])  22.6 us
    all_to_all x1, waiting for transfers between devices, per_device(): both = lax.all_to_all(both, FRAME, split_axis=0, concat_axis=0, tiled=True)  18.6 us
    all_to_all x1, starting transfers between devices, per_device(): both = lax.all_to_all(both, FRAME, split_axis=0, concat_axis=0, tiled=True)  13.7 us
    all_to_all x1, starting transfers between devices, per_device(): lax.all_to_all(grad_in, FRAME, split_axis=0, concat_axis=0, tiled=True)  8.19 us
    unnamed x6, local copies, waits for them, and re-layouts  5.01 us
  transfers between devices with their start and end apart: 20, of which 13 were waited for; matrix products, arithmetic and copies ran while one was open for 3% of the time, Pallas kernels for 12%

profile of v5, /device:TPU:8, one launch (start us, length us, event | category | flops | bytes accessed | tf_op | source)
XLA Modules:
  0.0 147.0 jit_solution(16606993768735407762)
XLA Ops:
  0.6 3.0 %shard_map.67 = bf16[512,1152]{1,0:T(8,128)(2,1)} custom-call(bf16[256,1152]{1,0:T(8,128)(2,1)} %bitcast.30, bf16[256,1152]{1,0:T(8,128)(2,1)} %bitcast.31), custom_call_target="tpu_custom_call" | custom-call | flops 1000000000 | bytes 10000000 | tf_op jit(solution)/shard_map/pallas_call | solution.py:226
  3.6 13.7 %all-to-all-start = ((bf16[64,8,1152]{2,1,0:T(8,128)(2,1)}), bf16[64,8,1152]{2,1,0:T(8,128)(2,1)S(1)}, u32[]{:S(2)}, u32[]{:S(2)}) async-start(bf16[64,8,1152]{2,1,0:T(8,128)(2,1)} %bitcast.29), calls=%async_computation | async-start | bytes 2359296 | tf_op jit(solution)/shard_map/all_to_all | solution.py:283
  17.4 3.3 %copy-done = bf16[1152,3456]{1,0:T(8,128)(2,1)S(1)} copy-done((bf16[1152,3456]{1,0:T(8,128)(2,1)S(1)}, bf16[1152,3456]{1,0:T(8,128)(2,1)}, u32[]{:S(2)}) %copy-start) | copy-done | bytes 7962648
  20.6 1.7 %copy-done.1 = bf16[1152,1152]{1,0:T(8,128)(2,1)S(1)} copy-done((bf16[1152,1152]{1,0:T(8,128)(2,1)S(1)}, bf16[1152,1152]{1,0:T(8,128)(2,1)}, u32[]{:S(2)}) %copy-start.1) | copy-done | bytes 2654232
  22.4 9.5 %shard_map.68.prepared = bf16[16128,1152]{1,0:T(8,128)(2,1)} custom-call(s32[5]{0:T(128)S(1)} %stack.23.place.home, bf16[1152,3456]{1,0:T(8,128)(2,1)S(1)} %copy-done, bf16[1152,1152]{1,0:T(8,128)(2,1)S(1)} %copy-done.1), custom_call_target="tpu_custom_call" | custom-call | flops 1000000000 | bytes 10000000 | tf_op jit(solution)/shard_map/pallas_call | solution.py:226
  31.9 18.6 %all-to-all-done = bf16[64,8,1152]{2,1,0:T(8,128)(2,1)S(1)} async-done(((bf16[64,8,1152]{2,1,0:T(8,128)(2,1)}), bf16[64,8,1152]{2,1,0:T(8,128)(2,1)S(1)}, u32[]{:S(2)}, u32[]{:S(2)}) %all-to-all-start) | async-done | bytes 1179680 | tf_op jit(solution)/shard_map/all_to_all | solution.py:283
  50.5 12.7 %shard_map.69 = (bf16[2304,256]{1,0:T(8,128)(2,1)S(1)}, bf16[2,1152,256]{2,1,0:T(8,128)(2,1)S(1)}, bf16[2,1152,256]{2,1,0:T(8,128)(2,1)S(1)}) custom-call(s32[5]{0:T(128)S(1)} %stack.23.place.home, bf16[512,1152]{1,0:T(8,128)(2,1)S(1)} %bitcast.25, bf16[16128,1152]{1,0:T(8,128)(2,1)} %shard_map.68.prepared), custom_call_target="tpu_custom_call" | custom-call | flops 10000000000 | bytes 10000000 | tf_op jit(solution)/shard_map/pallas_call | solution.py:226
  63.8 2.3 %collective-permute-done.x_oth = bf16[2304,256]{1,0:T(8,128)(2,1)S(1)} collective-permute-done((bf16[2304,256]{1,0:T(8,128)(2,1)S(1)}, bf16[2304,256]{1,0:T(8,128)(2,1)S(1)}, u32[]{:S(2)}, u32[]{:S(2)}) %collective-permute-start) | collective-permute-done | bytes 1179680 | tf_op jit(solution)/shard_map/ppermute | solution.py:26
  66.1 1.7 %collective-permute-done.1.dg_oth = bf16[2,1152,256]{2,1,0:T(8,128)(2,1)S(1)} collective-permute-done((bf16[2,1152,256]{2,1,0:T(8,128)(2,1)S(1)}, bf16[2,1152,256]{2,1,0:T(8,128)(2,1)S(1)}, u32[]{:S(2)}, u32[]{:S(2)}) %collective-permute-start.1) | collective-permute-done | bytes 1179680 | tf_op jit(solution)/shard_map/ppermute | solution.py:26
  67.8 5.7 %shard_map.70 = (bf16[2,144,1152]{2,1,0:T(8,128)(2,1)S(1)}, bf16[2,144,1152]{2,1,0:T(8,128)(2,1)S(1)}, bf16[2,144,1152]{2,1,0:T(8,128)(2,1)}, bf16[2,144,1152]{2...) custom-call(bf16[2304,256]{1,0:T(8,128)(2,1)S(1)} %get-tuple-element, ...), custom_call_target="tpu_custom_call" | custom-call | flops 6000000000 | bytes 10000000 | tf_op jit(solution)/shard_map/pallas_call | solution.py:226
  74.1 1.8 %collective-permute-start.3 = (bf16[2,144,1152]{2,1,0:T(8,128)(2,1)}, bf16[2,144,1152]{2,1,0:T(8,128)(2,1)}, u32[]{:S(2)}, u32[]{:S(2)}) collective-permute-start(bf16[2,144,1152]{2,1,0:T(8,128)(2,1)} %get-tuple-element.23), channel_id=1, source_target_pairs={{0,128},{64,192},{128,0},{192,64},{1,129},{65,193},{129,1},{193,65... | collective-permute-start | bytes 1990664 | tf_op jit(solution)/shard_map/ppermute | solution.py:26
  76.0 2.2 %collective-permute-start.4 = (bf16[2,144,1152]{2,1,0:T(8,128)(2,1)}, bf16[2,144,1152]{2,1,0:T(8,128)(2,1)}, u32[]{:S(2)}, u32[]{:S(2)}) collective-permute-start(bf16[2,144,1152]{2,1,0:T(8,128)(2,1)} %get-tuple-element.24), channel_id=1, source_target_pairs={{0,192},{64,128},{128,64},{192,0},{1,193},{65,129},{129,65},{193,1... | collective-permute-start | bytes 1990664 | tf_op jit(solution)/shard_map/ppermute | solution.py:26
  78.4 1.3 collective-permute-start.9
  79.8 11.4 %collective-permute-done.2 = bf16[2,144,1152]{2,1,0:T(8,128)(2,1)S(1)} collective-permute-done((bf16[2,144,1152]{2,1,0:T(8,128)(2,1)S(1)}, bf16[2,144,1152]{2,1,0:T(8,128)(2,1)S(1)}, u32[]{:S(2)}, u32[]{:S(2)}) %collective-permute-start.2) | collective-permute-done | bytes 663584 | tf_op jit(solution)/shard_map/ppermute | solution.py:26
  91.2 7.5 %shard_map.71 = bf16[512,640]{1,0:T(8,128)(2,1)} custom-call(s32[5]{0:T(128)S(1)} %stack.23.place.home, bf16[2,1152,256]{2,1,0:T(8,128)(2,1)S(1)} %get-tuple-element.29.dg_own, bf16[2,1152,256]{2,1,0:T(8,128)(2,1)S(1)} %get-tuple-element.30.dg_other, bf16[16128,1152]{1,0:T(8,128)(2,1)} %shard_map.68.prepared), custom_call_target="tpu_custom_call" | custom-call | flops 3000000000 | bytes 10000000 | tf_op jit(solution)/shard_map/pallas_call | solution.py:226
  98.7 8.2 %all-to-all-start.1 = ((bf16[64,8,640]{2,1,0:T(8,128)(2,1)}), bf16[64,8,640]{2,1,0:T(8,128)(2,1)S(1)}, u32[]{:S(2)}, u32[]{:S(2)}) async-start(bf16[64,8,640]{2,1,0:T(8,128)(2,1)} %bitcast.14), calls=%async_computation.1 | async-start | bytes 1310720 | tf_op jit(solution)/shard_map/all_to_all | solution.py:321
  106.9 1.2 collective-permute-done.4
  108.1 1.8 %add_convert_fusion.1 = bf16[2,144,1152]{2,1,0:T(8,128)(2,1)S(1)} fusion(bf16[2,144,1152]{2,1,0:T(8,128)(2,1)} %collective-permute-done.4, bf16[2,144,1152]{2,1,0:T(8,128)(2,1)} %collective-permute-done.3, bf16[2,144,1152]{2,1,0:T(8,128)(2,1)} %copy-done.2, bf16[2,144,1152]{2,1,0:T(8,128)(2,1)S(1)} %get-tuple-element.21), kind=kLoop, calls=%fused_computation.1 | loop fusion | flops 2654208 | bytes 3317760 | tf_op jit(solution)/shard_map/convert_element_type | solution.py:311
  110.0 2.4 %collective-permute-start.5 = (bf16[72,1152]{1,0:T(8,128)(2,1)S(1)}, bf16[72,1152]{1,0:T(8,128)(2,1)S(1)}, u32[]{:S(2)}, u32[]{:S(2)}) collective-permute-start(bf16[72,1152]{1,0:T(8,128)(2,1)S(1)} %get-tuple-element.40), channel_id=1, source_target_pairs={{0,4},{2,6},{4,0},{6,2},{1,5},{3,7},{5,1},{7,3},{8,12},{10,14},{12... | collective-permute-start | bytes 497672 | tf_op jit(solution)/shard_map/ppermute | solution.py:26
  113.1 1.7 %collective-permute-start.6 = (bf16[72,1152]{1,0:T(8,128)(2,1)S(1)}, bf16[72,1152]{1,0:T(8,128)(2,1)S(1)}, u32[]{:S(2)}, u32[]{:S(2)}) collective-permute-start(bf16[72,1152]{1,0:T(8,128)(2,1)S(1)} %get-tuple-element.42), channel_id=1, source_target_pairs={{0,2},{2,0},{4,6},{6,4},{1,3},{3,1},{5,7},{7,5},{8,10},{10,8},{12,... | collective-permute-start | bytes 497672 | tf_op jit(solution)/shard_map/ppermute | solution.py:26
  114.8 1.8 %add_convert_fusion = bf16[288,1152]{1,0:T(8,128)(2,1)S(1)} fusion(bf16[288,1152]{1,0:T(8,128)(2,1)} %collective-permute-done.10, bf16[288,1152]{1,0:T(8,128)(2,1)} %collective-permute-done.9, bf16[288,1152]{1,0:T(8,128)(2,1)} %collective-permute-done.8, bf16[288,1152]{1,0:T(8,128)(2,1)S(1)} %get-tuple-element.25), kind=kLoop, calls=%fused_computation | loop fusion | flops 2654208 | bytes 3317760 | tf_op jit(solution)/shard_map/convert_element_type | solution.py:312
  116.7 2.1 %collective-permute-start.11 = (bf16[72,1152]{1,0:T(8,128)(2,1)S(1)}, bf16[72,1152]{1,0:T(8,128)(2,1)S(1)}, u32[]{:S(2)}, u32[]{:S(2)}) collective-permute-start(bf16[72,1152]{1,0:T(8,128)(2,1)S(1)} %get-tuple-element.37), channel_id=1, source_target_pairs={{0,128},{64,192},{128,0},{192,64},{1,129},{65,193},{129,1},{193,65... | collective-permute-start | bytes 497672 | tf_op jit(solution)/shard_map/ppermute | solution.py:26
  119.9 1.9 %collective-permute-done.5 = bf16[72,1152]{1,0:T(8,128)(2,1)S(1)} collective-permute-done((bf16[72,1152]{1,0:T(8,128)(2,1)S(1)}, bf16[72,1152]{1,0:T(8,128)(2,1)S(1)}, u32[]{:S(2)}, u32[]{:S(2)}) %collective-permute-start.5) | collective-permute-done | bytes 165920 | tf_op jit(solution)/shard_map/ppermute | solution.py:26
  122.1 3.2 %collective-permute-done.7 = bf16[72,1152]{1,0:T(8,128)(2,1)S(1)} collective-permute-done((bf16[72,1152]{1,0:T(8,128)(2,1)S(1)}, bf16[72,1152]{1,0:T(8,128)(2,1)S(1)}, u32[]{:S(2)}, u32[]{:S(2)}) %collective-permute-start.7) | collective-permute-done | bytes 165920 | tf_op jit(solution)/shard_map/ppermute | solution.py:26
  126.4 2.2 %collective-permute-done.13 = bf16[72,1152]{1,0:T(8,128)(2,1)S(1)} collective-permute-done((bf16[72,1152]{1,0:T(8,128)(2,1)S(1)}, bf16[72,1152]{1,0:T(8,128)(2,1)S(1)}, u32[]{:S(2)}, u32[]{:S(2)}) %collective-permute-start.13) | collective-permute-done | bytes 165920 | tf_op jit(solution)/shard_map/ppermute | solution.py:26
  129.8 3.2 %collective-permute-start.16 = (bf16[36,1152]{1,0:T(8,128)(2,1)S(1)}, bf16[36,1152]{1,0:T(8,128)(2,1)S(1)}, u32[]{:S(2)}, u32[]{:S(2)}) collective-permute-start(bf16[36,1152]{1,0:T(8,128)(2,1)S(1)} %pad_maximum_fusion.2), channel_id=1, source_target_pairs={{0,8},{8,0},{16,24},{24,16},{32,40},{40,32},{48,56},{56,48},{1,9},... | collective-permute-start | bytes 248840 | tf_op jit(solution)/shard_map/ppermute | solution.py:26
  133.9 2.4 %collective-permute-done.15 = bf16[36,1152]{1,0:T(8,128)(2,1)S(1)} collective-permute-done((bf16[36,1152]{1,0:T(8,128)(2,1)S(1)}, bf16[36,1152]{1,0:T(8,128)(2,1)S(1)}, u32[]{:S(2)}, u32[]{:S(2)}) %collective-permute-start.15) | collective-permute-done | bytes 82976 | tf_op jit(solution)/shard_map/ppermute | solution.py:26
  136.3 1.6 %collective-permute-done.16 = bf16[36,1152]{1,0:T(8,128)(2,1)S(1)} collective-permute-done((bf16[36,1152]{1,0:T(8,128)(2,1)S(1)}, bf16[36,1152]{1,0:T(8,128)(2,1)S(1)}, u32[]{:S(2)}, u32[]{:S(2)}) %collective-permute-start.16) | collective-permute-done | bytes 82976 | tf_op jit(solution)/shard_map/ppermute | solution.py:26
  137.9 1.9 %collective-permute-done.14 = bf16[36,1152]{1,0:T(8,128)(2,1)S(1)} collective-permute-done((bf16[36,1152]{1,0:T(8,128)(2,1)S(1)}, bf16[36,1152]{1,0:T(8,128)(2,1)S(1)}, u32[]{:S(2)}, u32[]{:S(2)}) %collective-permute-start.14) | collective-permute-done | bytes 82976 | tf_op jit(solution)/shard_map/ppermute | solution.py:26
  139.9 2.4 %collective-permute-start.17 = (bf16[18,1152]{1,0:T(8,128)(2,1)S(1)}, bf16[18,1152]{1,0:T(8,128)(2,1)S(1)}, u32[]{:S(2)}, u32[]{:S(2)}) collective-permute-start(bf16[18,1152]{1,0:T(8,128)(2,1)S(1)} %get-tuple-element.43), channel_id=1, source_target_pairs={{0,16},{8,24},{16,0},{24,8},{32,48},{40,56},{48,32},{56,40},{1,17}... | collective-permute-start | bytes 124424 | tf_op jit(solution)/shard_map/ppermute | solution.py:26
  142.3 1.3 shard_map.72
  143.6 2.0 %collective-permute-done.17 = bf16[18,1152]{1,0:T(8,128)(2,1)S(1)} collective-permute-done((bf16[18,1152]{1,0:T(8,128)(2,1)S(1)}, bf16[18,1152]{1,0:T(8,128)(2,1)S(1)}, u32[]{:S(2)}, u32[]{:S(2)}) %collective-permute-start.17) | collective-permute-done | bytes 41504 | tf_op jit(solution)/shard_map/ppermute | solution.py:26
  (34 shorter events, 8.3 us)
Async XLA Ops:
  3.6 46.9 %all-to-all-start = ((bf16[64,8,1152]{2,1,0:T(8,128)(2,1)}), bf16[64,8,1152]{2,1,0:T(8,128)(2,1)S(1)}, u32[]{:S(2)}, u32[]{:S(2)}) async-start(bf16[64,8,1152]{2,1,0:T(8,128)(2,1)} %bitcast.29), calls=%async_computation | async-start | bytes 2359296 | tf_op jit(solution)/shard_map/all_to_all | solution.py:283
  17.4 3.3 %copy-start = (bf16[1152,3456]{1,0:T(8,128)(2,1)S(1)}, bf16[1152,3456]{1,0:T(8,128)(2,1)}, u32[]{:S(2)}) copy-start(bf16[1152,3456]{1,0:T(8,128)(2,1)} %w_qkv.1) | copy-start | bytes 23887876
  20.6 1.7 %copy-start.1 = (bf16[1152,1152]{1,0:T(8,128)(2,1)S(1)}, bf16[1152,1152]{1,0:T(8,128)(2,1)}, u32[]{:S(2)}) copy-start(bf16[1152,1152]{1,0:T(8,128)(2,1)} %w_out.1) | copy-start | bytes 7962628
  63.2 2.9 %collective-permute-start = (bf16[2304,256]{1,0:T(8,128)(2,1)S(1)}, bf16[2304,256]{1,0:T(8,128)(2,1)S(1)}, u32[]{:S(2)}, u32[]{:S(2)}) collective-permute-start(bf16[2304,256]{1,0:T(8,128)(2,1)S(1)} %get-tuple-element.18.x_own), channel_id=1, source_target_pairs={{0,1},{1,0},{2,3},{3,2},{4,5},{5,4},{6,7},{7,6},{8,9},{9,8},{10,11... | collective-permute-start | bytes 3538952 | tf_op jit(solution)/shard_map/ppermute | solution.py:26
  63.3 4.5 %collective-permute-start.1 = (bf16[2,1152,256]{2,1,0:T(8,128)(2,1)S(1)}, bf16[2,1152,256]{2,1,0:T(8,128)(2,1)S(1)}, u32[]{:S(2)}, u32[]{:S(2)}) collective-permute-start(bf16[2,1152,256]{2,1,0:T(8,128)(2,1)S(1)} %get-tuple-element.30.dg_other), channel_id=1, source_target_pairs={{0,1},{1,0},{2,3},{3,2},{4,5},{5,4},{6,7},{7,6},{8,9},{9,8},{10,11... | collective-permute-start | bytes 3538952 | tf_op jit(solution)/shard_map/ppermute | solution.py:26
  73.5 17.8 %collective-permute-start.2 = (bf16[2,144,1152]{2,1,0:T(8,128)(2,1)S(1)}, bf16[2,144,1152]{2,1,0:T(8,128)(2,1)S(1)}, u32[]{:S(2)}, u32[]{:S(2)}) collective-permute-start(bf16[2,144,1152]{2,1,0:T(8,128)(2,1)S(1)} %get-tuple-element.22), channel_id=1, source_target_pairs={{0,64},{64,0},{128,192},{192,128},{1,65},{65,1},{129,193},{193,129... | collective-permute-start | bytes 1990664 | tf_op jit(solution)/shard_map/ppermute | solution.py:26
  74.1 32.8 %collective-permute-start.3 = (bf16[2,144,1152]{2,1,0:T(8,128)(2,1)}, bf16[2,144,1152]{2,1,0:T(8,128)(2,1)}, u32[]{:S(2)}, u32[]{:S(2)}) collective-permute-start(bf16[2,144,1152]{2,1,0:T(8,128)(2,1)} %get-tuple-element.23), channel_id=1, source_target_pairs={{0,128},{64,192},{128,0},{192,64},{1,129},{65,193},{129,1},{193,65... | collective-permute-start | bytes 1990664 | tf_op jit(solution)/shard_map/ppermute | solution.py:26
  76.0 32.1 %collective-permute-start.4 = (bf16[2,144,1152]{2,1,0:T(8,128)(2,1)}, bf16[2,144,1152]{2,1,0:T(8,128)(2,1)}, u32[]{:S(2)}, u32[]{:S(2)}) collective-permute-start(bf16[2,144,1152]{2,1,0:T(8,128)(2,1)} %get-tuple-element.24), channel_id=1, source_target_pairs={{0,192},{64,128},{128,64},{192,0},{1,193},{65,129},{129,65},{193,1... | collective-permute-start | bytes 1990664 | tf_op jit(solution)/shard_map/ppermute | solution.py:26
  78.2 34.9 %collective-permute-start.8 = (bf16[288,1152]{1,0:T(8,128)(2,1)}, bf16[288,1152]{1,0:T(8,128)(2,1)}, u32[]{:S(2)}, u32[]{:S(2)}) collective-permute-start(bf16[288,1152]{1,0:T(8,128)(2,1)} %get-tuple-element.26), channel_id=1, source_target_pairs={{0,4},{2,6},{4,0},{6,2},{1,5},{3,7},{5,1},{7,3},{8,12},{10,14},{12... | collective-permute-start | bytes 1990664 | tf_op jit(solution)/shard_map/ppermute | solution.py:26
  78.4 36.4 %collective-permute-start.9 = (bf16[288,1152]{1,0:T(8,128)(2,1)S(1)}, bf16[288,1152]{1,0:T(8,128)(2,1)}, u32[]{:S(2)}, u32[]{:S(2)}) collective-permute-start(bf16[288,1152]{1,0:T(8,128)(2,1)S(1)} %get-tuple-element.27), channel_id=1, source_target_pairs={{0,2},{2,0},{4,6},{6,4},{1,3},{3,1},{5,7},{7,5},{8,10},{10,8},{12,... | collective-permute-start | bytes 1990664 | tf_op jit(solution)/shard_map/ppermute | solution.py:26
  91.2 7.5 %copy-start.2 = (bf16[2,144,1152]{2,1,0:T(8,128)(2,1)}, bf16[2,144,1152]{2,1,0:T(8,128)(2,1)S(1)}, u32[]{:S(2)}) copy-start(bf16[2,144,1152]{2,1,0:T(8,128)(2,1)S(1)} %collective-permute-done.2) | copy-start | bytes 1990660
  91.2 23.6 %collective-permute-start.10 = (bf16[288,1152]{1,0:T(8,128)(2,1)S(1)}, bf16[288,1152]{1,0:T(8,128)(2,1)}, u32[]{:S(2)}, u32[]{:S(2)}) collective-permute-start(bf16[288,1152]{1,0:T(8,128)(2,1)S(1)} %get-tuple-element.28), channel_id=1, source_target_pairs={{0,6},{2,4},{4,2},{6,0},{1,7},{3,5},{5,3},{7,1},{8,14},{10,12},{12... | collective-permute-start | bytes 1990664 | tf_op jit(solution)/shard_map/ppermute | solution.py:26
  98.7 43.6 %all-to-all-start.1 = ((bf16[64,8,640]{2,1,0:T(8,128)(2,1)}), bf16[64,8,640]{2,1,0:T(8,128)(2,1)S(1)}, u32[]{:S(2)}, u32[]{:S(2)}) async-start(bf16[64,8,640]{2,1,0:T(8,128)(2,1)} %bitcast.14), calls=%async_computation.1 | async-start | bytes 1310720 | tf_op jit(solution)/shard_map/all_to_all | solution.py:321
  110.0 11.8 %collective-permute-start.5 = (bf16[72,1152]{1,0:T(8,128)(2,1)S(1)}, bf16[72,1152]{1,0:T(8,128)(2,1)S(1)}, u32[]{:S(2)}, u32[]{:S(2)}) collective-permute-start(bf16[72,1152]{1,0:T(8,128)(2,1)S(1)} %get-tuple-element.40), channel_id=1, source_target_pairs={{0,4},{2,6},{4,0},{6,2},{1,5},{3,7},{5,1},{7,3},{8,12},{10,14},{12... | collective-permute-start | bytes 497672 | tf_op jit(solution)/shard_map/ppermute | solution.py:26
  112.4 12.9 %collective-permute-start.7 = (bf16[72,1152]{1,0:T(8,128)(2,1)S(1)}, bf16[72,1152]{1,0:T(8,128)(2,1)S(1)}, u32[]{:S(2)}, u32[]{:S(2)}) collective-permute-start(bf16[72,1152]{1,0:T(8,128)(2,1)S(1)} %get-tuple-element.41), channel_id=1, source_target_pairs={{0,6},{2,4},{4,2},{6,0},{1,7},{3,5},{5,3},{7,1},{8,14},{10,12},{12... | collective-permute-start | bytes 497672 | tf_op jit(solution)/shard_map/ppermute | solution.py:26
  113.1 12.3 %collective-permute-start.6 = (bf16[72,1152]{1,0:T(8,128)(2,1)S(1)}, bf16[72,1152]{1,0:T(8,128)(2,1)S(1)}, u32[]{:S(2)}, u32[]{:S(2)}) collective-permute-start(bf16[72,1152]{1,0:T(8,128)(2,1)S(1)} %get-tuple-element.42), channel_id=1, source_target_pairs={{0,2},{2,0},{4,6},{6,4},{1,3},{3,1},{5,7},{7,5},{8,10},{10,8},{12,... | collective-permute-start | bytes 497672 | tf_op jit(solution)/shard_map/ppermute | solution.py:26
  116.7 9.7 %collective-permute-start.11 = (bf16[72,1152]{1,0:T(8,128)(2,1)S(1)}, bf16[72,1152]{1,0:T(8,128)(2,1)S(1)}, u32[]{:S(2)}, u32[]{:S(2)}) collective-permute-start(bf16[72,1152]{1,0:T(8,128)(2,1)S(1)} %get-tuple-element.37), channel_id=1, source_target_pairs={{0,128},{64,192},{128,0},{192,64},{1,129},{65,193},{129,1},{193,65... | collective-permute-start | bytes 497672 | tf_op jit(solution)/shard_map/ppermute | solution.py:26
  118.8 9.7 %collective-permute-start.13 = (bf16[72,1152]{1,0:T(8,128)(2,1)S(1)}, bf16[72,1152]{1,0:T(8,128)(2,1)S(1)}, u32[]{:S(2)}, u32[]{:S(2)}) collective-permute-start(bf16[72,1152]{1,0:T(8,128)(2,1)S(1)} %get-tuple-element.38), channel_id=1, source_target_pairs={{0,192},{64,128},{128,64},{192,0},{1,193},{65,129},{129,65},{193,1... | collective-permute-start | bytes 497672 | tf_op jit(solution)/shard_map/ppermute | solution.py:26
  121.8 6.7 %collective-permute-start.12 = (bf16[72,1152]{1,0:T(8,128)(2,1)S(1)}, bf16[72,1152]{1,0:T(8,128)(2,1)S(1)}, u32[]{:S(2)}, u32[]{:S(2)}) collective-permute-start(bf16[72,1152]{1,0:T(8,128)(2,1)S(1)} %get-tuple-element.39), channel_id=1, source_target_pairs={{0,64},{64,0},{128,192},{192,128},{1,65},{65,1},{129,193},{193,129... | collective-permute-start | bytes 497672 | tf_op jit(solution)/shard_map/ppermute | solution.py:26
  128.7 7.6 %collective-permute-start.15 = (bf16[36,1152]{1,0:T(8,128)(2,1)S(1)}, bf16[36,1152]{1,0:T(8,128)(2,1)S(1)}, u32[]{:S(2)}, u32[]{:S(2)}) collective-permute-start(bf16[36,1152]{1,0:T(8,128)(2,1)S(1)} %pad_maximum_fusion.1), channel_id=1, source_target_pairs={{0,56},{8,48},{16,40},{24,32},{32,24},{40,16},{48,8},{56,0},{1,57}... | collective-permute-start | bytes 248840 | tf_op jit(solution)/shard_map/ppermute | solution.py:26
  129.8 8.1 %collective-permute-start.16 = (bf16[36,1152]{1,0:T(8,128)(2,1)S(1)}, bf16[36,1152]{1,0:T(8,128)(2,1)S(1)}, u32[]{:S(2)}, u32[]{:S(2)}) collective-permute-start(bf16[36,1152]{1,0:T(8,128)(2,1)S(1)} %pad_maximum_fusion.2), channel_id=1, source_target_pairs={{0,8},{8,0},{16,24},{24,16},{32,40},{40,32},{48,56},{56,48},{1,9},... | collective-permute-start | bytes 248840 | tf_op jit(solution)/shard_map/ppermute | solution.py:26
  133.1 6.8 %collective-permute-start.14 = (bf16[36,1152]{1,0:T(8,128)(2,1)S(1)}, bf16[36,1152]{1,0:T(8,128)(2,1)S(1)}, u32[]{:S(2)}, u32[]{:S(2)}) collective-permute-start(bf16[36,1152]{1,0:T(8,128)(2,1)S(1)} %pad_maximum_fusion), channel_id=1, source_target_pairs={{0,48},{8,56},{16,32},{24,40},{32,16},{40,24},{48,0},{56,8},{1,49}... | collective-permute-start | bytes 248840 | tf_op jit(solution)/shard_map/ppermute | solution.py:26
  139.9 5.7 %collective-permute-start.17 = (bf16[18,1152]{1,0:T(8,128)(2,1)S(1)}, bf16[18,1152]{1,0:T(8,128)(2,1)S(1)}, u32[]{:S(2)}, u32[]{:S(2)}) collective-permute-start(bf16[18,1152]{1,0:T(8,128)(2,1)S(1)} %get-tuple-element.43), channel_id=1, source_target_pairs={{0,16},{8,24},{16,0},{24,8},{32,48},{40,56},{48,32},{56,40},{1,17}... | collective-permute-start | bytes 124424 | tf_op jit(solution)/shard_map/ppermute | solution.py:26
